TPU v7x, 128 devices: a whole 4x4x4 slice. The times are simulated.
128 devices in a mesh: row: 8 (over y, core), col: 16 (over z, x).
Axes of the slice: x: 4, y: 4, z: 4, core: 2. Of those that a mesh axis runs over, the one named last changes fastest.
Arguments:
- state: float32 [2, 262144], P(None, ('row', 'col')), may hold values from -2.5 to 2.5
- friction: float32 [3, 262144], P(None, ('row', 'col')), as said below
- near_blocks: bfloat16 [1024, 256, 256], P(('row', 'col')), as said below
- left_factor: bfloat16 [16384, 64, 256], P(('row', 'col')), may hold values from -0.1875 to 0.1875
- right_factor: bfloat16 [16384, 64, 256], P(('row', 'col')), may hold values from -0.375 to 0.375
- pairs: int32 [16384, 2], P(('row', 'col')), may hold values from 0 to 1023, as said below
- ranks: int32 [16384], P(('row', 'col')), may hold values from 8 to 64, as said below
- perm: int32 [262144], P(('row', 'col')), may hold values from 0 to 262143, as said below
Outputs:
- new_state: float32 [2, 262144], P(None, ('row', 'col'))
- error_norm: float32 [], replicated
Inputs may be any that keep to these rules, and one draw needn't show every extreme that they name: `pairs`: pairs are held in blocks of 128 rows, the block of device d = i * 16 + j on row+col. In that block the first cluster lies in i * 16 * 8 to (i + 1) * 16 * 8 - 1 and the second cluster is (k * 16 + j) * 8 + e with k != i and 0 <= e < 8. `ranks`: multiples of 8. `perm`: A permutation that maps each block of 2048 consecutive positions onto the same block. `friction`: all entries positive. `near_blocks`: each block is symmetric.
All inputs are finite; a program needn't handle non-finite values.
Results may differ from a plain program's by a relative error of at most 0.00055.
Values may be sent and summed in bfloat16 or wider, within the bound.
No kernel may reach another device: no remote copies, remote signals or barrier semaphores. Data moves between devices by JAX's collectives and lax.ppermute only.
A program may use at most 64 MiB of HBM per device.

v0:
```python
import jax
import jax.numpy as jnp
from jax import lax
from jax.sharding import PartitionSpec as P

step_size = 0.1
damping = 0.5
abs_tol = 0.001
rel_tol = 0.001


def pair_terms(first, second, left_factor, right_factor, ranks):
    width = left_factor.shape[1]
    mask = (jnp.arange(width, dtype=jnp.int32)[None, :] < ranks[:, None]).astype(jnp.float32)
    coef_j = (
        jnp.einsum("prc,pc->pr", right_factor, second, preferred_element_type=jnp.float32) * mask
    ).astype(jnp.bfloat16)
    coef_i = (
        jnp.einsum("prc,pc->pr", left_factor, first, preferred_element_type=jnp.float32) * mask
    ).astype(jnp.bfloat16)
    to_first = jnp.einsum("prc,pr->pc", left_factor, coef_j, preferred_element_type=jnp.float32)
    to_second = jnp.einsum("prc,pr->pc", right_factor, coef_i, preferred_element_type=jnp.float32)
    return (to_first, to_second)


def local_stress(ordered, near_blocks, left_factor, right_factor, pairs, ranks):
    cluster = ordered.shape[1]
    near_term = jnp.einsum("qij,qj->qi", near_blocks, ordered, preferred_element_type=jnp.float32)
    everything = lax.all_gather(ordered, ("row", "col"), axis=0, tiled=True)
    to_first, to_second = pair_terms(
        everything[pairs[:, 0]], everything[pairs[:, 1]], left_factor, right_factor, ranks
    )
    total = jnp.zeros((everything.shape[0], cluster), jnp.float32)
    total = total.at[pairs[:, 0]].add(to_first).at[pairs[:, 1]].add(to_second)
    far_term = lax.psum_scatter(total, ("row", "col"), scatter_dimension=0, tiled=True)
    return near_term + far_term


def derivative(current, friction, near_blocks, left_factor, right_factor, pairs, ranks, local_perm):
    own_count = near_blocks.shape[0]
    cluster = near_blocks.shape[1]
    rate = jnp.exp(current[0])
    deficit = (1.0 - rate).astype(jnp.bfloat16)
    ordered = deficit[local_perm].reshape(own_count, cluster)
    stress = local_stress(ordered, near_blocks, left_factor, right_factor, pairs, ranks)
    stress_rate = jnp.zeros((rate.shape[0],), jnp.float32).at[local_perm].set(stress.reshape(-1))
    coef_a, coef_b, sigma = (friction[0], friction[1], friction[2])
    dlt = jnp.exp(-current[1]) - rate
    dlv = (stress_rate - coef_b * sigma * dlt) / (coef_a * sigma + damping * rate)
    return jnp.stack([dlv, dlt])


def shards(state, friction, near_blocks, left_factor, right_factor, pairs, ranks, perm):
    local_perm = perm % perm.shape[0]
    first_k = derivative(
        state, friction, near_blocks, left_factor, right_factor, pairs, ranks, local_perm
    )
    section = state + step_size * first_k
    second_k = derivative(
        section, friction, near_blocks, left_factor, right_factor, pairs, ranks, local_perm
    )
    new_state = state + 0.5 * step_size * (first_k + second_k)
    scaled = 0.5 * step_size * (second_k - first_k) / (abs_tol + rel_tol * jnp.abs(new_state))
    total = lax.psum(jnp.sum(scaled * scaled), ("row", "col"))
    entries = 2.0 * state.shape[1] * lax.axis_size("row") * lax.axis_size("col")
    error_norm = jnp.sqrt(total / entries)
    return (new_state, error_norm)


def solution(mesh):
    placed = (
        P(None, ("row", "col")),
        P(None, ("row", "col")),
        P(("row", "col"), None, None),
        P(("row", "col"), None, None),
        P(("row", "col"), None, None),
        P(("row", "col"), None),
        P(("row", "col")),
        P(("row", "col")),
    )
    return jax.shard_map(
        shards,
        mesh=mesh,
        in_specs=placed,
        out_specs=(P(None, ("row", "col")), P()),
        check_vma=False,
    )
```

profile of v0, /device:TPU:1, one launch (start us, length us, event | category | flops | bytes accessed | tf_op | source)
XLA Modules:
  0.0 1529.3 jit_solution(6182582524146746599)
XLA Ops:
  7.2 0.0 copy-start
  7.2 0.0 reduce-scatter.3.cloned.1.call-start
  7.2 0.8 fusion.44
  8.0 0.7 broadcast_clamp_fusion
  8.7 0.8 convert_reduce_fusion.1
  9.5 13.1 gather_fusion
  22.6 55.7 %all_gather.6 = bf16[1024,256]{1,0:T(8,128)(2,1)S(1)} all-gather(bf16[8,256]{1,0:T(8,128)(2,1)S(1)} %reshape.41), channel_id=1, replica_groups=mesh['row'=8,'col'=16] {'row','col'}, dimensions={0}, use_global_device_ids=true | all-gather | bytes 528384 | tf_op jit(solution)/shard_map/all_gather | solution.py:29
  78.3 0.8 gather_fusion.2
  79.2 0.8 gather_fusion.1
  80.0 0.0 copy-start.3
  80.0 0.0 copy-start.8
  80.1 0.0 copy-start.1
  80.1 3.5 fusion.17
  83.6 0.0 copy-done.3
  83.6 1.2 fusion.20
  84.8 0.0 copy-done.8
  84.8 0.1 fusion.31
  84.9 0.0 copy-done.1
  84.9 0.7 fusion.28
  85.6 0.0 copy-start.6
  85.6 0.0 copy-start.7
  85.6 0.7 fusion.26
  86.2 1.5 scatter_custom_fusion
  87.8 1.7 scatter_custom_fusion.1
  89.5 0.0 copy-start.5
  89.5 1.0 copy-done.5
  90.4 0.0 reduce-scatter.3.cloned.1.call-update
  90.5 0.0 reduce-scatter.5.cloned.1.call-start
  90.5 0.0 copy-done
  90.5 0.4 fusion.48
  90.9 0.0 copy-done.6
  90.9 0.0 copy-done.7
  90.9 0.1 fusion.46
  91.0 603.4 %reduce-scatter.3.cloned.1.call-done = f32[8,256]{1,0:T(8,128)} async-done(((f32[1024,256]{1,0:T(8,128)}), f32[8,256]{1,0:T(8,128)}) %reduce-scatter.3.cloned.1.call-update) | async-done | bytes 8208 | tf_op jit(solution)/shard_map/reduce_scatter | solution.py:35
  694.3 0.7 fusion.38
  695.0 8.0 scatter_custom_fusion.2
  703.2 13.1 gather_fusion.3
  716.3 81.5 %all_gather.7 = bf16[1024,256]{1,0:T(8,128)(2,1)S(1)} all-gather(bf16[8,256]{1,0:T(8,128)(2,1)S(1)} %reshape.43), channel_id=1, replica_groups=mesh['row'=8,'col'=16] {'row','col'}, dimensions={0}, use_global_device_ids=true | all-gather | bytes 528384 | tf_op jit(solution)/shard_map/all_gather | solution.py:29
  797.8 0.8 gather_fusion.4
  798.6 0.8 gather_fusion.5
  799.5 0.0 copy-start.2
  799.5 3.5 fusion.14
  803.0 0.0 copy-done.2
  803.0 1.2 fusion.11
  804.2 0.1 fusion.33
  804.3 0.7 fusion.24
  804.9 1.5 scatter_custom_fusion.3
  806.5 2.8 fusion.22
  809.3 1.7 scatter_custom_fusion.4
  811.0 0.0 copy-start.4
  811.0 1.0 copy-done.4
  812.0 0.0 reduce-scatter.5.cloned.1.call-update
  812.0 0.4 fusion.49
  812.4 0.1 fusion.45
  812.5 604.5 %reduce-scatter.5.cloned.1.call-done = f32[8,256]{1,0:T(8,128)} async-done(((f32[1024,256]{1,0:T(8,128)}), f32[8,256]{1,0:T(8,128)}) %reduce-scatter.5.cloned.1.call-update) | async-done | bytes 8208 | tf_op jit(solution)/shard_map/reduce_scatter | solution.py:35
  1417.0 0.7 fusion.37
  1417.7 8.0 scatter_custom_fusion.5
  1425.8 1.3 multiply_reduce_fusion
  1427.0 93.6 %psum.7 = f32[]{:T(128)} all-reduce(f32[]{:T(128)} %get-tuple-element.2), channel_id=1, replica_groups=mesh['row'=8,'col'=16] {'row','col'}, use_global_device_ids=true, to_apply=%region_9.10 | all-reduce | flops 1 | bytes 8 | tf_op jit(solution)/shard_map/psum | solution.py:64
  (11 shorter events, 0.1 us)
Async XLA Ops:
  7.2 83.4 %copy-start = (bf16[8,256,256]{2,1,0:T(8,128)(2,1)S(1)}, bf16[8,256,256]{2,1,0:T(8,128)(2,1)}, u32[]{:S(2)}) copy-start(bf16[8,256,256]{2,1,0:T(8,128)(2,1)} %param.10) | copy-start | bytes 3145732
  7.2 687.2 %reduce-scatter.3.cloned.1.call-start = ((), (), s32[]{:S(2)}) async-start(), calls=%async_computation.2 | async-start | bytes 1056768 | tf_op jit(solution)/shard_map/reduce_scatter | solution.py:35
  80.0 3.6 copy-start.3
  80.0 4.7 copy-start.8
  80.1 4.8 copy-start.1
  85.6 5.4 copy-start.6
  85.6 5.4 copy-start.7
  89.5 1.0 copy-start.5
  90.5 1326.5 %reduce-scatter.5.cloned.1.call-start = ((), (), s32[]{:S(2)}) async-start(), calls=%async_computation.3 | async-start | bytes 1056768 | tf_op jit(solution)/shard_map/reduce_scatter | solution.py:35
  799.5 3.5 copy-start.2
  811.0 1.0 copy-start.4
Sparse Core Ops, SparseCore 0:
  90.6 603.7 reduce-scatter.2
  812.1 604.7 reduce-scatter.4
where the time goes:
time: 1530 us
  waiting for transfers between devices  1210 us (79%)
  blocking collectives  231 us (15%)
  local copies, waits for them, and re-layouts  47.7 us (3%)
  between operations  16.1 us (1%)
    reduce_scatter x2, waiting for transfers between devices, local_stress(): lax.psum_scatter(total, ('row', 'col'), scatter_dimension=0, tiled=True)  1210 us
    all_gather x2, blocking collectives, local_stress(): everything = lax.all_gather(ordered, ('row', 'col'), axis=0, tiled=True)  137 us
    psum x1, blocking collectives, shards(): total = lax.psum(jnp.sum(scaled * scaled), ('row', 'col'))  93.6 us
  transfers between devices with their start and end apart: 2, of which 2 were waited for; matrix products, arithmetic and copies ran while one was open for 0% of the time, Pallas kernels for 0%

commit v1 on v0

v1 whole, which is shorter than its diff:
```python
import functools

import jax
import jax.numpy as jnp
from jax import lax
from jax.experimental import pallas as pl
from jax.experimental.pallas import tpu as pltpu
from jax.sharding import PartitionSpec as P

step_size = 0.1
damping = 0.5
abs_tol = 0.001
rel_tol = 0.001

f32 = jnp.float32
bf16 = jnp.bfloat16
LANES = 128
VMEM = pl.BlockSpec(memory_space=pltpu.VMEM)
HBM = pl.BlockSpec(memory_space=pl.ANY)


def mxu(a, b):
    return lax.dot_general(a, b, (((1,), (0,)), ((), ())), preferred_element_type=f32)


def mxu_nt(a, b):
    return lax.dot_general(a, b, (((1,), (1,)), ((), ())), preferred_element_type=f32)


def to_tiles(row):
    return jnp.concatenate([row[:, k * LANES:(k + 1) * LANES] for k in range(row.shape[1] // LANES)], axis=0)


def to_row(tiles):
    return jnp.concatenate([tiles[k:k + 1, :] for k in range(tiles.shape[0])], axis=1)


def to_clusters(row, cluster):
    return jnp.concatenate([row[:, k * cluster:(k + 1) * cluster] for k in range(row.shape[1] // cluster)], axis=0)


def split3(x):
    hi = x.astype(bf16)
    rest = x - hi.astype(f32)
    mid = rest.astype(bf16)
    low = (rest - mid.astype(f32)).astype(bf16)
    return hi, mid, low


def place(perm_row, tiles):
    count = perm_row.shape[1]
    local = lax.rem(perm_row, count)
    tile = lax.div(local, LANES)
    lane = local - tile * LANES
    at_tile = lax.broadcasted_iota(jnp.int32, (tiles, count), 0) == tile
    at_lane = lax.broadcasted_iota(jnp.int32, (LANES, count), 0) == lane
    return at_tile, jnp.where(at_lane, 1.0, 0.0).astype(bf16)


def spread(ordered, out_ref, copies):
    value = ordered.astype(bf16)
    for k in range(copies):
        out_ref[k] = value


def first_deficit(copies, state_ref, perm_ref, own_ref, copies_ref):
    cluster = own_ref.shape[1]
    at_tile, at_lane = place(perm_ref[...], perm_ref.shape[1] // LANES)
    deficit = to_tiles(1.0 - jnp.exp(state_ref[0:1, :])).astype(bf16)
    picked = jnp.where(at_tile, mxu(deficit, at_lane), 0.0)
    ordered = to_clusters(jnp.sum(picked, axis=0, keepdims=True), cluster)
    own_ref[...] = ordered
    spread(ordered, copies_ref, copies)


def to_order(state_ref, friction_ref, perm_ref, fields_ref):
    cluster = fields_ref.shape[2]
    tiles = perm_ref.shape[1] // LANES
    at_tile, at_lane = place(perm_ref[...], tiles)
    coef_a, coef_b, sigma = (friction_ref[k:k + 1, :] for k in range(3))
    rows = (state_ref[0:1, :], state_ref[1:2, :], coef_a * sigma, coef_b * sigma)
    parts = [part for row in rows for part in split3(to_tiles(row))]
    moved = mxu(jnp.concatenate(parts, axis=0), at_lane)
    for k in range(len(rows)):
        three = [moved[(3 * k + s) * tiles:(3 * k + s + 1) * tiles] for s in range(3)]
        picked = jnp.where(at_tile, (three[0] + three[1]) + three[2], 0.0)
        fields_ref[k] = to_clusters(jnp.sum(picked, axis=0, keepdims=True), cluster)


def from_order(new_ref, perm_ref, out_ref):
    tiles = perm_ref.shape[1] // LANES
    at_tile, at_lane = place(perm_ref[...], tiles)
    parts = []
    for k in range(2):
        row = to_row_of_clusters(new_ref[k])
        parts += [jnp.where(at_tile, part.astype(f32), 0.0).astype(bf16) for part in split3(row)]
    moved = mxu_nt(jnp.concatenate(parts, axis=0), at_lane)
    for k in range(2):
        three = [moved[(3 * k + s) * tiles:(3 * k + s + 1) * tiles] for s in range(3)]
        out_ref[k:k + 1, :] = to_row((three[0] + three[1]) + three[2])


def to_row_of_clusters(x):
    return jnp.concatenate([x[k:k + 1, :] for k in range(x.shape[0])], axis=1)


def stress_terms(chunk, everyone_ref, own_ref, partner_ref, y1_ref, y2_ref, y3_ref, sel_ref, near_hbm, left_hbm,
                 right_hbm, first_ref, *rest):
    second_refs = rest[:4]
    near, left, right, sem = rest[4:]
    total = left.shape[0]
    chunks = total // chunk

    def fetch(k):
        part = pl.ds(k * chunk, chunk)
        return (
            pltpu.make_async_copy(right_hbm.at[part], right.at[part], sem.at[0, k]),
            pltpu.make_async_copy(left_hbm.at[part], left.at[part], sem.at[1, k]),
        )

    near_copy = pltpu.make_async_copy(near_hbm, near, sem.at[0, chunks])
    for k in range(chunks):
        for copy in fetch(k):
            copy.start()
    near_copy.start()

    everyone = everyone_ref[...]
    own = own_ref[...]
    group = jnp.concatenate([own, partner_ref[...], y1_ref[...], y2_ref[...], y3_ref[...]], axis=0).astype(bf16)
    firsts, seconds = everyone.shape[0], group.shape[0]
    row_first = lax.broadcasted_iota(jnp.int32, (firsts, chunk), 0)
    row_second = lax.broadcasted_iota(jnp.int32, (seconds, chunk), 0)
    to_first = jnp.zeros((firsts, own.shape[1]), f32)
    to_second = jnp.zeros((seconds, own.shape[1]), f32)
    for k in range(chunks):
        part = pl.ds(k * chunk, chunk)
        at_first = row_first == sel_ref[0:1, part]
        at_second = row_second == sel_ref[1:2, part]
        copy_right, copy_left = fetch(k)
        copy_right.wait()
        r = right[part]
        coef_j = jnp.sum(jnp.where(at_second, mxu_nt(group, r), 0.0), axis=0, keepdims=True)
        copy_left.wait()
        l = left[part]
        coef_i = jnp.sum(jnp.where(at_first, mxu_nt(everyone, l), 0.0), axis=0, keepdims=True)
        to_first += mxu(jnp.where(at_first, coef_j, 0.0).astype(bf16), l)
        to_second += mxu(jnp.where(at_second, coef_i, 0.0).astype(bf16), r)
    near_copy.wait()
    mine = own.astype(bf16)
    count = own.shape[0]
    row_own = lax.broadcasted_iota(jnp.int32, own.shape, 0)
    near_term = jnp.zeros(own.shape, f32)
    for k in range(count):
        near_term += jnp.where(row_own == k, mxu(mine, near[k]), 0.0)
    first_ref[...] = to_first.astype(first_ref.dtype)
    for k, ref in enumerate(second_refs):
        ref[...] = to_second[2 * count * k:2 * count * (k + 1)]
    second_refs[0][0:count, :] += near_term


def slopes(lv, lt, a_sigma, b_sigma, stress):
    rate = jnp.exp(lv)
    dlt = jnp.exp(-lt) - rate
    return (stress - b_sigma * dlt) / (a_sigma + damping * rate), dlt


def total_stress(from_first_ref, kept_ref, partner_ref):
    total = kept_ref[...] + partner_ref[...]
    for k in range(from_first_ref.shape[0]):
        total += from_first_ref[k].astype(f32)
    return total


def half_step(copies, from_first_ref, kept_ref, partner_ref, fields_ref, slope_ref, own_ref, copies_ref):
    lv, lt, a_sigma, b_sigma = (fields_ref[k] for k in range(4))
    dlv, dlt = slopes(lv, lt, a_sigma, b_sigma, total_stress(from_first_ref, kept_ref, partner_ref))
    slope_ref[0] = dlv
    slope_ref[1] = dlt
    ordered = (1.0 - jnp.exp(lv + step_size * dlv)).astype(bf16).astype(f32)
    own_ref[...] = ordered
    spread(ordered, copies_ref, copies)


def last_step(from_first_ref, kept_ref, partner_ref, fields_ref, slope_ref, new_ref, sum_ref):
    lv, lt, a_sigma, b_sigma = (fields_ref[k] for k in range(4))
    stress = total_stress(from_first_ref, kept_ref, partner_ref)
    first = (slope_ref[0], slope_ref[1])
    second = slopes(lv + step_size * first[0], lt + step_size * first[1], a_sigma, b_sigma, stress)
    squares = jnp.zeros(lv.shape, f32)
    for k, base in enumerate((lv, lt)):
        new = base + 0.5 * step_size * (first[k] + second[k])
        new_ref[k] = new
        scaled = 0.5 * step_size * (second[k] - first[k]) / (abs_tol + rel_tol * jnp.abs(new))
        squares += scaled * scaled
    sum_ref[...] = jnp.full(sum_ref.shape, jnp.sum(squares), f32)


def call(kernel, out_shape, ins, name, scratch=()):
    many = isinstance(out_shape, (list, tuple))
    return pl.pallas_call(
        kernel,
        out_shape=out_shape,
        in_specs=ins,
        out_specs=[VMEM] * len(out_shape) if many else VMEM,
        scratch_shapes=list(scratch),
        name=name,
        compiler_params=pltpu.CompilerParams(vmem_limit_bytes=32 * 1024 * 1024),
    )


def shards(rows, columns, state, friction, near_blocks, left_factor, right_factor, pairs, ranks, perm):
    own_count, cluster = near_blocks.shape[:2]
    count, width = left_factor.shape[:2]
    span = columns * own_count
    sds = jax.ShapeDtypeStruct
    block = sds((own_count, cluster), f32)
    copies = sds((columns, own_count, cluster), bf16)
    row = lax.axis_index("row")
    perm_row = perm.reshape(1, -1)

    def swap(x, distance):
        return lax.ppermute(x, "row", [(r, r ^ distance) for r in range(rows)])

    own, spread_out = call(functools.partial(first_deficit, columns), [block, copies], [VMEM] * 2, "first_deficit")(
        state, perm_row)
    fields = call(to_order, sds((4, own_count, cluster), f32), [VMEM] * 3, "to_order")(state, friction, perm_row)

    first_at = pairs[:, 0] - row * span
    second_at = ((pairs[:, 1] // span) ^ row) * own_count + pairs[:, 1] % own_count
    within = jnp.arange(width, dtype=jnp.int32)[None, :] < ranks[:, None]
    sel = jnp.stack([
        jnp.where(within, first_at[:, None], -1).reshape(-1),
        jnp.where(within, second_at[:, None], -1).reshape(-1),
    ])
    left = left_factor.reshape(count * width, cluster)
    right = right_factor.reshape(count * width, cluster)

    chunk = 2048
    pair_block = sds((2 * own_count, cluster), f32)
    terms = call(
        functools.partial(stress_terms, chunk),
        [sds((span, cluster), bf16)] + [pair_block] * 4,
        [VMEM] * 7 + [HBM] * 3,
        "stress_terms",
        [
            pltpu.VMEM(near_blocks.shape, bf16),
            pltpu.VMEM(left.shape, bf16),
            pltpu.VMEM(right.shape, bf16),
            pltpu.SemaphoreType.DMA((2, count * width // chunk + 1)),
        ],
    )

    def exchange(own, spread_out):
        everyone = lax.all_to_all(spread_out, "col", 0, 0)
        partner = swap(own, 1)
        two = jnp.concatenate([own, partner], axis=0)
        others = [swap(two, 2 * k) for k in (1, 2, 3)]
        first, *second = terms(everyone.reshape(span, cluster), own, partner, *others, sel, near_blocks, left, right)
        from_first = lax.all_to_all(first.reshape(columns, own_count, cluster), "col", 0, 0)
        both = second[0] + swap(second[1], 2) + swap(second[2], 4) + swap(second[3], 6)
        return from_first, both[:own_count], swap(both[own_count:], 1)

    slope, own, spread_out = call(
        functools.partial(half_step, columns), [sds((2, own_count, cluster), f32), block, copies], [VMEM] * 4, "half_step"
    )(*exchange(own, spread_out), fields)
    devices = rows * columns
    new, squares = call(
        last_step, [sds((2, own_count, cluster), f32), sds((devices, LANES), f32)], [VMEM] * 5, "last_step"
    )(*exchange(own, spread_out), fields, slope)
    everywhere = lax.all_to_all(squares, ("row", "col"), 0, 0, tiled=True)
    new_state = call(from_order, sds(state.shape, f32), [VMEM] * 2, "from_order")(new, perm_row)
    entries = 2.0 * state.shape[1] * devices
    return new_state, jnp.sqrt(jnp.sum(everywhere[:, 0]) / entries)


def solution(mesh):
    both = ("row", "col")
    placed = (P(None, both), P(None, both), P(both, None, None), P(both, None, None), P(both, None, None),
              P(both, None), P(both), P(both))
    return jax.shard_map(
        functools.partial(shards, mesh.shape["row"], mesh.shape["col"]),
        mesh=mesh,
        in_specs=placed,
        out_specs=(P(None, both), P()),
        check_vma=False,
    )
```

time: 1530 us -> 114 us (0.07)
  waiting for transfers between devices: 1210 us -> 22.5 us
  blocking collectives: 231 us -> 0 us
  starting transfers between devices: 0.08 us -> 57 us
  local copies, waits for them, and re-layouts: 47.7 us -> 11.6 us
  Pallas kernels: 0 us -> 17.3 us
    reduce_scatter x2 -> x0, waiting for transfers between devices: 1210 us -> none  [local_stress(): lax.psum_scatter(total, ('row', 'col'), scatter_dimension=0, tiled=True)]
    all_gather x2 -> x0, blocking collectives: 137 us -> none  [local_stress(): everything = lax.all_gather(ordered, ('row', 'col'), axis=0, tiled=True)]
    psum x1 -> x0, blocking collectives: 93.6 us -> none  [shards(): total = lax.psum(jnp.sum(scaled * scaled), ('row', 'col'))]
    all_to_all x0 -> x5, starting transfers between devices: none -> 32 us  [the longest x2 11.9 us: exchange(): lax.all_to_all(first.reshape(columns, own_count, cluster), 'col', 0, 0)]
    gather x6 -> x0, local copies, waits for them, and re-layouts: 29.6 us -> none  [the longest x2 26.2 us: derivative(): ordered = deficit[local_perm].reshape(own_count, cluster)]
    ppermute x0 -> x16, starting transfers between devices: none -> 25 us  [swap(): return lax.ppermute(x, 'row', [(r, r ^ distance) for r in range(rows)])]
    pallas_call x0 -> x7, Pallas kernels: none -> 17.3 us  [the longest x2 13.7 us: exchange(): terms(everyone.reshape(span, cluster), own, partner, *others, sel, near_b...]
    scatter x2 -> x0, local copies, waits for them, and re-layouts: 16.1 us -> none  [derivative(): jnp.zeros((rate.shape[0],), jnp.float32).at[local_perm]]
  transfers between devices with their start and end apart: 2 -> 21, of which waited for: 2 -> 10; matrix products, arithmetic and copies ran while one was open for 0% -> 2% of each run, Pallas kernels for 0% -> 1%
where the time goes in v1:
time: 114 us; the launch traced here: 113 us
  starting transfers between devices  57 us (50%)
  waiting for transfers between devices  22.5 us (20%)
  Pallas kernels  17.3 us (15%)
  local copies, waits for them, and re-layouts  11.6 us (10%)
  between operations  2.71 us (2%)
  other arithmetic  2.23 us (2%)
    ppermute x16, starting transfers between devices, swap(): return lax.ppermute(x, 'row', [(r, r ^ distance) for r in range(rows)])  25 us
    pallas_call x2, Pallas kernels, exchange(): terms(everyone.reshape(span, cluster), own, partner, *others, sel, near_b...  13.7 us
    all_to_all x2, starting transfers between devices, exchange(): lax.all_to_all(first.reshape(columns, own_count, cluster), 'col', 0, 0)  11.9 us
    all_to_all x2, starting transfers between devices, exchange(): everyone = lax.all_to_all(spread_out, 'col', 0, 0)  11.9 us
    unnamed x24, local copies, waits for them, and re-layouts  11.4 us
    all_to_all x1, waiting for transfers between devices, shards(): everywhere = lax.all_to_all(squares, ('row', 'col'), 0, 0, tiled=True)  8.85 us
    all_to_all x1, starting transfers between devices, shards(): everywhere = lax.all_to_all(squares, ('row', 'col'), 0, 0, tiled=True)  8.16 us
    ppermute x16, waiting for transfers between devices, swap(): return lax.ppermute(x, 'row', [(r, r ^ distance) for r in range(rows)])  6.73 us
  transfers between devices with their start and end apart: 21, of which 10 were waited for; matrix products, arithmetic and copies ran while one was open for 2% of the time, Pallas kernels for 1%

profile of v1, /device:TPU:1, one launch (start us, length us, event | category | flops | bytes accessed | tf_op | source)
XLA Modules:
  0.0 113.4 jit_solution(12284772732669001798)
XLA Ops:
  0.6 0.0 copy-start.6
  0.6 0.7 copy-done.6
  1.3 0.7 copy-done.8
  2.0 0.8 first_deficit.1
  2.9 8.4 %all-to-all-start = ((bf16[16,8,256]{2,1,0:T(8,128)(2,1)}), bf16[16,8,256]{2,1,0:T(8,128)(2,1)S(1)}, u32[]{:S(2)}, u32[]{:S(2)}) async-start(bf16[16,8,256]{2,1,0:T(8,128)(2,1)} %get-tuple-element.19), calls=%async_computation | async-start | bytes 131072 | tf_op jit(solution)/shard_map/all_to_all | solution.py:254
  11.3 1.0 collective-permute-start
  12.3 0.8 subtract_bitcast_fusion
  13.1 0.8 fusion.1
  13.9 0.1 select_n.42
  14.0 0.1 select_n.46
  14.1 0.0 collective-permute-done.partner_ref
  14.1 2.8 %collective-permute-start.3 = (f32[16,256]{1,0:T(8,128)S(1)}, f32[16,256]{1,0:T(8,128)S(1)}, u32[]{:S(2)}, u32[]{:S(2)}) collective-permute-start(f32[16,256]{1,0:T(8,128)S(1)} %constant_dynamic-update-slice_fusion), channel_id=1, source_target_pairs={{0,96},{16,112},{32,64},{48,80},{64,32},{80,48},{96,0},{112,16},{1... | collective-permute-start | bytes 49160 | tf_op jit(solution)/shard_map/ppermute | solution.py:222
  16.9 0.3 collective-permute-start.2
  17.3 0.3 collective-permute-start.1
  17.6 0.1 pad_add_fusion.sel_ref
  17.7 0.7 collective-permute-done.3.y3_ref
  18.4 2.7 %collective-permute-done.2.y2_ref = f32[16,256]{1,0:T(8,128)S(1)} collective-permute-done((f32[16,256]{1,0:T(8,128)S(1)}, f32[16,256]{1,0:T(8,128)S(1)}, u32[]{:S(2)}, u32[]{:S(2)}) %collective-permute-start.2) | collective-permute-done | bytes 16416 | tf_op jit(solution)/shard_map/ppermute | solution.py:222
  21.0 0.0 collective-permute-done.1.y1_ref
  21.0 0.0 all-to-all-done
  21.0 2.2 %copy-done = bf16[128,64,256]{2,1,0:T(8,128)(2,1)S(1)} copy-done((bf16[128,64,256]{2,1,0:T(8,128)(2,1)S(1)}, bf16[128,64,256]{2,1,0:T(8,128)(2,1)}, u32[]{:S(2)}) %copy-start) | copy-done | bytes 4194328
  23.2 2.2 %copy-done.2 = bf16[128,64,256]{2,1,0:T(8,128)(2,1)S(1)} copy-done((bf16[128,64,256]{2,1,0:T(8,128)(2,1)S(1)}, bf16[128,64,256]{2,1,0:T(8,128)(2,1)}, u32[]{:S(2)}) %copy-start.2) | copy-done | bytes 4194328
  25.4 1.2 %copy-done.4 = bf16[8,256,256]{2,1,0:T(8,128)(2,1)S(1)} copy-done((bf16[8,256,256]{2,1,0:T(8,128)(2,1)S(1)}, bf16[8,256,256]{2,1,0:T(8,128)(2,1)}, u32[]{:S(2)}) %copy-start.4) | copy-done | bytes 1048600
  26.7 6.9 %stress_terms.2 = (bf16[128,256]{1,0:T(8,128)(2,1)}, f32[16,256]{1,0:T(8,128)S(1)}, f32[16,256]{1,0:T(8,128)S(1)}, f32[16,256]{1,0:T(8,128)S(1)}, f32[16,256]{1,0:T(8,128)S(1)}) custom-call(bf16[128,256]{1,0:T(8,128)(2,1)S(1)} %bitcast.19, f32[8,256]{1,0:T(8,128)S(1)} %get-tuple-element.20.own_ref, f32[8,256]{1,0:T(8,128)S(1)} %collective-permute-done.partner_ref, ...), custom_call_target="tpu_custom_call" | custom-call | tf_op jit(solution)/shard_map/stress_terms/pallas_call | solution.py:258
  33.5 0.1 collective-permute-start.4
  33.6 2.2 %collective-permute-start.5 = (f32[16,256]{1,0:T(8,128)S(1)}, f32[16,256]{1,0:T(8,128)S(1)}, u32[]{:S(2)}, u32[]{:S(2)}) collective-permute-start(f32[16,256]{1,0:T(8,128)S(1)} %get-tuple-element.24), channel_id=1, source_target_pairs={{0,64},{16,80},{32,96},{48,112},{64,0},{80,16},{96,32},{112,48},{1... | collective-permute-start | bytes 49160 | tf_op jit(solution)/shard_map/ppermute | solution.py:222
  35.8 1.6 %collective-permute-start.6 = (f32[16,256]{1,0:T(8,128)S(1)}, f32[16,256]{1,0:T(8,128)S(1)}, u32[]{:S(2)}, u32[]{:S(2)}) collective-permute-start(f32[16,256]{1,0:T(8,128)S(1)} %get-tuple-element.25), channel_id=1, source_target_pairs={{0,96},{16,112},{32,64},{48,80},{64,32},{80,48},{96,0},{112,16},{1... | collective-permute-start | bytes 49160 | tf_op jit(solution)/shard_map/ppermute | solution.py:222
  37.5 6.9 %all-to-all-start.1 = ((bf16[16,8,256]{2,1,0:T(8,128)(2,1)}), bf16[16,8,256]{2,1,0:T(8,128)(2,1)S(1)}, u32[]{:S(2)}, u32[]{:S(2)}) async-start(bf16[16,8,256]{2,1,0:T(8,128)(2,1)} %bitcast.6), calls=%async_computation.1 | async-start | bytes 131072 | tf_op jit(solution)/shard_map/all_to_all | solution.py:259
  44.3 0.0 collective-permute-done.4
  44.3 0.0 collective-permute-done.5
  44.4 0.0 collective-permute-done.6
  44.4 2.6 %collective-permute-start.7 = (f32[8,256]{1,0:T(8,128)S(1)}, f32[8,256]{1,0:T(8,128)S(1)}, u32[]{:S(2)}, u32[]{:S(2)}) collective-permute-start(f32[8,256]{1,0:T(8,128)S(1)} %get-tuple-element.38), channel_id=1, source_target_pairs={{0,16},{16,0},{32,48},{48,32},{64,80},{80,64},{96,112},{112,96},{1... | collective-permute-start | bytes 24584 | tf_op jit(solution)/shard_map/ppermute | solution.py:222
  47.0 0.0 copy-done.9
  47.0 0.5 to_order.1.fields_ref
  47.5 0.4 collective-permute-done.7.partner_ref
  47.9 3.0 %all-to-all-done.1.from_first_ref = bf16[16,8,256]{2,1,0:T(8,128)(2,1)S(1)} async-done(((bf16[16,8,256]{2,1,0:T(8,128)(2,1)}), bf16[16,8,256]{2,1,0:T(8,128)(2,1)S(1)}, u32[]{:S(2)}, u32[]{:S(2)}) %all-to-all-start.1) | async-done | bytes 65568 | tf_op jit(solution)/shard_map/all_to_all | solution.py:259
  50.8 0.7 half_step.1
  51.5 3.7 %collective-permute-start.8 = (f32[8,256]{1,0:T(8,128)S(1)}, f32[8,256]{1,0:T(8,128)S(1)}, u32[]{:S(2)}, u32[]{:S(2)}) collective-permute-start(f32[8,256]{1,0:T(8,128)S(1)} %get-tuple-element.27.own_ref), channel_id=1, source_target_pairs={{0,16},{16,0},{32,48},{48,32},{64,80},{80,64},{96,112},{112,96},{1... | collective-permute-start | bytes 24584 | tf_op jit(solution)/shard_map/ppermute | solution.py:222
  55.2 3.5 %all-to-all-start.2 = ((bf16[16,8,256]{2,1,0:T(8,128)(2,1)}), bf16[16,8,256]{2,1,0:T(8,128)(2,1)S(1)}, u32[]{:S(2)}, u32[]{:S(2)}) async-start(bf16[16,8,256]{2,1,0:T(8,128)(2,1)} %get-tuple-element.26), calls=%async_computation.2 | async-start | bytes 131072 | tf_op jit(solution)/shard_map/all_to_all | solution.py:254
  58.7 0.0 collective-permute-done.8.partner_ref
  58.7 1.1 collective-permute-start.11
  59.8 0.0 collective-permute-start.10
  59.8 2.2 %collective-permute-start.9 = (f32[16,256]{1,0:T(8,128)S(1)}, f32[16,256]{1,0:T(8,128)S(1)}, u32[]{:S(2)}, u32[]{:S(2)}) collective-permute-start(f32[16,256]{1,0:T(8,128)S(1)} %constant_dynamic-update-slice_fusion.2), channel_id=1, source_target_pairs={{0,32},{16,48},{32,0},{48,16},{64,96},{80,112},{96,64},{112,80},{1... | collective-permute-start | bytes 49160 | tf_op jit(solution)/shard_map/ppermute | solution.py:222
  62.1 0.5 collective-permute-done.11.y3_ref
  62.6 1.6 %collective-permute-done.10.y2_ref = f32[16,256]{1,0:T(8,128)S(1)} collective-permute-done((f32[16,256]{1,0:T(8,128)S(1)}, f32[16,256]{1,0:T(8,128)S(1)}, u32[]{:S(2)}, u32[]{:S(2)}) %collective-permute-start.10) | collective-permute-done | bytes 16416 | tf_op jit(solution)/shard_map/ppermute | solution.py:222
  64.2 0.0 collective-permute-done.9.y1_ref
  64.2 1.2 %all-to-all-done.2 = bf16[16,8,256]{2,1,0:T(8,128)(2,1)S(1)} async-done(((bf16[16,8,256]{2,1,0:T(8,128)(2,1)}), bf16[16,8,256]{2,1,0:T(8,128)(2,1)S(1)}, u32[]{:S(2)}, u32[]{:S(2)}) %all-to-all-start.2) | async-done | bytes 65568 | tf_op jit(solution)/shard_map/all_to_all | solution.py:254
  65.5 2.2 %copy-done.1 = bf16[128,64,256]{2,1,0:T(8,128)(2,1)S(1)} copy-done((bf16[128,64,256]{2,1,0:T(8,128)(2,1)S(1)}, bf16[128,64,256]{2,1,0:T(8,128)(2,1)}, u32[]{:S(2)}) %copy-start.1) | copy-done | bytes 4194328
  67.7 2.2 %copy-done.3 = bf16[128,64,256]{2,1,0:T(8,128)(2,1)S(1)} copy-done((bf16[128,64,256]{2,1,0:T(8,128)(2,1)S(1)}, bf16[128,64,256]{2,1,0:T(8,128)(2,1)}, u32[]{:S(2)}) %copy-start.3) | copy-done | bytes 4194328
  69.8 6.8 %stress_terms.3 = (bf16[128,256]{1,0:T(8,128)(2,1)}, f32[16,256]{1,0:T(8,128)S(1)}, f32[16,256]{1,0:T(8,128)S(1)}, f32[16,256]{1,0:T(8,128)S(1)}, f32[16,256]{1,0:T(8,128)S(1)}) custom-call(bf16[128,256]{1,0:T(8,128)(2,1)S(1)} %bitcast.20, f32[8,256]{1,0:T(8,128)S(1)} %get-tuple-element.27.own_ref, f32[8,256]{1,0:T(8,128)S(1)} %collective-permute-done.8.partner_ref, ...), custom_call_target="tpu_custom_call" | custom-call | tf_op jit(solution)/shard_map/stress_terms/pallas_call | solution.py:258
  76.7 0.1 collective-permute-start.12
  76.8 2.2 %collective-permute-start.13 = (f32[16,256]{1,0:T(8,128)S(1)}, f32[16,256]{1,0:T(8,128)S(1)}, u32[]{:S(2)}, u32[]{:S(2)}) collective-permute-start(f32[16,256]{1,0:T(8,128)S(1)} %get-tuple-element.31), channel_id=1, source_target_pairs={{0,64},{16,80},{32,96},{48,112},{64,0},{80,16},{96,32},{112,48},{1... | collective-permute-start | bytes 49160 | tf_op jit(solution)/shard_map/ppermute | solution.py:222
  79.0 1.6 %collective-permute-start.14 = (f32[16,256]{1,0:T(8,128)S(1)}, f32[16,256]{1,0:T(8,128)S(1)}, u32[]{:S(2)}, u32[]{:S(2)}) collective-permute-start(f32[16,256]{1,0:T(8,128)S(1)} %get-tuple-element.32), channel_id=1, source_target_pairs={{0,96},{16,112},{32,64},{48,80},{64,32},{80,48},{96,0},{112,16},{1... | collective-permute-start | bytes 49160 | tf_op jit(solution)/shard_map/ppermute | solution.py:222
  80.6 5.1 %all-to-all-start.3 = ((bf16[16,8,256]{2,1,0:T(8,128)(2,1)}), bf16[16,8,256]{2,1,0:T(8,128)(2,1)S(1)}, u32[]{:S(2)}, u32[]{:S(2)}) async-start(bf16[16,8,256]{2,1,0:T(8,128)(2,1)} %bitcast.8), calls=%async_computation.3 | async-start | bytes 131072 | tf_op jit(solution)/shard_map/all_to_all | solution.py:259
  85.7 0.0 collective-permute-done.12
  85.7 0.0 collective-permute-done.13
  85.7 0.0 collective-permute-done.14
  85.8 2.9 %collective-permute-start.15 = (f32[8,256]{1,0:T(8,128)S(1)}, f32[8,256]{1,0:T(8,128)S(1)}, u32[]{:S(2)}, u32[]{:S(2)}) collective-permute-start(f32[8,256]{1,0:T(8,128)S(1)} %get-tuple-element.36), channel_id=1, source_target_pairs={{0,16},{16,0},{32,48},{48,32},{64,80},{80,64},{96,112},{112,96},{1... | collective-permute-start | bytes 24584 | tf_op jit(solution)/shard_map/ppermute | solution.py:222
  88.7 0.8 collective-permute-done.15.partner_ref
  89.5 2.7 %all-to-all-done.3.from_first_ref = bf16[16,8,256]{2,1,0:T(8,128)(2,1)S(1)} async-done(((bf16[16,8,256]{2,1,0:T(8,128)(2,1)}), bf16[16,8,256]{2,1,0:T(8,128)(2,1)S(1)}, u32[]{:S(2)}, u32[]{:S(2)}) %all-to-all-start.3) | async-done | bytes 65568 | tf_op jit(solution)/shard_map/all_to_all | solution.py:259
  92.2 0.8 last_step.1
  93.0 8.2 %all-to-all-start.4 = ((f32[128,1,128]{2,1,0:T(1,128)}), f32[128,1,128]{2,1,0:T(1,128)S(1)}, u32[]{:S(2)}, u32[]{:S(2)}) async-start(f32[128,1,128]{2,1,0:T(1,128)} %bitcast.10), calls=%async_computation.4 | async-start | bytes 131072 | tf_op jit(solution)/shard_map/all_to_all | solution.py:270
  101.2 0.9 from_order.1
  102.1 8.9 %all-to-all-done.4 = f32[128,1,128]{2,1,0:T(1,128)S(1)} async-done(((f32[128,1,128]{2,1,0:T(1,128)}), f32[128,1,128]{2,1,0:T(1,128)S(1)}, u32[]{:S(2)}, u32[]{:S(2)}) %all-to-all-start.4) | async-done | bytes 65568 | tf_op jit(solution)/shard_map/all_to_all | solution.py:270
  111.0 0.6 slice_reduce_fusion
  (21 shorter events, 0.1 us)
Async XLA Ops:
  0.6 0.7 copy-start.6
  1.3 0.7 copy-start.8
  2.9 18.2 %all-to-all-start = ((bf16[16,8,256]{2,1,0:T(8,128)(2,1)}), bf16[16,8,256]{2,1,0:T(8,128)(2,1)S(1)}, u32[]{:S(2)}, u32[]{:S(2)}) async-start(bf16[16,8,256]{2,1,0:T(8,128)(2,1)} %get-tuple-element.19), calls=%async_computation | async-start | bytes 131072 | tf_op jit(solution)/shard_map/all_to_all | solution.py:254
  11.3 2.8 %collective-permute-start = (f32[8,256]{1,0:T(8,128)S(1)}, f32[8,256]{1,0:T(8,128)S(1)}, u32[]{:S(2)}, u32[]{:S(2)}) collective-permute-start(f32[8,256]{1,0:T(8,128)S(1)} %get-tuple-element.20.own_ref), channel_id=1, source_target_pairs={{0,16},{16,0},{32,48},{48,32},{64,80},{80,64},{96,112},{112,96},{1... | collective-permute-start | bytes 24584 | tf_op jit(solution)/shard_map/ppermute | solution.py:222
  14.1 4.2 %collective-permute-start.3 = (f32[16,256]{1,0:T(8,128)S(1)}, f32[16,256]{1,0:T(8,128)S(1)}, u32[]{:S(2)}, u32[]{:S(2)}) collective-permute-start(f32[16,256]{1,0:T(8,128)S(1)} %constant_dynamic-update-slice_fusion), channel_id=1, source_target_pairs={{0,96},{16,112},{32,64},{48,80},{64,32},{80,48},{96,0},{112,16},{1... | collective-permute-start | bytes 49160 | tf_op jit(solution)/shard_map/ppermute | solution.py:222
  16.9 4.1 %collective-permute-start.2 = (f32[16,256]{1,0:T(8,128)S(1)}, f32[16,256]{1,0:T(8,128)S(1)}, u32[]{:S(2)}, u32[]{:S(2)}) collective-permute-start(f32[16,256]{1,0:T(8,128)S(1)} %constant_dynamic-update-slice_fusion), channel_id=1, source_target_pairs={{0,64},{16,80},{32,96},{48,112},{64,0},{80,16},{96,32},{112,48},{1... | collective-permute-start | bytes 49160 | tf_op jit(solution)/shard_map/ppermute | solution.py:222
  17.3 3.7 %collective-permute-start.1 = (f32[16,256]{1,0:T(8,128)S(1)}, f32[16,256]{1,0:T(8,128)S(1)}, u32[]{:S(2)}, u32[]{:S(2)}) collective-permute-start(f32[16,256]{1,0:T(8,128)S(1)} %constant_dynamic-update-slice_fusion), channel_id=1, source_target_pairs={{0,32},{16,48},{32,0},{48,16},{64,96},{80,112},{96,64},{112,80},{1... | collective-permute-start | bytes 49160 | tf_op jit(solution)/shard_map/ppermute | solution.py:222
  21.0 2.2 %copy-start = (bf16[128,64,256]{2,1,0:T(8,128)(2,1)S(1)}, bf16[128,64,256]{2,1,0:T(8,128)(2,1)}, u32[]{:S(2)}) copy-start(bf16[128,64,256]{2,1,0:T(8,128)(2,1)} %param.11) | copy-start | bytes 12582916
  23.2 2.2 %copy-start.2 = (bf16[128,64,256]{2,1,0:T(8,128)(2,1)S(1)}, bf16[128,64,256]{2,1,0:T(8,128)(2,1)}, u32[]{:S(2)}) copy-start(bf16[128,64,256]{2,1,0:T(8,128)(2,1)} %param.12) | copy-start | bytes 12582916
  25.4 1.2 %copy-start.4 = (bf16[8,256,256]{2,1,0:T(8,128)(2,1)S(1)}, bf16[8,256,256]{2,1,0:T(8,128)(2,1)}, u32[]{:S(2)}) copy-start(bf16[8,256,256]{2,1,0:T(8,128)(2,1)} %near_hbm.3) | copy-start | bytes 3145732
  26.6 20.4 %copy-start.7 = (s32[2048]{0:T(1024)S(1)}, s32[2048]{0:T(1024)}, u32[]{:S(2)}) copy-start(s32[2048]{0:T(1024)} %param.15) | copy-start | bytes 24580
  26.7 20.4 %copy-start.9 = (f32[2,2048]{1,0:T(2,128)S(1)}, f32[2,2048]{1,0:T(2,128)}, u32[]{:S(2)}) copy-start(f32[2,2048]{1,0:T(2,128)} %state_ref.3) | copy-start | bytes 49156
  26.7 20.4 %copy-start.10 = (f32[3,2048]{1,0:T(4,128)S(1)}, f32[3,2048]{1,0:T(4,128)}, u32[]{:S(2)}) copy-start(f32[3,2048]{1,0:T(4,128)} %friction_ref.1) | copy-start | bytes 73732
  26.7 38.8 %copy-start.5 = (bf16[8,256,256]{2,1,0:T(8,128)(2,1)S(1)}, bf16[8,256,256]{2,1,0:T(8,128)(2,1)}, u32[]{:S(2)}) copy-start(bf16[8,256,256]{2,1,0:T(8,128)(2,1)} %near_hbm.3) | copy-start | bytes 3145732
  33.5 10.8 %collective-permute-start.4 = (f32[16,256]{1,0:T(8,128)S(1)}, f32[16,256]{1,0:T(8,128)S(1)}, u32[]{:S(2)}, u32[]{:S(2)}) collective-permute-start(f32[16,256]{1,0:T(8,128)S(1)} %get-tuple-element.23), channel_id=1, source_target_pairs={{0,32},{16,48},{32,0},{48,16},{64,96},{80,112},{96,64},{112,80},{1... | collective-permute-start | bytes 49160 | tf_op jit(solution)/shard_map/ppermute | solution.py:222
  33.6 10.7 %collective-permute-start.5 = (f32[16,256]{1,0:T(8,128)S(1)}, f32[16,256]{1,0:T(8,128)S(1)}, u32[]{:S(2)}, u32[]{:S(2)}) collective-permute-start(f32[16,256]{1,0:T(8,128)S(1)} %get-tuple-element.24), channel_id=1, source_target_pairs={{0,64},{16,80},{32,96},{48,112},{64,0},{80,16},{96,32},{112,48},{1... | collective-permute-start | bytes 49160 | tf_op jit(solution)/shard_map/ppermute | solution.py:222
  35.8 8.5 %collective-permute-start.6 = (f32[16,256]{1,0:T(8,128)S(1)}, f32[16,256]{1,0:T(8,128)S(1)}, u32[]{:S(2)}, u32[]{:S(2)}) collective-permute-start(f32[16,256]{1,0:T(8,128)S(1)} %get-tuple-element.25), channel_id=1, source_target_pairs={{0,96},{16,112},{32,64},{48,80},{64,32},{80,48},{96,0},{112,16},{1... | collective-permute-start | bytes 49160 | tf_op jit(solution)/shard_map/ppermute | solution.py:222
  37.5 13.4 %all-to-all-start.1 = ((bf16[16,8,256]{2,1,0:T(8,128)(2,1)}), bf16[16,8,256]{2,1,0:T(8,128)(2,1)S(1)}, u32[]{:S(2)}, u32[]{:S(2)}) async-start(bf16[16,8,256]{2,1,0:T(8,128)(2,1)} %bitcast.6), calls=%async_computation.1 | async-start | bytes 131072 | tf_op jit(solution)/shard_map/all_to_all | solution.py:259
  44.4 3.5 %collective-permute-start.7 = (f32[8,256]{1,0:T(8,128)S(1)}, f32[8,256]{1,0:T(8,128)S(1)}, u32[]{:S(2)}, u32[]{:S(2)}) collective-permute-start(f32[8,256]{1,0:T(8,128)S(1)} %get-tuple-element.38), channel_id=1, source_target_pairs={{0,16},{16,0},{32,48},{48,32},{64,80},{80,64},{96,112},{112,96},{1... | collective-permute-start | bytes 24584 | tf_op jit(solution)/shard_map/ppermute | solution.py:222
  51.5 7.2 %collective-permute-start.8 = (f32[8,256]{1,0:T(8,128)S(1)}, f32[8,256]{1,0:T(8,128)S(1)}, u32[]{:S(2)}, u32[]{:S(2)}) collective-permute-start(f32[8,256]{1,0:T(8,128)S(1)} %get-tuple-element.27.own_ref), channel_id=1, source_target_pairs={{0,16},{16,0},{32,48},{48,32},{64,80},{80,64},{96,112},{112,96},{1... | collective-permute-start | bytes 24584 | tf_op jit(solution)/shard_map/ppermute | solution.py:222
  55.2 10.2 %all-to-all-start.2 = ((bf16[16,8,256]{2,1,0:T(8,128)(2,1)}), bf16[16,8,256]{2,1,0:T(8,128)(2,1)S(1)}, u32[]{:S(2)}, u32[]{:S(2)}) async-start(bf16[16,8,256]{2,1,0:T(8,128)(2,1)} %get-tuple-element.26), calls=%async_computation.2 | async-start | bytes 131072 | tf_op jit(solution)/shard_map/all_to_all | solution.py:254
  58.7 3.9 %collective-permute-start.11 = (f32[16,256]{1,0:T(8,128)S(1)}, f32[16,256]{1,0:T(8,128)S(1)}, u32[]{:S(2)}, u32[]{:S(2)}) collective-permute-start(f32[16,256]{1,0:T(8,128)S(1)} %constant_dynamic-update-slice_fusion.2), channel_id=1, source_target_pairs={{0,96},{16,112},{32,64},{48,80},{64,32},{80,48},{96,0},{112,16},{1... | collective-permute-start | bytes 49160 | tf_op jit(solution)/shard_map/ppermute | solution.py:222
  59.8 4.4 %collective-permute-start.10 = (f32[16,256]{1,0:T(8,128)S(1)}, f32[16,256]{1,0:T(8,128)S(1)}, u32[]{:S(2)}, u32[]{:S(2)}) collective-permute-start(f32[16,256]{1,0:T(8,128)S(1)} %constant_dynamic-update-slice_fusion.2), channel_id=1, source_target_pairs={{0,64},{16,80},{32,96},{48,112},{64,0},{80,16},{96,32},{112,48},{1... | collective-permute-start | bytes 49160 | tf_op jit(solution)/shard_map/ppermute | solution.py:222
  59.8 4.4 %collective-permute-start.9 = (f32[16,256]{1,0:T(8,128)S(1)}, f32[16,256]{1,0:T(8,128)S(1)}, u32[]{:S(2)}, u32[]{:S(2)}) collective-permute-start(f32[16,256]{1,0:T(8,128)S(1)} %constant_dynamic-update-slice_fusion.2), channel_id=1, source_target_pairs={{0,32},{16,48},{32,0},{48,16},{64,96},{80,112},{96,64},{112,80},{1... | collective-permute-start | bytes 49160 | tf_op jit(solution)/shard_map/ppermute | solution.py:222
  65.5 2.2 %copy-start.1 = (bf16[128,64,256]{2,1,0:T(8,128)(2,1)S(1)}, bf16[128,64,256]{2,1,0:T(8,128)(2,1)}, u32[]{:S(2)}) copy-start(bf16[128,64,256]{2,1,0:T(8,128)(2,1)} %param.11) | copy-start | bytes 12582916
  67.7 2.2 %copy-start.3 = (bf16[128,64,256]{2,1,0:T(8,128)(2,1)S(1)}, bf16[128,64,256]{2,1,0:T(8,128)(2,1)}, u32[]{:S(2)}) copy-start(bf16[128,64,256]{2,1,0:T(8,128)(2,1)} %param.12) | copy-start | bytes 12582916
  76.7 9.0 %collective-permute-start.12 = (f32[16,256]{1,0:T(8,128)S(1)}, f32[16,256]{1,0:T(8,128)S(1)}, u32[]{:S(2)}, u32[]{:S(2)}) collective-permute-start(f32[16,256]{1,0:T(8,128)S(1)} %get-tuple-element.30), channel_id=1, source_target_pairs={{0,32},{16,48},{32,0},{48,16},{64,96},{80,112},{96,64},{112,80},{1... | collective-permute-start | bytes 49160 | tf_op jit(solution)/shard_map/ppermute | solution.py:222
  76.8 8.9 %collective-permute-start.13 = (f32[16,256]{1,0:T(8,128)S(1)}, f32[16,256]{1,0:T(8,128)S(1)}, u32[]{:S(2)}, u32[]{:S(2)}) collective-permute-start(f32[16,256]{1,0:T(8,128)S(1)} %get-tuple-element.31), channel_id=1, source_target_pairs={{0,64},{16,80},{32,96},{48,112},{64,0},{80,16},{96,32},{112,48},{1... | collective-permute-start | bytes 49160 | tf_op jit(solution)/shard_map/ppermute | solution.py:222
  79.0 6.8 %collective-permute-start.14 = (f32[16,256]{1,0:T(8,128)S(1)}, f32[16,256]{1,0:T(8,128)S(1)}, u32[]{:S(2)}, u32[]{:S(2)}) collective-permute-start(f32[16,256]{1,0:T(8,128)S(1)} %get-tuple-element.32), channel_id=1, source_target_pairs={{0,96},{16,112},{32,64},{48,80},{64,32},{80,48},{96,0},{112,16},{1... | collective-permute-start | bytes 49160 | tf_op jit(solution)/shard_map/ppermute | solution.py:222
  80.6 11.6 %all-to-all-start.3 = ((bf16[16,8,256]{2,1,0:T(8,128)(2,1)}), bf16[16,8,256]{2,1,0:T(8,128)(2,1)S(1)}, u32[]{:S(2)}, u32[]{:S(2)}) async-start(bf16[16,8,256]{2,1,0:T(8,128)(2,1)} %bitcast.8), calls=%async_computation.3 | async-start | bytes 131072 | tf_op jit(solution)/shard_map/all_to_all | solution.py:259
  85.8 3.7 %collective-permute-start.15 = (f32[8,256]{1,0:T(8,128)S(1)}, f32[8,256]{1,0:T(8,128)S(1)}, u32[]{:S(2)}, u32[]{:S(2)}) collective-permute-start(f32[8,256]{1,0:T(8,128)S(1)} %get-tuple-element.36), channel_id=1, source_target_pairs={{0,16},{16,0},{32,48},{48,32},{64,80},{80,64},{96,112},{112,96},{1... | collective-permute-start | bytes 24584 | tf_op jit(solution)/shard_map/ppermute | solution.py:222
  93.0 18.0 %all-to-all-start.4 = ((f32[128,1,128]{2,1,0:T(1,128)}), f32[128,1,128]{2,1,0:T(1,128)S(1)}, u32[]{:S(2)}, u32[]{:S(2)}) async-start(f32[128,1,128]{2,1,0:T(1,128)} %bitcast.10), calls=%async_computation.4 | async-start | bytes 131072 | tf_op jit(solution)/shard_map/all_to_all | solution.py:270

commit v2 on v1

v2 whole, which is shorter than its diff:
```python
import functools

import jax
import jax.numpy as jnp
from jax import lax
from jax.experimental import pallas as pl
from jax.experimental.pallas import tpu as pltpu
from jax.sharding import PartitionSpec as P

step_size = 0.1
damping = 0.5
abs_tol = 0.001
rel_tol = 0.001

f32 = jnp.float32
bf16 = jnp.bfloat16
LANES = 128
PAIRS = 16
VMEM = pl.BlockSpec(memory_space=pltpu.VMEM)


def mxu(a, b):
    return lax.dot_general(a, b, (((1,), (0,)), ((), ())), preferred_element_type=f32)


def mxu_nt(a, b):
    return lax.dot_general(a, b, (((1,), (1,)), ((), ())), preferred_element_type=f32)


def to_tiles(row):
    return jnp.concatenate([row[:, k * LANES:(k + 1) * LANES] for k in range(row.shape[1] // LANES)], axis=0)


def to_row(tiles):
    return jnp.concatenate([tiles[k:k + 1, :] for k in range(tiles.shape[0])], axis=1)


def to_clusters(row, cluster):
    return jnp.concatenate([row[:, k * cluster:(k + 1) * cluster] for k in range(row.shape[1] // cluster)], axis=0)


def split3(x):
    hi = x.astype(bf16)
    rest = x - hi.astype(f32)
    mid = rest.astype(bf16)
    low = (rest - mid.astype(f32)).astype(bf16)
    return hi, mid, low


def place(perm_row, tiles):
    count = perm_row.shape[1]
    local = lax.rem(perm_row, count)
    tile = lax.div(local, LANES)
    lane = local - tile * LANES
    at_tile = lax.broadcasted_iota(jnp.int32, (tiles, count), 0) == tile
    at_lane = lax.broadcasted_iota(jnp.int32, (LANES, count), 0) == lane
    return at_tile, jnp.where(at_lane, 1.0, 0.0).astype(bf16)


def first_deficit(state_ref, perm_ref, own_ref):
    cluster = own_ref.shape[1]
    at_tile, at_lane = place(perm_ref[...], perm_ref.shape[1] // LANES)
    deficit = to_tiles(1.0 - jnp.exp(state_ref[0:1, :])).astype(bf16)
    picked = jnp.where(at_tile, mxu(deficit, at_lane), 0.0)
    own_ref[...] = to_clusters(jnp.sum(picked, axis=0, keepdims=True), cluster)


def to_order(state_ref, friction_ref, perm_ref, fields_ref):
    cluster = fields_ref.shape[2]
    tiles = perm_ref.shape[1] // LANES
    at_tile, at_lane = place(perm_ref[...], tiles)
    coef_a, coef_b, sigma = (friction_ref[k:k + 1, :] for k in range(3))
    rows = (state_ref[0:1, :], state_ref[1:2, :], coef_a * sigma, coef_b * sigma)
    parts = [part for row in rows for part in split3(to_tiles(row))]
    moved = mxu(jnp.concatenate(parts, axis=0), at_lane)
    for k in range(len(rows)):
        three = [moved[(3 * k + s) * tiles:(3 * k + s + 1) * tiles] for s in range(3)]
        picked = jnp.where(at_tile, (three[0] + three[1]) + three[2], 0.0)
        fields_ref[k] = to_clusters(jnp.sum(picked, axis=0, keepdims=True), cluster)


def from_order(new_ref, perm_ref, out_ref):
    tiles = perm_ref.shape[1] // LANES
    at_tile, at_lane = place(perm_ref[...], tiles)
    parts = []
    for k in range(2):
        row = to_row_of_clusters(new_ref[k])
        parts += [jnp.where(at_tile, part.astype(f32), 0.0).astype(bf16) for part in split3(row)]
    moved = mxu_nt(jnp.concatenate(parts, axis=0), at_lane)
    for k in range(2):
        three = [moved[(3 * k + s) * tiles:(3 * k + s + 1) * tiles] for s in range(3)]
        out_ref[k:k + 1, :] = to_row((three[0] + three[1]) + three[2])


def to_row_of_clusters(x):
    return jnp.concatenate([x[k:k + 1, :] for k in range(x.shape[0])], axis=1)


def one_hot(mask):
    return jnp.where(mask, 1.0, 0.0).astype(bf16)


def collect(mask, terms):
    hot = one_hot(mask)
    high, mid, low = split3(terms)
    return mxu(hot, high) + (mxu(hot, mid) + mxu(hot, low))


def picked(at, values):
    hot = one_hot(lax.broadcasted_iota(jnp.int32, (at.shape[0], values.shape[0]), 1) == at)
    return mxu(hot, values).astype(bf16)


def stress_terms(chunk, everyone_ref, line_ref, more_ref, info_ref, col_ref, left_hbm, right_hbm, first_ref, kept_ref,
                 sent_ref, left, right, sem):
    pairs = info_ref.shape[1]
    width = left.shape[0] // pairs
    chunks = left.shape[0] // chunk

    def fetch(k):
        part = pl.ds(k * chunk, chunk)
        return (
            pltpu.make_async_copy(right_hbm.at[part], right.at[part], sem.at[0, k]),
            pltpu.make_async_copy(left_hbm.at[part], left.at[part], sem.at[1, k]),
        )

    for k in range(chunks):
        for copy in fetch(k):
            copy.start()
    line = jnp.concatenate([line_ref[...], more_ref[...]], axis=0).astype(bf16)
    x_first = picked(col_ref[:, 0:1], everyone_ref[...])
    x_second = picked(col_ref[:, 1:2], line)
    shape = (PAIRS, PAIRS * width)
    rank = lax.broadcasted_iota(jnp.int32, shape, 1) - width * lax.broadcasted_iota(jnp.int32, shape, 0)
    to_first, to_second = [], []
    for k in range(pairs // PAIRS):
        if k * shape[1] % chunk == 0:
            for copy in fetch(k * shape[1] // chunk):
                copy.wait()
        rows = slice(k * PAIRS, (k + 1) * PAIRS)
        part = pl.ds(k * shape[1], shape[1])
        within = (rank >= 0) & (rank < col_ref[rows, 2:3])
        coef_j = jnp.where(within, mxu_nt(x_second[rows], right[part]), 0.0).astype(bf16)
        coef_i = jnp.where(within, mxu_nt(x_first[rows], left[part]), 0.0).astype(bf16)
        to_first.append(mxu(coef_j, left[part]))
        to_second.append(mxu(coef_i, right[part]))
    first_ref[...] = sums_at(info_ref, 0, first_ref.shape[0], jnp.concatenate(to_first, axis=0)).astype(bf16)
    halves(sums_at(info_ref, 1, 2 * kept_ref.shape[0], jnp.concatenate(to_second, axis=0)), kept_ref, sent_ref)


def sums_at(info_ref, side, rows, terms):
    at = lax.broadcasted_iota(jnp.int32, (rows, info_ref.shape[1]), 0) == info_ref[side:side + 1, :]
    return collect(at, terms)


def halves(x, kept_ref, sent_ref):
    step = kept_ref.shape[0]
    kept_ref[...] = x[:step]
    sent_ref[...] = x[step:].astype(sent_ref.dtype)


def join(held_ref, received_ref, out_ref):
    out_ref[...] = jnp.concatenate([held_ref[...], received_ref[...]], axis=0)


def join_and_spread(held_ref, received_ref, out_ref, copies_ref):
    join(held_ref, received_ref, out_ref)
    for k in range(copies_ref.shape[0]):
        copies_ref[k] = held_ref[...].astype(bf16)


def add(held_ref, received_ref, *out_refs):
    halves(held_ref[...] + received_ref[...], *out_refs)


def place_of(difference):
    return difference ^ ((difference >> 1) & 1)


def pair_info(own_count, columns, pairs_ref, ranks_ref, info_ref, col_ref):
    row = lax.axis_index("row")
    owner = lax.div(pairs_ref[...], own_count)
    inside = pairs_ref[...] - owner * own_count
    owner_row = lax.div(owner, columns)
    by_row = owner_row ^ row
    first_at = (owner - owner_row * columns) * own_count + inside
    second_at = ((by_row & 1) + 2 * place_of(by_row >> 1)) * own_count + inside
    count = ranks_ref.shape[1]
    sublane = lax.broadcasted_iota(jnp.int32, (count, LANES), 0)
    lane = lax.broadcasted_iota(jnp.int32, (count, LANES), 1)
    rank = jnp.sum(jnp.where(sublane == lane, jnp.broadcast_to(ranks_ref[...], (count, LANES)), 0), axis=1, keepdims=True)
    columns_of = jnp.where(lane == 0, first_at[:, 0:1], jnp.where(lane == 1, second_at[:, 1:2], rank))
    col_ref[...] = columns_of
    info_ref[...] = jnp.transpose(columns_of)[:info_ref.shape[0]]


def near_terms(own_ref, near, out_ref):
    own = own_ref[...]
    row_own = lax.broadcasted_iota(jnp.int32, own.shape, 0)
    mine = own.astype(bf16)
    total = jnp.zeros(own.shape, f32)
    for k in range(own.shape[0]):
        total += jnp.where(row_own == k, mxu(mine, near[k]), 0.0)
    out_ref[...] = total


def slopes(lv, lt, a_sigma, b_sigma, stress):
    rate = jnp.exp(lv)
    dlt = jnp.exp(-lt) - rate
    return (stress - b_sigma * dlt) / (a_sigma + damping * rate), dlt


def total_stress(refs):
    near_ref, from_first_ref, kept_ref, received_ref = refs
    parts = [from_first_ref[k].astype(f32) for k in range(from_first_ref.shape[0])]
    while len(parts) > 1:
        parts = [parts[k] + parts[k + 1] for k in range(0, len(parts), 2)]
    return (near_ref[...] + parts[0]) + (kept_ref[...] + received_ref[...])


def half_step(*refs):
    *stress_refs, fields_ref, slope_ref, own_ref = refs
    lv, lt, a_sigma, b_sigma = (fields_ref[k] for k in range(4))
    dlv, dlt = slopes(lv, lt, a_sigma, b_sigma, total_stress(stress_refs))
    slope_ref[0] = dlv
    slope_ref[1] = dlt
    own_ref[...] = (1.0 - jnp.exp(lv + step_size * dlv)).astype(bf16).astype(f32)


def last_step(*refs):
    *stress_refs, fields_ref, slope_ref, new_ref, sum_ref = refs
    lv, lt, a_sigma, b_sigma = (fields_ref[k] for k in range(4))
    first = (slope_ref[0], slope_ref[1])
    second = slopes(lv + step_size * first[0], lt + step_size * first[1], a_sigma, b_sigma, total_stress(stress_refs))
    squares = jnp.zeros(lv.shape, f32)
    for k, base in enumerate((lv, lt)):
        new = base + 0.5 * step_size * (first[k] + second[k])
        new_ref[k] = new
        scaled = 0.5 * step_size * (second[k] - first[k]) / (abs_tol + rel_tol * jnp.abs(new))
        squares += scaled * scaled
    sum_ref[...] = jnp.full(sum_ref.shape, jnp.sum(squares), f32)


def in_hbm(x):
    return pltpu.with_memory_space_constraint(x, pltpu.HBM)


def call(kernel, out_shape, inputs, micros, scratch=(), streamed=()):
    many = isinstance(out_shape, (list, tuple))
    name = getattr(kernel, "func", kernel).__name__
    return pl.pallas_call(
        kernel,
        out_shape=out_shape,
        in_specs=[pl.BlockSpec(memory_space=pl.ANY) if any(x is y for y in streamed) else VMEM for x in inputs],
        out_specs=[VMEM] * len(out_shape) if many else VMEM,
        name=name,
        scratch_shapes=list(scratch),
        cost_estimate=pl.CostEstimate(flops=int(micros * 1.1e9), bytes_accessed=0, transcendentals=0),
        compiler_params=pltpu.CompilerParams(vmem_limit_bytes=32 * 1024 * 1024),
    )(*inputs)


def shards(rows, columns, state, friction, near_blocks, left_factor, right_factor, pairs, ranks, perm):
    own_count, cluster = near_blocks.shape[:2]
    count, width = left_factor.shape[:2]
    span = columns * own_count
    sds = jax.ShapeDtypeStruct
    block = sds((own_count, cluster), f32)
    perm_row = perm.reshape(1, -1)

    def swap(x, axis, distance):
        size = rows if axis == "row" else columns
        return lax.ppermute(x, axis, [(r, r ^ distance) for r in range(size)])

    own = call(first_deficit, block, [in_hbm(state), in_hbm(perm_row)], 6)
    fields = call(to_order, sds((4, own_count, cluster), f32), [state, friction, perm_row], 0.5)

    info, info_col = call(
        functools.partial(pair_info, own_count, columns),
        [sds((8, count), jnp.int32), sds((count, LANES), jnp.int32)], [pairs, ranks.reshape(1, -1)], 0.5)
    near = near_blocks
    left = in_hbm(left_factor.reshape(count * width, cluster))
    right = in_hbm(right_factor.reshape(count * width, cluster))

    def block_of(blocks, dtype):
        return sds((blocks * own_count, cluster), dtype)

    chunk = 2048
    scratch = [pltpu.VMEM(left.shape, bf16), pltpu.VMEM(right.shape, bf16),
               pltpu.SemaphoreType.DMA((2, count * width // chunk))]

    def exchange(own):
        two, copies = call(join_and_spread, [block_of(2, f32), sds((columns, own_count, cluster), bf16)],
                           [own, swap(own, "row", 1)], 0.2)
        four = call(join, block_of(4, f32), [two, swap(two, "row", 2)], 0.2)
        more = swap(four, "row", 6)
        everyone = lax.all_to_all(copies, "col", 0, 0).reshape(span, cluster)
        near_term = call(near_terms, block, [own, near], 0.3)
        first, kept, sent = call(
            functools.partial(stress_terms, chunk), [block_of(columns, bf16)] + [block_of(4, f32)] * 2,
            [everyone, four, more, info, info_col, left, right], 6, scratch, (left, right))
        for blocks, hop in ((2, 6), (1, 2)):
            kept, sent = call(add, [block_of(blocks, f32)] * 2, [kept, swap(sent, "row", hop)], 0.2)
        from_first = lax.all_to_all(first.reshape(columns, own_count, cluster), "col", 0, 0)
        return [near_term, from_first, kept, swap(sent, "row", 1)]

    slope, own = call(half_step, [sds((2, own_count, cluster), f32), block], [*exchange(own), fields], 0.1)
    devices = rows * columns
    new, squares = call(last_step, [sds((2, own_count, cluster), f32), sds((devices, LANES), f32)],
                        [*exchange(own), fields, slope], 0.8)
    everywhere = lax.all_to_all(squares, ("row", "col"), 0, 0, tiled=True)
    new_state = call(from_order, sds(state.shape, f32), [new, perm_row], 0.9)
    entries = 2.0 * state.shape[1] * devices
    return new_state, jnp.sqrt(jnp.sum(everywhere[:, 0]) / entries)


def solution(mesh):
    both = ("row", "col")
    placed = (P(None, both), P(None, both), P(both, None, None), P(both, None, None), P(both, None, None),
              P(both, None), P(both), P(both))
    return jax.shard_map(
        functools.partial(shards, mesh.shape["row"], mesh.shape["col"]),
        mesh=mesh,
        in_specs=placed,
        out_specs=(P(None, both), P()),
        check_vma=False,
    )
```

time: 114 us -> 99.7 us (0.87)
  local copies, waits for them, and re-layouts: 11.6 us -> 0.14 us
  starting transfers between devices: 57 us -> 49.1 us
  waiting for transfers between devices: 22.5 us -> 29 us
  other arithmetic: 2.23 us -> 0.62 us
    unnamed x24 -> x13, local copies, waits for them, and re-layouts: 11.4 us -> 0.14 us
    ppermute x16 -> x12, waiting for transfers between devices: 6.73 us -> 13.2 us  [swap(): return lax.ppermute(x, axis, [(r, r ^ distance) for r in range(size)])]
    ppermute x16 -> x12, starting transfers between devices: 25 us -> 19.6 us  [swap(): return lax.ppermute(x, axis, [(r, r ^ distance) for r in range(size)])]
    all_to_all x2, starting transfers between devices: 11.9 us -> 8.2 us  [exchange(): lax.all_to_all(first.reshape(columns, own_count, cluster), 'col', 0, 0)]
    all_to_all x2, waiting for transfers between devices: 1.23 us -> 4.89 us  [exchange(): everyone = lax.all_to_all(copies, 'col', 0, 0).reshape(span, cluster)]
    all_to_all x2, waiting for transfers between devices: 5.71 us -> 2.1 us  [exchange(): lax.all_to_all(first.reshape(columns, own_count, cluster), 'col', 0, 0)]
    all_to_all x1, starting transfers between devices: 8.16 us -> 9.38 us  [shards(): everywhere = lax.all_to_all(squares, ('row', 'col'), 0, 0, tiled=True)]
    pallas_call x7 -> x18, Pallas kernels: 17.3 us -> 17.8 us  [call(): pl.pallas_call(kernel, out_shape=out_shape, in_specs=[pl.BlockSpec(memory...]
  transfers between devices with their start and end apart: 21 -> 17, of which waited for: 10 -> 12; matrix products, arithmetic and copies ran while one was open for 2% -> 0% of each run, Pallas kernels for 1% -> 2%
where the time goes in v2:
time: 99.7 us; the launch traced here: 99.3 us
  starting transfers between devices  49.1 us (49%)
  waiting for transfers between devices  29 us (29%)
  Pallas kernels  17.8 us (18%)
  between operations  2.65 us (3%)
    ppermute x12, starting transfers between devices, swap(): return lax.ppermute(x, axis, [(r, r ^ distance) for r in range(size)])  19.6 us
    pallas_call x18, Pallas kernels, call(): pl.pallas_call(kernel, out_shape=out_shape, in_specs=[pl.BlockSpec(memory...  17.8 us
    ppermute x12, waiting for transfers between devices, swap(): return lax.ppermute(x, axis, [(r, r ^ distance) for r in range(size)])  13.2 us
    all_to_all x2, starting transfers between devices, exchange(): everyone = lax.all_to_all(copies, 'col', 0, 0).reshape(span, cluster)  11.9 us
    all_to_all x1, starting transfers between devices, shards(): everywhere = lax.all_to_all(squares, ('row', 'col'), 0, 0, tiled=True)  9.38 us
    all_to_all x1, waiting for transfers between devices, shards(): everywhere = lax.all_to_all(squares, ('row', 'col'), 0, 0, tiled=True)  8.85 us
    all_to_all x2, starting transfers between devices, exchange(): lax.all_to_all(first.reshape(columns, own_count, cluster), 'col', 0, 0)  8.2 us
    all_to_all x2, waiting for transfers between devices, exchange(): everyone = lax.all_to_all(copies, 'col', 0, 0).reshape(span, cluster)  4.89 us
  transfers between devices with their start and end apart: 17, of which 12 were waited for; matrix products, arithmetic and copies ran while one was open for 0% of the time, Pallas kernels for 2%

profile of v2, /device:TPU:1, one launch (start us, length us, event | category | flops | bytes accessed | tf_op | source)
XLA Modules:
  0.0 99.3 jit_solution(16736994429528207677)
XLA Ops:
  0.6 0.0 copy-start.5
  0.6 0.0 copy-start.4
  0.6 0.9 first_deficit.1.own_ref.held_ref
  1.6 1.5 %collective-permute-start = (f32[8,256]{1,0:T(8,128)S(1)}, f32[8,256]{1,0:T(8,128)S(1)}, u32[]{:S(2)}, u32[]{:S(2)}) collective-permute-start(f32[8,256]{1,0:T(8,128)S(1)} %first_deficit.1.own_ref.held_ref), channel_id=1, source_target_pairs={{0,16},{16,0},{32,48},{48,32},{64,80},{80,64},{96,112},{112,96},{1... | collective-permute-start | bytes 24584 | tf_op jit(solution)/shard_map/ppermute | solution.py:273
  3.1 0.8 collective-permute-done.received_ref
  3.9 0.6 join_and_spread.2
  4.6 1.4 %collective-permute-start.1 = (f32[16,256]{1,0:T(8,128)S(1)}, f32[16,256]{1,0:T(8,128)S(1)}, u32[]{:S(2)}, u32[]{:S(2)}) collective-permute-start(f32[16,256]{1,0:T(8,128)S(1)} %get-tuple-element.27.held_ref), channel_id=1, source_target_pairs={{0,32},{16,48},{32,0},{48,16},{64,96},{80,112},{96,64},{112,80},{1... | collective-permute-start | bytes 49160 | tf_op jit(solution)/shard_map/ppermute | solution.py:273
  5.9 0.0 copy-done.5
  5.9 0.1 copy.11.pairs_ref
  6.1 7.6 %all-to-all-start = ((bf16[16,8,256]{2,1,0:T(8,128)(2,1)}), bf16[16,8,256]{2,1,0:T(8,128)(2,1)S(1)}, u32[]{:S(2)}, u32[]{:S(2)}) async-start(bf16[16,8,256]{2,1,0:T(8,128)(2,1)} %get-tuple-element.26), calls=%async_computation | async-start | bytes 131072 | tf_op jit(solution)/shard_map/all_to_all | solution.py:297
  13.7 0.0 collective-permute-done.1.received_ref
  13.7 2.0 %collective-permute-start.2 = (f32[32,256]{1,0:T(8,128)S(1)}, f32[32,256]{1,0:T(8,128)S(1)}, u32[]{:S(2)}, u32[]{:S(2)}) collective-permute-start(f32[32,256]{1,0:T(8,128)S(1)} %join.2.line_ref), channel_id=1, source_target_pairs={{0,96},{16,112},{32,64},{48,80},{64,32},{80,48},{96,0},{112,16},{1... | collective-permute-start | bytes 98312 | tf_op jit(solution)/shard_map/ppermute | solution.py:273
  15.7 0.0 copy-done.4
  15.7 0.2 pair_info.1
  15.9 1.9 %collective-permute-done.2.more_ref = f32[32,256]{1,0:T(8,128)S(1)} collective-permute-done((f32[32,256]{1,0:T(8,128)S(1)}, f32[32,256]{1,0:T(8,128)S(1)}, u32[]{:S(2)}, u32[]{:S(2)}) %collective-permute-start.2) | collective-permute-done | bytes 32800 | tf_op jit(solution)/shard_map/ppermute | solution.py:273
  17.7 2.5 %all-to-all-done = bf16[16,8,256]{2,1,0:T(8,128)(2,1)S(1)} async-done(((bf16[16,8,256]{2,1,0:T(8,128)(2,1)}), bf16[16,8,256]{2,1,0:T(8,128)(2,1)S(1)}, u32[]{:S(2)}, u32[]{:S(2)}) %all-to-all-start) | async-done | bytes 65568 | tf_op jit(solution)/shard_map/all_to_all | solution.py:297
  20.2 0.0 copy-start.1
  20.2 0.0 copy-start.2
  20.2 0.0 copy-start.3
  20.2 0.0 copy-start
  20.2 6.4 %stress_terms.2 = (bf16[128,256]{1,0:T(8,128)(2,1)}, f32[32,256]{1,0:T(8,128)S(1)}, f32[32,256]{1,0:T(8,128)S(1)}) custom-call(bf16[128,256]{1,0:T(8,128)(2,1)S(1)} %bitcast.12, f32[32,256]{1,0:T(8,128)S(1)} %join.2.line_ref, f32[32,256]{1,0:T(8,128)S(1)} %collective-permute-done.2.more_ref, s32[8,128]{1,0:T(8,128)S(1)} %get-tuple-element.28.info_ref, ...), custom_call_target="tpu_custom_call" | custom-call | flops 6600000000 | tf_op jit(solution)/shard_map/stress_terms/pallas_call | solution.py:251
  26.6 2.0 %collective-permute-start.3 = (f32[32,256]{1,0:T(8,128)S(1)}, f32[32,256]{1,0:T(8,128)S(1)}, u32[]{:S(2)}, u32[]{:S(2)}) collective-permute-start(f32[32,256]{1,0:T(8,128)S(1)} %get-tuple-element.32), channel_id=1, source_target_pairs={{0,96},{16,112},{32,64},{48,80},{64,32},{80,48},{96,0},{112,16},{1... | collective-permute-start | bytes 98312 | tf_op jit(solution)/shard_map/ppermute | solution.py:273
  28.6 4.2 %all-to-all-start.1 = ((bf16[16,8,256]{2,1,0:T(8,128)(2,1)}), bf16[16,8,256]{2,1,0:T(8,128)(2,1)S(1)}, u32[]{:S(2)}, u32[]{:S(2)}) async-start(bf16[16,8,256]{2,1,0:T(8,128)(2,1)} %bitcast.5), calls=%async_computation.1 | async-start | bytes 131072 | tf_op jit(solution)/shard_map/all_to_all | solution.py:304
  32.8 0.0 collective-permute-done.3.received_ref
  32.8 0.1 collective-permute-start.4
  32.9 0.0 copy-done.1
  32.9 0.0 copy-done.2
  32.9 0.0 copy-done.3
  32.9 0.5 to_order.1.refs_4_
  33.4 2.1 %collective-permute-done.4.received_ref = f32[16,256]{1,0:T(8,128)S(1)} collective-permute-done((f32[16,256]{1,0:T(8,128)S(1)}, f32[16,256]{1,0:T(8,128)S(1)}, u32[]{:S(2)}, u32[]{:S(2)}) %collective-permute-start.4) | collective-permute-done | bytes 16416 | tf_op jit(solution)/shard_map/ppermute | solution.py:273
  35.5 4.0 %collective-permute-start.5 = (f32[8,256]{1,0:T(8,128)S(1)}, f32[8,256]{1,0:T(8,128)S(1)}, u32[]{:S(2)}, u32[]{:S(2)}) collective-permute-start(f32[8,256]{1,0:T(8,128)S(1)} %get-tuple-element.36), channel_id=1, source_target_pairs={{0,16},{16,0},{32,48},{48,32},{64,80},{80,64},{96,112},{112,96},{1... | collective-permute-start | bytes 24584 | tf_op jit(solution)/shard_map/ppermute | solution.py:273
  39.5 0.0 copy-done
  39.5 0.2 near_terms.2.refs_0_
  39.8 0.6 collective-permute-done.5.refs_3_
  40.4 0.0 all-to-all-done.1.refs_1_
  40.4 3.1 %collective-permute-start.6 = (f32[8,256]{1,0:T(8,128)S(1)}, f32[8,256]{1,0:T(8,128)S(1)}, u32[]{:S(2)}, u32[]{:S(2)}) collective-permute-start(f32[8,256]{1,0:T(8,128)S(1)} %get-tuple-element.37.own_ref.held_ref), channel_id=1, source_target_pairs={{0,16},{16,0},{32,48},{48,32},{64,80},{80,64},{96,112},{112,96},{1... | collective-permute-start | bytes 24584 | tf_op jit(solution)/shard_map/ppermute | solution.py:273
  43.5 0.8 collective-permute-done.6.received_ref
  44.3 0.6 join_and_spread.3
  44.9 0.0 collective-permute-start.7
  44.9 4.3 %all-to-all-start.2 = ((bf16[16,8,256]{2,1,0:T(8,128)(2,1)}), bf16[16,8,256]{2,1,0:T(8,128)(2,1)S(1)}, u32[]{:S(2)}, u32[]{:S(2)}) async-start(bf16[16,8,256]{2,1,0:T(8,128)(2,1)} %get-tuple-element.38), calls=%async_computation.2 | async-start | bytes 131072 | tf_op jit(solution)/shard_map/all_to_all | solution.py:297
  49.2 0.0 collective-permute-done.7.received_ref
  49.3 0.9 collective-permute-start.8
  50.1 3.2 %collective-permute-done.8.more_ref = f32[32,256]{1,0:T(8,128)S(1)} collective-permute-done((f32[32,256]{1,0:T(8,128)S(1)}, f32[32,256]{1,0:T(8,128)S(1)}, u32[]{:S(2)}, u32[]{:S(2)}) %collective-permute-start.8) | collective-permute-done | bytes 32800 | tf_op jit(solution)/shard_map/ppermute | solution.py:273
  53.3 2.4 %all-to-all-done.2 = bf16[16,8,256]{2,1,0:T(8,128)(2,1)S(1)} async-done(((bf16[16,8,256]{2,1,0:T(8,128)(2,1)}), bf16[16,8,256]{2,1,0:T(8,128)(2,1)S(1)}, u32[]{:S(2)}, u32[]{:S(2)}) %all-to-all-start.2) | async-done | bytes 65568 | tf_op jit(solution)/shard_map/all_to_all | solution.py:297
  55.7 6.3 %stress_terms.3 = (bf16[128,256]{1,0:T(8,128)(2,1)}, f32[32,256]{1,0:T(8,128)S(1)}, f32[32,256]{1,0:T(8,128)S(1)}) custom-call(bf16[128,256]{1,0:T(8,128)(2,1)S(1)} %bitcast.13, f32[32,256]{1,0:T(8,128)S(1)} %join.3.line_ref, f32[32,256]{1,0:T(8,128)S(1)} %collective-permute-done.8.more_ref, s32[8,128]{1,0:T(8,128)S(1)} %get-tuple-element.28.info_ref, ...), custom_call_target="tpu_custom_call" | custom-call | flops 6600000000 | tf_op jit(solution)/shard_map/stress_terms/pallas_call | solution.py:251
  62.0 0.9 collective-permute-start.9
  62.9 3.2 %collective-permute-done.9.received_ref = f32[32,256]{1,0:T(8,128)S(1)} collective-permute-done((f32[32,256]{1,0:T(8,128)S(1)}, f32[32,256]{1,0:T(8,128)S(1)}, u32[]{:S(2)}, u32[]{:S(2)}) %collective-permute-start.9) | collective-permute-done | bytes 32800 | tf_op jit(solution)/shard_map/ppermute | solution.py:273
  66.1 0.3 collective-permute-start.10
  66.3 4.0 %all-to-all-start.3 = ((bf16[16,8,256]{2,1,0:T(8,128)(2,1)}), bf16[16,8,256]{2,1,0:T(8,128)(2,1)S(1)}, u32[]{:S(2)}, u32[]{:S(2)}) async-start(bf16[16,8,256]{2,1,0:T(8,128)(2,1)} %bitcast.7), calls=%async_computation.3 | async-start | bytes 131072 | tf_op jit(solution)/shard_map/all_to_all | solution.py:304
  70.3 0.0 collective-permute-done.10.received_ref
  70.4 3.6 %collective-permute-start.11 = (f32[8,256]{1,0:T(8,128)S(1)}, f32[8,256]{1,0:T(8,128)S(1)}, u32[]{:S(2)}, u32[]{:S(2)}) collective-permute-start(f32[8,256]{1,0:T(8,128)S(1)} %get-tuple-element.46), channel_id=1, source_target_pairs={{0,16},{16,0},{32,48},{48,32},{64,80},{80,64},{96,112},{112,96},{1... | collective-permute-start | bytes 24584 | tf_op jit(solution)/shard_map/ppermute | solution.py:273
  73.9 0.2 near_terms.3.refs_0_
  74.2 0.6 collective-permute-done.11.refs_3_
  74.8 2.1 %all-to-all-done.3.refs_1_ = bf16[16,8,256]{2,1,0:T(8,128)(2,1)S(1)} async-done(((bf16[16,8,256]{2,1,0:T(8,128)(2,1)}), bf16[16,8,256]{2,1,0:T(8,128)(2,1)S(1)}, u32[]{:S(2)}, u32[]{:S(2)}) %all-to-all-start.3) | async-done | bytes 65568 | tf_op jit(solution)/shard_map/all_to_all | solution.py:304
  76.9 0.8 last_step.1
  77.6 9.4 %all-to-all-start.4 = ((f32[128,1,128]{2,1,0:T(1,128)}), f32[128,1,128]{2,1,0:T(1,128)S(1)}, u32[]{:S(2)}, u32[]{:S(2)}) async-start(f32[128,1,128]{2,1,0:T(1,128)} %bitcast.9), calls=%async_computation.4 | async-start | bytes 131072 | tf_op jit(solution)/shard_map/all_to_all | solution.py:311
  87.0 0.9 from_order.1
  88.0 8.9 %all-to-all-done.4 = f32[128,1,128]{2,1,0:T(1,128)S(1)} async-done(((f32[128,1,128]{2,1,0:T(1,128)}), f32[128,1,128]{2,1,0:T(1,128)S(1)}, u32[]{:S(2)}, u32[]{:S(2)}) %all-to-all-start.4) | async-done | bytes 65568 | tf_op jit(solution)/shard_map/all_to_all | solution.py:311
  96.8 0.6 slice_reduce_fusion
  (7 shorter events, 0.1 us)
Async XLA Ops:
  0.6 5.3 %copy-start.5 = (s32[128,2]{0,1:T(2,128)S(1)}, s32[128,2]{0,1:T(2,128)}, u32[]{:S(2)}) copy-start(s32[128,2]{0,1:T(2,128)} %param.13) | copy-start | bytes 3076
  0.6 15.0 %copy-start.4 = (s32[128]{0:T(128)S(1)}, s32[128]{0:T(128)}, u32[]{:S(2)}) copy-start(s32[128]{0:T(128)} %param.14) | copy-start | bytes 1540
  1.6 2.3 %collective-permute-start = (f32[8,256]{1,0:T(8,128)S(1)}, f32[8,256]{1,0:T(8,128)S(1)}, u32[]{:S(2)}, u32[]{:S(2)}) collective-permute-start(f32[8,256]{1,0:T(8,128)S(1)} %first_deficit.1.own_ref.held_ref), channel_id=1, source_target_pairs={{0,16},{16,0},{32,48},{48,32},{64,80},{80,64},{96,112},{112,96},{1... | collective-permute-start | bytes 24584 | tf_op jit(solution)/shard_map/ppermute | solution.py:273
  4.6 9.1 %collective-permute-start.1 = (f32[16,256]{1,0:T(8,128)S(1)}, f32[16,256]{1,0:T(8,128)S(1)}, u32[]{:S(2)}, u32[]{:S(2)}) collective-permute-start(f32[16,256]{1,0:T(8,128)S(1)} %get-tuple-element.27.held_ref), channel_id=1, source_target_pairs={{0,32},{16,48},{32,0},{48,16},{64,96},{80,112},{96,64},{112,80},{1... | collective-permute-start | bytes 49160 | tf_op jit(solution)/shard_map/ppermute | solution.py:273
  6.1 14.1 %all-to-all-start = ((bf16[16,8,256]{2,1,0:T(8,128)(2,1)}), bf16[16,8,256]{2,1,0:T(8,128)(2,1)S(1)}, u32[]{:S(2)}, u32[]{:S(2)}) async-start(bf16[16,8,256]{2,1,0:T(8,128)(2,1)} %get-tuple-element.26), calls=%async_computation | async-start | bytes 131072 | tf_op jit(solution)/shard_map/all_to_all | solution.py:297
  13.7 4.1 %collective-permute-start.2 = (f32[32,256]{1,0:T(8,128)S(1)}, f32[32,256]{1,0:T(8,128)S(1)}, u32[]{:S(2)}, u32[]{:S(2)}) collective-permute-start(f32[32,256]{1,0:T(8,128)S(1)} %join.2.line_ref), channel_id=1, source_target_pairs={{0,96},{16,112},{32,64},{48,80},{64,32},{80,48},{96,0},{112,16},{1... | collective-permute-start | bytes 98312 | tf_op jit(solution)/shard_map/ppermute | solution.py:273
  20.2 12.7 %copy-start.1 = (f32[3,2048]{1,0:T(4,128)S(1)}, f32[3,2048]{1,0:T(4,128)}, u32[]{:S(2)}) copy-start(f32[3,2048]{1,0:T(4,128)} %friction_ref.1) | copy-start | bytes 73732
  20.2 12.7 %copy-start.2 = (f32[2,2048]{1,0:T(2,128)S(1)}, f32[2,2048]{1,0:T(2,128)}, u32[]{:S(2)}) copy-start(f32[2,2048]{1,0:T(2,128)} %state_ref.3) | copy-start | bytes 49156
  20.2 12.7 %copy-start.3 = (s32[2048]{0:T(1024)S(1)}, s32[2048]{0:T(1024)}, u32[]{:S(2)}) copy-start(s32[2048]{0:T(1024)} %param.15) | copy-start | bytes 24580
  20.2 19.3 %copy-start = (bf16[8,256,256]{2,1,0:T(8,128)(2,1)S(1)}, bf16[8,256,256]{2,1,0:T(8,128)(2,1)}, u32[]{:S(2)}) copy-start(bf16[8,256,256]{2,1,0:T(8,128)(2,1)} %near.3) | copy-start | bytes 3145732
  26.6 6.2 %collective-permute-start.3 = (f32[32,256]{1,0:T(8,128)S(1)}, f32[32,256]{1,0:T(8,128)S(1)}, u32[]{:S(2)}, u32[]{:S(2)}) collective-permute-start(f32[32,256]{1,0:T(8,128)S(1)} %get-tuple-element.32), channel_id=1, source_target_pairs={{0,96},{16,112},{32,64},{48,80},{64,32},{80,48},{96,0},{112,16},{1... | collective-permute-start | bytes 98312 | tf_op jit(solution)/shard_map/ppermute | solution.py:273
  28.6 11.8 %all-to-all-start.1 = ((bf16[16,8,256]{2,1,0:T(8,128)(2,1)}), bf16[16,8,256]{2,1,0:T(8,128)(2,1)S(1)}, u32[]{:S(2)}, u32[]{:S(2)}) async-start(bf16[16,8,256]{2,1,0:T(8,128)(2,1)} %bitcast.5), calls=%async_computation.1 | async-start | bytes 131072 | tf_op jit(solution)/shard_map/all_to_all | solution.py:304
  32.8 2.7 %collective-permute-start.4 = (f32[16,256]{1,0:T(8,128)S(1)}, f32[16,256]{1,0:T(8,128)S(1)}, u32[]{:S(2)}, u32[]{:S(2)}) collective-permute-start(f32[16,256]{1,0:T(8,128)S(1)} %get-tuple-element.34), channel_id=1, source_target_pairs={{0,32},{16,48},{32,0},{48,16},{64,96},{80,112},{96,64},{112,80},{1... | collective-permute-start | bytes 49160 | tf_op jit(solution)/shard_map/ppermute | solution.py:273
  35.5 4.9 %collective-permute-start.5 = (f32[8,256]{1,0:T(8,128)S(1)}, f32[8,256]{1,0:T(8,128)S(1)}, u32[]{:S(2)}, u32[]{:S(2)}) collective-permute-start(f32[8,256]{1,0:T(8,128)S(1)} %get-tuple-element.36), channel_id=1, source_target_pairs={{0,16},{16,0},{32,48},{48,32},{64,80},{80,64},{96,112},{112,96},{1... | collective-permute-start | bytes 24584 | tf_op jit(solution)/shard_map/ppermute | solution.py:273
  40.4 3.9 %collective-permute-start.6 = (f32[8,256]{1,0:T(8,128)S(1)}, f32[8,256]{1,0:T(8,128)S(1)}, u32[]{:S(2)}, u32[]{:S(2)}) collective-permute-start(f32[8,256]{1,0:T(8,128)S(1)} %get-tuple-element.37.own_ref.held_ref), channel_id=1, source_target_pairs={{0,16},{16,0},{32,48},{48,32},{64,80},{80,64},{96,112},{112,96},{1... | collective-permute-start | bytes 24584 | tf_op jit(solution)/shard_map/ppermute | solution.py:273
  44.9 4.3 %collective-permute-start.7 = (f32[16,256]{1,0:T(8,128)S(1)}, f32[16,256]{1,0:T(8,128)S(1)}, u32[]{:S(2)}, u32[]{:S(2)}) collective-permute-start(f32[16,256]{1,0:T(8,128)S(1)} %get-tuple-element.39.held_ref), channel_id=1, source_target_pairs={{0,32},{16,48},{32,0},{48,16},{64,96},{80,112},{96,64},{112,80},{1... | collective-permute-start | bytes 49160 | tf_op jit(solution)/shard_map/ppermute | solution.py:273
  44.9 10.8 %all-to-all-start.2 = ((bf16[16,8,256]{2,1,0:T(8,128)(2,1)}), bf16[16,8,256]{2,1,0:T(8,128)(2,1)S(1)}, u32[]{:S(2)}, u32[]{:S(2)}) async-start(bf16[16,8,256]{2,1,0:T(8,128)(2,1)} %get-tuple-element.38), calls=%async_computation.2 | async-start | bytes 131072 | tf_op jit(solution)/shard_map/all_to_all | solution.py:297
  49.3 4.1 %collective-permute-start.8 = (f32[32,256]{1,0:T(8,128)S(1)}, f32[32,256]{1,0:T(8,128)S(1)}, u32[]{:S(2)}, u32[]{:S(2)}) collective-permute-start(f32[32,256]{1,0:T(8,128)S(1)} %join.3.line_ref), channel_id=1, source_target_pairs={{0,96},{16,112},{32,64},{48,80},{64,32},{80,48},{96,0},{112,16},{1... | collective-permute-start | bytes 98312 | tf_op jit(solution)/shard_map/ppermute | solution.py:273
  62.0 4.1 %collective-permute-start.9 = (f32[32,256]{1,0:T(8,128)S(1)}, f32[32,256]{1,0:T(8,128)S(1)}, u32[]{:S(2)}, u32[]{:S(2)}) collective-permute-start(f32[32,256]{1,0:T(8,128)S(1)} %get-tuple-element.42), channel_id=1, source_target_pairs={{0,96},{16,112},{32,64},{48,80},{64,32},{80,48},{96,0},{112,16},{1... | collective-permute-start | bytes 98312 | tf_op jit(solution)/shard_map/ppermute | solution.py:273
  66.1 4.3 %collective-permute-start.10 = (f32[16,256]{1,0:T(8,128)S(1)}, f32[16,256]{1,0:T(8,128)S(1)}, u32[]{:S(2)}, u32[]{:S(2)}) collective-permute-start(f32[16,256]{1,0:T(8,128)S(1)} %get-tuple-element.44), channel_id=1, source_target_pairs={{0,32},{16,48},{32,0},{48,16},{64,96},{80,112},{96,64},{112,80},{1... | collective-permute-start | bytes 49160 | tf_op jit(solution)/shard_map/ppermute | solution.py:273
  66.3 10.5 %all-to-all-start.3 = ((bf16[16,8,256]{2,1,0:T(8,128)(2,1)}), bf16[16,8,256]{2,1,0:T(8,128)(2,1)S(1)}, u32[]{:S(2)}, u32[]{:S(2)}) async-start(bf16[16,8,256]{2,1,0:T(8,128)(2,1)} %bitcast.7), calls=%async_computation.3 | async-start | bytes 131072 | tf_op jit(solution)/shard_map/all_to_all | solution.py:304
  70.4 4.4 %collective-permute-start.11 = (f32[8,256]{1,0:T(8,128)S(1)}, f32[8,256]{1,0:T(8,128)S(1)}, u32[]{:S(2)}, u32[]{:S(2)}) collective-permute-start(f32[8,256]{1,0:T(8,128)S(1)} %get-tuple-element.46), channel_id=1, source_target_pairs={{0,16},{16,0},{32,48},{48,32},{64,80},{80,64},{96,112},{112,96},{1... | collective-permute-start | bytes 24584 | tf_op jit(solution)/shard_map/ppermute | solution.py:273
  77.6 19.2 %all-to-all-start.4 = ((f32[128,1,128]{2,1,0:T(1,128)}), f32[128,1,128]{2,1,0:T(1,128)S(1)}, u32[]{:S(2)}, u32[]{:S(2)}) async-start(f32[128,1,128]{2,1,0:T(1,128)} %bitcast.9), calls=%async_computation.4 | async-start | bytes 131072 | tf_op jit(solution)/shard_map/all_to_all | solution.py:311

commit v3 on v2

--- a/solution.py
+++ b/solution.py
@@ -79,15 +79,15 @@
         fields_ref[k] = to_clusters(jnp.sum(picked, axis=0, keepdims=True), cluster)
 
 
-def from_order(new_ref, perm_ref, out_ref):
-    tiles = perm_ref.shape[1] // LANES
-    at_tile, at_lane = place(perm_ref[...], tiles)
+def from_order(fields, perm_row, out_ref):
+    tiles = perm_row.shape[1] // LANES
+    at_tile, at_lane = place(perm_row, tiles)
     parts = []
-    for k in range(2):
-        row = to_row_of_clusters(new_ref[k])
+    for field in fields:
+        row = to_row_of_clusters(field)
         parts += [jnp.where(at_tile, part.astype(f32), 0.0).astype(bf16) for part in split3(row)]
     moved = mxu_nt(jnp.concatenate(parts, axis=0), at_lane)
-    for k in range(2):
+    for k in range(len(fields)):
         three = [moved[(3 * k + s) * tiles:(3 * k + s + 1) * tiles] for s in range(3)]
         out_ref[k:k + 1, :] = to_row((three[0] + three[1]) + three[2])
 
@@ -111,41 +111,49 @@
     return mxu(hot, values).astype(bf16)
 
 
-def stress_terms(chunk, everyone_ref, line_ref, more_ref, info_ref, col_ref, left_hbm, right_hbm, first_ref, kept_ref,
-                 sent_ref, left, right, sem):
-    pairs = info_ref.shape[1]
-    width = left.shape[0] // pairs
-    chunks = left.shape[0] // chunk
-
-    def fetch(k):
-        part = pl.ds(k * chunk, chunk)
-        return (
-            pltpu.make_async_copy(right_hbm.at[part], right.at[part], sem.at[0, k]),
-            pltpu.make_async_copy(left_hbm.at[part], left.at[part], sem.at[1, k]),
-        )
-
-    for k in range(chunks):
-        for copy in fetch(k):
-            copy.start()
-    line = jnp.concatenate([line_ref[...], more_ref[...]], axis=0).astype(bf16)
-    x_first = picked(col_ref[:, 0:1], everyone_ref[...])
-    x_second = picked(col_ref[:, 1:2], line)
+def pair_terms(at, ranks, values, taken, given, wait=lambda row: None):
+    pairs = at.shape[0]
+    width = taken.shape[0] // pairs
+    x = picked(at, values)
     shape = (PAIRS, PAIRS * width)
     rank = lax.broadcasted_iota(jnp.int32, shape, 1) - width * lax.broadcasted_iota(jnp.int32, shape, 0)
-    to_first, to_second = [], []
+    terms = []
     for k in range(pairs // PAIRS):
-        if k * shape[1] % chunk == 0:
-            for copy in fetch(k * shape[1] // chunk):
-                copy.wait()
+        wait(k * shape[1])
         rows = slice(k * PAIRS, (k + 1) * PAIRS)
         part = pl.ds(k * shape[1], shape[1])
-        within = (rank >= 0) & (rank < col_ref[rows, 2:3])
-        coef_j = jnp.where(within, mxu_nt(x_second[rows], right[part]), 0.0).astype(bf16)
-        coef_i = jnp.where(within, mxu_nt(x_first[rows], left[part]), 0.0).astype(bf16)
-        to_first.append(mxu(coef_j, left[part]))
-        to_second.append(mxu(coef_i, right[part]))
-    first_ref[...] = sums_at(info_ref, 0, first_ref.shape[0], jnp.concatenate(to_first, axis=0)).astype(bf16)
-    halves(sums_at(info_ref, 1, 2 * kept_ref.shape[0], jnp.concatenate(to_second, axis=0)), kept_ref, sent_ref)
+        within = (rank >= 0) & (rank < ranks[rows])
+        coef = jnp.where(within, mxu_nt(x[rows], taken[part]), 0.0).astype(bf16)
+        terms.append(mxu(coef, given[part]))
+    return jnp.concatenate(terms, axis=0)
+
+
+def terms_to_second(chunk, everyone_ref, near_0_ref, near_1_ref, info_ref, col_ref, left_hbm, right_hbm, kept_ref, sent_ref,
+                    left, right, sem):
+    copies = []
+    for k in range(left.shape[0] // chunk):
+        part = pl.ds(k * chunk, chunk)
+        copies.append((pltpu.make_async_copy(left_hbm.at[part], left.at[part], sem.at[0, k]),
+                       pltpu.make_async_copy(right_hbm.at[part], right.at[part], sem.at[1, k])))
+        for copy in copies[k]:
+            copy.start()
+
+    def wait(row):
+        if row % chunk == 0:
+            for copy in copies[row // chunk]:
+                copy.wait()
+
+    terms = pair_terms(col_ref[:, 0:1], col_ref[:, 2:3], everyone_ref[...], left, right, wait)
+    halves(sums_at(info_ref, 1, 2 * kept_ref.shape[0], terms), kept_ref, sent_ref)
+    half = near_0_ref.shape[0]
+    kept_ref[0:half, :] += near_0_ref[...]
+    kept_ref[half:2 * half, :] += near_1_ref[...]
+
+
+def terms_to_first(line_ref, more_ref, info_ref, col_ref, left, right, first_ref):
+    line = jnp.concatenate([line_ref[...], more_ref[...]], axis=0).astype(bf16)
+    terms = pair_terms(col_ref[:, 1:2], col_ref[:, 2:3], line, right, left)
+    first_ref[...] = sums_at(info_ref, 0, first_ref.shape[0], terms).astype(bf16)
 
 
 def sums_at(info_ref, side, rows, terms):
@@ -163,18 +171,27 @@
     out_ref[...] = jnp.concatenate([held_ref[...], received_ref[...]], axis=0)
 
 
-def join_and_spread(held_ref, received_ref, out_ref, copies_ref):
-    join(held_ref, received_ref, out_ref)
+def spread(own_ref, copies_ref):
+    value = own_ref[...].astype(bf16)
     for k in range(copies_ref.shape[0]):
-        copies_ref[k] = held_ref[...].astype(bf16)
+        copies_ref[k] = value
 
 
 def add(held_ref, received_ref, *out_refs):
     halves(held_ref[...] + received_ref[...], *out_refs)
 
 
+HOPS = (1, 3, 7)
+
+
 def place_of(difference):
-    return difference ^ ((difference >> 1) & 1)
+    place = jnp.zeros_like(difference)
+    for k in range(2 ** len(HOPS)):
+        reached = 0
+        for bit, hop in enumerate(HOPS):
+            reached ^= hop * (k >> bit & 1)
+        place = jnp.where(difference == reached, k, place)
+    return place
 
 
 def pair_info(own_count, columns, pairs_ref, ranks_ref, info_ref, col_ref):
@@ -184,7 +201,7 @@
     owner_row = lax.div(owner, columns)
     by_row = owner_row ^ row
     first_at = (owner - owner_row * columns) * own_count + inside
-    second_at = ((by_row & 1) + 2 * place_of(by_row >> 1)) * own_count + inside
+    second_at = place_of(by_row) * own_count + inside
     count = ranks_ref.shape[1]
     sublane = lax.broadcasted_iota(jnp.int32, (count, LANES), 0)
     lane = lax.broadcasted_iota(jnp.int32, (count, LANES), 1)
@@ -194,14 +211,21 @@
     info_ref[...] = jnp.transpose(columns_of)[:info_ref.shape[0]]
 
 
-def near_terms(own_ref, near, out_ref):
+def near_terms(which, own_ref, near, out_ref):
     own = own_ref[...]
-    row_own = lax.broadcasted_iota(jnp.int32, own.shape, 0)
+    half = own.shape[0] // 2
+    row_own = lax.broadcasted_iota(jnp.int32, (half, own.shape[1]), 0)
     mine = own.astype(bf16)
-    total = jnp.zeros(own.shape, f32)
-    for k in range(own.shape[0]):
-        total += jnp.where(row_own == k, mxu(mine, near[k]), 0.0)
+    total = jnp.zeros(row_own.shape, f32)
+    for k in range(half):
+        product = mxu(mine, near[which * half + k])[which * half:(which + 1) * half]
+        total += jnp.where(row_own == k, product, 0.0)
     out_ref[...] = total
+
+
+def prepare(own_count, columns, pairs_ref, ranks_ref, state_ref, friction_ref, perm_ref, info_ref, col_ref, fields_ref):
+    pair_info(own_count, columns, pairs_ref, ranks_ref, info_ref, col_ref)
+    to_order(state_ref, friction_ref, perm_ref, fields_ref)
 
 
 def slopes(lv, lt, a_sigma, b_sigma, stress):
@@ -211,11 +235,11 @@
 
 
 def total_stress(refs):
-    near_ref, from_first_ref, kept_ref, received_ref = refs
+    from_first_ref, kept_ref, received_ref = refs
     parts = [from_first_ref[k].astype(f32) for k in range(from_first_ref.shape[0])]
     while len(parts) > 1:
         parts = [parts[k] + parts[k + 1] for k in range(0, len(parts), 2)]
-    return (near_ref[...] + parts[0]) + (kept_ref[...] + received_ref[...])
+    return parts[0] + (kept_ref[...] + received_ref[...])
 
 
 def half_step(*refs):
@@ -228,17 +252,19 @@
 
 
 def last_step(*refs):
-    *stress_refs, fields_ref, slope_ref, new_ref, sum_ref = refs
+    *stress_refs, fields_ref, slope_ref, perm_ref, out_ref, sum_ref = refs
     lv, lt, a_sigma, b_sigma = (fields_ref[k] for k in range(4))
     first = (slope_ref[0], slope_ref[1])
     second = slopes(lv + step_size * first[0], lt + step_size * first[1], a_sigma, b_sigma, total_stress(stress_refs))
     squares = jnp.zeros(lv.shape, f32)
+    news = []
     for k, base in enumerate((lv, lt)):
         new = base + 0.5 * step_size * (first[k] + second[k])
-        new_ref[k] = new
+        news.append(new)
         scaled = 0.5 * step_size * (second[k] - first[k]) / (abs_tol + rel_tol * jnp.abs(new))
         squares += scaled * scaled
     sum_ref[...] = jnp.full(sum_ref.shape, jnp.sum(squares), f32)
+    from_order(news, perm_ref[...], out_ref)
 
 
 def in_hbm(x):
@@ -273,11 +299,10 @@
         return lax.ppermute(x, axis, [(r, r ^ distance) for r in range(size)])
 
     own = call(first_deficit, block, [in_hbm(state), in_hbm(perm_row)], 6)
-    fields = call(to_order, sds((4, own_count, cluster), f32), [state, friction, perm_row], 0.5)
-
-    info, info_col = call(
-        functools.partial(pair_info, own_count, columns),
-        [sds((8, count), jnp.int32), sds((count, LANES), jnp.int32)], [pairs, ranks.reshape(1, -1)], 0.5)
+    info, info_col, fields = call(
+        functools.partial(prepare, own_count, columns),
+        [sds((8, count), jnp.int32), sds((count, LANES), jnp.int32), sds((4, own_count, cluster), f32)],
+        [pairs, ranks.reshape(1, -1), state, friction, perm_row], 0.7)
     near = near_blocks
     left = in_hbm(left_factor.reshape(count * width, cluster))
     right = in_hbm(right_factor.reshape(count * width, cluster))
@@ -286,30 +311,31 @@
         return sds((blocks * own_count, cluster), dtype)
 
     chunk = 2048
-    scratch = [pltpu.VMEM(left.shape, bf16), pltpu.VMEM(right.shape, bf16),
-               pltpu.SemaphoreType.DMA((2, count * width // chunk))]
+    scratch = [pltpu.SemaphoreType.DMA((2, count * width // chunk))]
+    loaded = [pltpu.VMEM(x.shape, bf16) for x in (left, right)]
 
     def exchange(own):
-        two, copies = call(join_and_spread, [block_of(2, f32), sds((columns, own_count, cluster), bf16)],
-                           [own, swap(own, "row", 1)], 0.2)
-        four = call(join, block_of(4, f32), [two, swap(two, "row", 2)], 0.2)
-        more = swap(four, "row", 6)
+        copies = call(spread, sds((columns, own_count, cluster), bf16), [own], 0.6)
+        two = call(join, block_of(2, f32), [own, swap(own, "row", HOPS[0])], 0.1)
+        four = call(join, block_of(4, f32), [two, swap(two, "row", HOPS[1])], 0.1)
+        more = swap(four, "row", HOPS[2])
         everyone = lax.all_to_all(copies, "col", 0, 0).reshape(span, cluster)
-        near_term = call(near_terms, block, [own, near], 0.3)
-        first, kept, sent = call(
-            functools.partial(stress_terms, chunk), [block_of(columns, bf16)] + [block_of(4, f32)] * 2,
-            [everyone, four, more, info, info_col, left, right], 6, scratch, (left, right))
-        for blocks, hop in ((2, 6), (1, 2)):
-            kept, sent = call(add, [block_of(blocks, f32)] * 2, [kept, swap(sent, "row", hop)], 0.2)
+        near_term = [call(functools.partial(near_terms, k), sds((own_count // 2, cluster), f32), [own, near], 0.3)
+                     for k in range(2)]
+        kept, sent, *factors = call(
+            functools.partial(terms_to_second, chunk), [block_of(4, f32)] * 2 + loaded,
+            [everyone, *near_term, info, info_col, left, right], 5, scratch, (left, right))
+        first = call(terms_to_first, block_of(columns, bf16), [four, more, info, info_col, *factors], 2.5)
+        for blocks, hop in ((2, HOPS[2]), (1, HOPS[1])):
+            kept, sent = call(add, [block_of(blocks, f32)] * 2, [kept, swap(sent, "row", hop)], 0.1)
         from_first = lax.all_to_all(first.reshape(columns, own_count, cluster), "col", 0, 0)
-        return [near_term, from_first, kept, swap(sent, "row", 1)]
+        return [from_first, kept, swap(sent, "row", HOPS[0])]
 
     slope, own = call(half_step, [sds((2, own_count, cluster), f32), block], [*exchange(own), fields], 0.1)
     devices = rows * columns
-    new, squares = call(last_step, [sds((2, own_count, cluster), f32), sds((devices, LANES), f32)],
-                        [*exchange(own), fields, slope], 0.8)
+    new_state, squares = call(last_step, [sds(state.shape, f32), sds((devices, LANES), f32)],
+                              [*exchange(own), fields, slope, perm_row], 1.3)
     everywhere = lax.all_to_all(squares, ("row", "col"), 0, 0, tiled=True)
-    new_state = call(from_order, sds(state.shape, f32), [new, perm_row], 0.9)
     entries = 2.0 * state.shape[1] * devices
     return new_state, jnp.sqrt(jnp.sum(everywhere[:, 0]) / entries)
 

time: 99.7 us -> 94.4 us (0.947)
  blocking collectives: 0 us -> 16.7 us
  waiting for transfers between devices: 29 us -> 16.1 us
  starting transfers between devices: 49.1 us -> 38.5 us
  Pallas kernels: 17.8 us -> 19.2 us
    all_to_all x0 -> x1, blocking collectives: none -> 16.7 us  [shards(): everywhere = lax.all_to_all(squares, ('row', 'col'), 0, 0, tiled=True)]
    all_to_all x1 -> x0, starting transfers between devices: 9.38 us -> none  [shards(): everywhere = lax.all_to_all(squares, ('row', 'col'), 0, 0, tiled=True)]
    all_to_all x1 -> x0, waiting for transfers between devices: 8.85 us -> none  [shards(): everywhere = lax.all_to_all(squares, ('row', 'col'), 0, 0, tiled=True)]
    all_to_all x2, waiting for transfers between devices: 4.89 us -> 0.01 us  [exchange(): everyone = lax.all_to_all(copies, 'col', 0, 0).reshape(span, cluster)]
    all_to_all x2, waiting for transfers between devices: 2.1 us -> 3.77 us  [exchange(): lax.all_to_all(first.reshape(columns, own_count, cluster), 'col', 0, 0)]
    pallas_call x18 -> x22, Pallas kernels: 17.8 us -> 19.2 us  [call(): pl.pallas_call(kernel, out_shape=out_shape, in_specs=[pl.BlockSpec(memory...]
    all_to_all x2, starting transfers between devices: 8.2 us -> 6.99 us  [exchange(): lax.all_to_all(first.reshape(columns, own_count, cluster), 'col', 0, 0)]
  transfers between devices with their start and end apart: 17 -> 16, of which waited for: 12 -> 8; matrix products, arithmetic and copies ran while one was open for 0% -> 0% of each run, Pallas kernels for 2% -> 18%
where the time goes in v3:
time: 94.4 us; the launch traced here: 93.9 us
  starting transfers between devices  38.5 us (41%)
  Pallas kernels  19.2 us (20%)
  blocking collectives  16.7 us (18%)
  waiting for transfers between devices  16.1 us (17%)
  between operations  2.68 us (3%)
    ppermute x12, starting transfers between devices, swap(): return lax.ppermute(x, axis, [(r, r ^ distance) for r in range(size)])  20.1 us
    pallas_call x22, Pallas kernels, call(): pl.pallas_call(kernel, out_shape=out_shape, in_specs=[pl.BlockSpec(memory...  19.2 us
    all_to_all x1, blocking collectives, shards(): everywhere = lax.all_to_all(squares, ('row', 'col'), 0, 0, tiled=True)  16.7 us
    ppermute x12, waiting for transfers between devices, swap(): return lax.ppermute(x, axis, [(r, r ^ distance) for r in range(size)])  12.4 us
    all_to_all x2, starting transfers between devices, exchange(): everyone = lax.all_to_all(copies, 'col', 0, 0).reshape(span, cluster)  11.4 us
    all_to_all x2, starting transfers between devices, exchange(): lax.all_to_all(first.reshape(columns, own_count, cluster), 'col', 0, 0)  6.99 us
    all_to_all x2, waiting for transfers between devices, exchange(): lax.all_to_all(first.reshape(columns, own_count, cluster), 'col', 0, 0)  3.77 us
  transfers between devices with their start and end apart: 16, of which 8 were waited for; matrix products, arithmetic and copies ran while one was open for 0% of the time, Pallas kernels for 18%

profile of v3, /device:TPU:1, one launch (start us, length us, event | category | flops | bytes accessed | tf_op | source)
XLA Modules:
  0.0 93.9 jit_solution(5837990988492987073)
XLA Ops:
  0.6 0.0 copy-start.5
  0.6 0.0 copy-start.1
  0.7 0.0 copy-start.2
  0.7 0.0 copy-start.3
  0.7 0.0 copy-start.4
  0.7 1.0 %first_deficit.1.held_ref.own_ref = f32[8,256]{1,0:T(8,128)S(1)} custom-call(f32[2,2048]{1,0:T(2,128)} %state_ref.3, s32[1,2048]{1,0:T(1,128)} %bitcast.15), custom_call_target="tpu_custom_call" | custom-call | flops 6600000000 | tf_op jit(solution)/shard_map/first_deficit/pallas_call | solution.py:277
  1.7 0.0 copy-start
  1.7 1.5 %collective-permute-start = (f32[8,256]{1,0:T(8,128)S(1)}, f32[8,256]{1,0:T(8,128)S(1)}, u32[]{:S(2)}, u32[]{:S(2)}) collective-permute-start(f32[8,256]{1,0:T(8,128)S(1)} %first_deficit.1.held_ref.own_ref), channel_id=1, source_target_pairs={{0,16},{16,0},{32,48},{48,32},{64,80},{80,64},{96,112},{112,96},{1... | collective-permute-start | bytes 24584 | tf_op jit(solution)/shard_map/ppermute | solution.py:299
  3.2 0.6 spread.2
  3.8 7.7 %all-to-all-start = ((bf16[16,8,256]{2,1,0:T(8,128)(2,1)}), bf16[16,8,256]{2,1,0:T(8,128)(2,1)S(1)}, u32[]{:S(2)}, u32[]{:S(2)}) async-start(bf16[16,8,256]{2,1,0:T(8,128)(2,1)} %spread.2), calls=%async_computation | async-start | bytes 131072 | tf_op jit(solution)/shard_map/all_to_all | solution.py:322
  11.5 0.0 copy-done.5
  11.5 0.1 copy.11.pairs_ref
  11.6 0.0 copy-done.1
  11.6 0.0 copy-done.2
  11.6 0.0 copy-done.3
  11.6 0.0 copy-done.4
  11.7 0.5 prepare.1
  12.2 0.0 copy-done
  12.2 0.2 near_terms.4.near_0_ref
  12.4 0.0 collective-permute-done.received_ref
  12.4 1.6 %collective-permute-start.1 = (f32[16,256]{1,0:T(8,128)S(1)}, f32[16,256]{1,0:T(8,128)S(1)}, u32[]{:S(2)}, u32[]{:S(2)}) collective-permute-start(f32[16,256]{1,0:T(8,128)S(1)} %join.4.held_ref), channel_id=1, source_target_pairs={{0,48},{16,32},{32,16},{48,0},{64,112},{80,96},{96,80},{112,64},{1... | collective-permute-start | bytes 49160 | tf_op jit(solution)/shard_map/ppermute | solution.py:299
  14.0 0.2 near_terms.5.near_1_ref
  14.1 1.8 %collective-permute-done.1.received_ref = f32[16,256]{1,0:T(8,128)S(1)} collective-permute-done((f32[16,256]{1,0:T(8,128)S(1)}, f32[16,256]{1,0:T(8,128)S(1)}, u32[]{:S(2)}, u32[]{:S(2)}) %collective-permute-start.1) | collective-permute-done | bytes 16416 | tf_op jit(solution)/shard_map/ppermute | solution.py:299
  15.9 2.6 %collective-permute-start.2 = (f32[32,256]{1,0:T(8,128)S(1)}, f32[32,256]{1,0:T(8,128)S(1)}, u32[]{:S(2)}, u32[]{:S(2)}) collective-permute-start(f32[32,256]{1,0:T(8,128)S(1)} %join.5.line_ref), channel_id=1, source_target_pairs={{0,112},{16,96},{32,80},{48,64},{64,48},{80,32},{96,16},{112,0},{1... | collective-permute-start | bytes 98312 | tf_op jit(solution)/shard_map/ppermute | solution.py:299
  18.6 0.0 all-to-all-done
  18.6 4.4 %terms_to_second.2 = (f32[32,256]{1,0:T(8,128)S(1)}, f32[32,256]{1,0:T(8,128)S(1)}, bf16[8192,256]{1,0:T(8,128)(2,1)S(1)}, bf16[8192,256]{1,0:T(8,128)(2,1)S(1)}) custom-call(bf16[128,256]{1,0:T(8,128)(2,1)S(1)} %bitcast.12, f32[4,256]{1,0:T(4,128)S(1)} %near_terms.4.near_0_ref, f32[4,256]{1,0:T(4,128)S(1)} %near_terms.5.near_1_ref, ...), custom_call_target="tpu_custom_call" | custom-call | flops 5500000256 | tf_op jit(solution)/shard_map/terms_to_second/pallas_call | solution.py:277
  23.0 3.6 %collective-permute-start.3 = (f32[32,256]{1,0:T(8,128)S(1)}, f32[32,256]{1,0:T(8,128)S(1)}, u32[]{:S(2)}, u32[]{:S(2)}) collective-permute-start(f32[32,256]{1,0:T(8,128)S(1)} %get-tuple-element.30), channel_id=1, source_target_pairs={{0,112},{16,96},{32,80},{48,64},{64,48},{80,32},{96,16},{112,0},{1... | collective-permute-start | bytes 98312 | tf_op jit(solution)/shard_map/ppermute | solution.py:299
  26.6 0.0 collective-permute-done.2.more_ref
  26.6 2.9 %terms_to_first.2 = bf16[128,256]{1,0:T(8,128)(2,1)} custom-call(f32[32,256]{1,0:T(8,128)S(1)} %join.5.line_ref, f32[32,256]{1,0:T(8,128)S(1)} %collective-permute-done.2.more_ref, s32[8,128]{1,0:T(8,128)S(1)} %get-tuple-element.25.info_ref, s32[128,128]{1,0:T(8,128)S(1)} %get-tuple-element.26.col_ref, bf16[8192,256]{1,0:T(8,128)(2,1)S(1)} %get-tuple-element.27.left, ...), custom_call_target="tpu_custom_call" | custom-call | flops 2750000128 | tf_op jit(solution)/shard_map/terms_to_first/pallas_call | solution.py:277
  29.5 3.5 %all-to-all-start.1 = ((bf16[16,8,256]{2,1,0:T(8,128)(2,1)}), bf16[16,8,256]{2,1,0:T(8,128)(2,1)S(1)}, u32[]{:S(2)}, u32[]{:S(2)}) async-start(bf16[16,8,256]{2,1,0:T(8,128)(2,1)} %bitcast.5), calls=%async_computation.1 | async-start | bytes 131072 | tf_op jit(solution)/shard_map/all_to_all | solution.py:331
  33.0 0.0 collective-permute-done.3.received_ref
  33.0 0.6 collective-permute-start.4
  33.7 2.8 %collective-permute-done.4.received_ref = f32[16,256]{1,0:T(8,128)S(1)} collective-permute-done((f32[16,256]{1,0:T(8,128)S(1)}, f32[16,256]{1,0:T(8,128)S(1)}, u32[]{:S(2)}, u32[]{:S(2)}) %collective-permute-start.4) | collective-permute-done | bytes 16416 | tf_op jit(solution)/shard_map/ppermute | solution.py:299
  36.5 0.4 collective-permute-start.5
  36.9 0.8 collective-permute-done.5.refs_2_
  37.8 1.8 %all-to-all-done.1.refs_0_ = bf16[16,8,256]{2,1,0:T(8,128)(2,1)S(1)} async-done(((bf16[16,8,256]{2,1,0:T(8,128)(2,1)}), bf16[16,8,256]{2,1,0:T(8,128)(2,1)S(1)}, u32[]{:S(2)}, u32[]{:S(2)}) %all-to-all-start.1) | async-done | bytes 65568 | tf_op jit(solution)/shard_map/all_to_all | solution.py:331
  39.6 0.7 spread.3
  40.2 1.7 %collective-permute-start.6 = (f32[8,256]{1,0:T(8,128)S(1)}, f32[8,256]{1,0:T(8,128)S(1)}, u32[]{:S(2)}, u32[]{:S(2)}) collective-permute-start(f32[8,256]{1,0:T(8,128)S(1)} %get-tuple-element.36.held_ref.own_ref), channel_id=1, source_target_pairs={{0,16},{16,0},{32,48},{48,32},{64,80},{80,64},{96,112},{112,96},{1... | collective-permute-start | bytes 24584 | tf_op jit(solution)/shard_map/ppermute | solution.py:299
  42.0 3.7 %all-to-all-start.2 = ((bf16[16,8,256]{2,1,0:T(8,128)(2,1)}), bf16[16,8,256]{2,1,0:T(8,128)(2,1)S(1)}, u32[]{:S(2)}, u32[]{:S(2)}) async-start(bf16[16,8,256]{2,1,0:T(8,128)(2,1)} %spread.3), calls=%async_computation.2 | async-start | bytes 131072 | tf_op jit(solution)/shard_map/all_to_all | solution.py:322
  45.7 0.2 near_terms.6.near_0_ref
  45.9 0.0 collective-permute-done.6.received_ref
  45.9 0.7 collective-permute-start.7
  46.5 0.2 near_terms.7.near_1_ref
  46.7 2.5 %collective-permute-done.7.received_ref = f32[16,256]{1,0:T(8,128)S(1)} collective-permute-done((f32[16,256]{1,0:T(8,128)S(1)}, f32[16,256]{1,0:T(8,128)S(1)}, u32[]{:S(2)}, u32[]{:S(2)}) %collective-permute-start.7) | collective-permute-done | bytes 16416 | tf_op jit(solution)/shard_map/ppermute | solution.py:299
  49.2 3.0 %collective-permute-start.8 = (f32[32,256]{1,0:T(8,128)S(1)}, f32[32,256]{1,0:T(8,128)S(1)}, u32[]{:S(2)}, u32[]{:S(2)}) collective-permute-start(f32[32,256]{1,0:T(8,128)S(1)} %join.7.line_ref), channel_id=1, source_target_pairs={{0,112},{16,96},{32,80},{48,64},{64,48},{80,32},{96,16},{112,0},{1... | collective-permute-start | bytes 98312 | tf_op jit(solution)/shard_map/ppermute | solution.py:299
  52.2 0.0 all-to-all-done.2
  52.2 4.4 %terms_to_second.3 = (f32[32,256]{1,0:T(8,128)S(1)}, f32[32,256]{1,0:T(8,128)S(1)}, bf16[8192,256]{1,0:T(8,128)(2,1)S(1)}, bf16[8192,256]{1,0:T(8,128)(2,1)S(1)}) custom-call(bf16[128,256]{1,0:T(8,128)(2,1)S(1)} %bitcast.13, f32[4,256]{1,0:T(4,128)S(1)} %near_terms.6.near_0_ref, f32[4,256]{1,0:T(4,128)S(1)} %near_terms.7.near_1_ref, ...), custom_call_target="tpu_custom_call" | custom-call | flops 5500000256 | tf_op jit(solution)/shard_map/terms_to_second/pallas_call | solution.py:277
  56.6 4.3 %collective-permute-start.9 = (f32[32,256]{1,0:T(8,128)S(1)}, f32[32,256]{1,0:T(8,128)S(1)}, u32[]{:S(2)}, u32[]{:S(2)}) collective-permute-start(f32[32,256]{1,0:T(8,128)S(1)} %get-tuple-element.40), channel_id=1, source_target_pairs={{0,112},{16,96},{32,80},{48,64},{64,48},{80,32},{96,16},{112,0},{1... | collective-permute-start | bytes 98312 | tf_op jit(solution)/shard_map/ppermute | solution.py:299
  60.9 0.0 collective-permute-done.8.more_ref
  60.9 2.9 %terms_to_first.3 = bf16[128,256]{1,0:T(8,128)(2,1)} custom-call(f32[32,256]{1,0:T(8,128)S(1)} %join.7.line_ref, f32[32,256]{1,0:T(8,128)S(1)} %collective-permute-done.8.more_ref, s32[8,128]{1,0:T(8,128)S(1)} %get-tuple-element.25.info_ref, s32[128,128]{1,0:T(8,128)S(1)} %get-tuple-element.26.col_ref, bf16[8192,256]{1,0:T(8,128)(2,1)S(1)} %get-tuple-element.37.left, ...), custom_call_target="tpu_custom_call" | custom-call | flops 2750000128 | tf_op jit(solution)/shard_map/terms_to_first/pallas_call | solution.py:277
  63.9 3.5 %all-to-all-start.3 = ((bf16[16,8,256]{2,1,0:T(8,128)(2,1)}), bf16[16,8,256]{2,1,0:T(8,128)(2,1)S(1)}, u32[]{:S(2)}, u32[]{:S(2)}) async-start(bf16[16,8,256]{2,1,0:T(8,128)(2,1)} %bitcast.7), calls=%async_computation.3 | async-start | bytes 131072 | tf_op jit(solution)/shard_map/all_to_all | solution.py:331
  67.3 0.0 collective-permute-done.9.received_ref
  67.4 0.1 collective-permute-start.10
  67.5 3.2 %collective-permute-done.10.received_ref = f32[16,256]{1,0:T(8,128)S(1)} collective-permute-done((f32[16,256]{1,0:T(8,128)S(1)}, f32[16,256]{1,0:T(8,128)S(1)}, u32[]{:S(2)}, u32[]{:S(2)}) %collective-permute-start.10) | collective-permute-done | bytes 16416 | tf_op jit(solution)/shard_map/ppermute | solution.py:299
  70.7 0.0 collective-permute-start.11
  70.7 1.2 %collective-permute-done.11.refs_2_ = f32[8,256]{1,0:T(8,128)S(1)} collective-permute-done((f32[8,256]{1,0:T(8,128)S(1)}, f32[8,256]{1,0:T(8,128)S(1)}, u32[]{:S(2)}, u32[]{:S(2)}) %collective-permute-start.11) | collective-permute-done | bytes 8224 | tf_op jit(solution)/shard_map/ppermute | solution.py:299
  71.9 2.0 %all-to-all-done.3.refs_0_ = bf16[16,8,256]{2,1,0:T(8,128)(2,1)S(1)} async-done(((bf16[16,8,256]{2,1,0:T(8,128)(2,1)}), bf16[16,8,256]{2,1,0:T(8,128)(2,1)S(1)}, u32[]{:S(2)}, u32[]{:S(2)}) %all-to-all-start.3) | async-done | bytes 65568 | tf_op jit(solution)/shard_map/all_to_all | solution.py:331
  73.9 0.9 last_step.1
  74.8 16.7 %all_to_all.32 = f32[128,1,128]{2,1,0:T(1,128)S(1)} all-to-all(f32[128,1,128]{2,1,0:T(1,128)S(1)} %bitcast.14), channel_id=1, replica_groups=mesh['row'=8,'col'=16] {'row','col'}, dimensions={0} | all-to-all | bytes 131072 | tf_op jit(solution)/shard_map/all_to_all | solution.py:338
  91.5 0.6 slice_reduce_fusion
  (9 shorter events, 0.1 us)
Async XLA Ops:
  0.6 10.9 %copy-start.5 = (s32[128,2]{0,1:T(2,128)S(1)}, s32[128,2]{0,1:T(2,128)}, u32[]{:S(2)}) copy-start(s32[128,2]{0,1:T(2,128)} %param.13) | copy-start | bytes 3076
  0.6 11.0 %copy-start.1 = (f32[3,2048]{1,0:T(4,128)S(1)}, f32[3,2048]{1,0:T(4,128)}, u32[]{:S(2)}) copy-start(f32[3,2048]{1,0:T(4,128)} %friction_ref.1) | copy-start | bytes 73732
  0.7 11.0 %copy-start.2 = (f32[2,2048]{1,0:T(2,128)S(1)}, f32[2,2048]{1,0:T(2,128)}, u32[]{:S(2)}) copy-start(f32[2,2048]{1,0:T(2,128)} %state_ref.3) | copy-start | bytes 49156
  0.7 11.0 %copy-start.3 = (s32[2048]{0:T(1024)S(1)}, s32[2048]{0:T(1024)}, u32[]{:S(2)}) copy-start(s32[2048]{0:T(1024)} %param.15) | copy-start | bytes 24580
  0.7 11.0 %copy-start.4 = (s32[128]{0:T(128)S(1)}, s32[128]{0:T(128)}, u32[]{:S(2)}) copy-start(s32[128]{0:T(128)} %param.14) | copy-start | bytes 1540
  1.7 10.5 %copy-start = (bf16[8,256,256]{2,1,0:T(8,128)(2,1)S(1)}, bf16[8,256,256]{2,1,0:T(8,128)(2,1)}, u32[]{:S(2)}) copy-start(bf16[8,256,256]{2,1,0:T(8,128)(2,1)} %near.7) | copy-start | bytes 3145732
  1.7 10.7 %collective-permute-start = (f32[8,256]{1,0:T(8,128)S(1)}, f32[8,256]{1,0:T(8,128)S(1)}, u32[]{:S(2)}, u32[]{:S(2)}) collective-permute-start(f32[8,256]{1,0:T(8,128)S(1)} %first_deficit.1.held_ref.own_ref), channel_id=1, source_target_pairs={{0,16},{16,0},{32,48},{48,32},{64,80},{80,64},{96,112},{112,96},{1... | collective-permute-start | bytes 24584 | tf_op jit(solution)/shard_map/ppermute | solution.py:299
  3.8 14.8 %all-to-all-start = ((bf16[16,8,256]{2,1,0:T(8,128)(2,1)}), bf16[16,8,256]{2,1,0:T(8,128)(2,1)S(1)}, u32[]{:S(2)}, u32[]{:S(2)}) async-start(bf16[16,8,256]{2,1,0:T(8,128)(2,1)} %spread.2), calls=%async_computation | async-start | bytes 131072 | tf_op jit(solution)/shard_map/all_to_all | solution.py:322
  12.4 3.5 %collective-permute-start.1 = (f32[16,256]{1,0:T(8,128)S(1)}, f32[16,256]{1,0:T(8,128)S(1)}, u32[]{:S(2)}, u32[]{:S(2)}) collective-permute-start(f32[16,256]{1,0:T(8,128)S(1)} %join.4.held_ref), channel_id=1, source_target_pairs={{0,48},{16,32},{32,16},{48,0},{64,112},{80,96},{96,80},{112,64},{1... | collective-permute-start | bytes 49160 | tf_op jit(solution)/shard_map/ppermute | solution.py:299
  15.9 10.6 %collective-permute-start.2 = (f32[32,256]{1,0:T(8,128)S(1)}, f32[32,256]{1,0:T(8,128)S(1)}, u32[]{:S(2)}, u32[]{:S(2)}) collective-permute-start(f32[32,256]{1,0:T(8,128)S(1)} %join.5.line_ref), channel_id=1, source_target_pairs={{0,112},{16,96},{32,80},{48,64},{64,48},{80,32},{96,16},{112,0},{1... | collective-permute-start | bytes 98312 | tf_op jit(solution)/shard_map/ppermute | solution.py:299
  23.0 10.1 %collective-permute-start.3 = (f32[32,256]{1,0:T(8,128)S(1)}, f32[32,256]{1,0:T(8,128)S(1)}, u32[]{:S(2)}, u32[]{:S(2)}) collective-permute-start(f32[32,256]{1,0:T(8,128)S(1)} %get-tuple-element.30), channel_id=1, source_target_pairs={{0,112},{16,96},{32,80},{48,64},{64,48},{80,32},{96,16},{112,0},{1... | collective-permute-start | bytes 98312 | tf_op jit(solution)/shard_map/ppermute | solution.py:299
  29.5 10.0 %all-to-all-start.1 = ((bf16[16,8,256]{2,1,0:T(8,128)(2,1)}), bf16[16,8,256]{2,1,0:T(8,128)(2,1)S(1)}, u32[]{:S(2)}, u32[]{:S(2)}) async-start(bf16[16,8,256]{2,1,0:T(8,128)(2,1)} %bitcast.5), calls=%async_computation.1 | async-start | bytes 131072 | tf_op jit(solution)/shard_map/all_to_all | solution.py:331
  33.0 3.5 %collective-permute-start.4 = (f32[16,256]{1,0:T(8,128)S(1)}, f32[16,256]{1,0:T(8,128)S(1)}, u32[]{:S(2)}, u32[]{:S(2)}) collective-permute-start(f32[16,256]{1,0:T(8,128)S(1)} %get-tuple-element.32), channel_id=1, source_target_pairs={{0,48},{16,32},{32,16},{48,0},{64,112},{80,96},{96,80},{112,64},{1... | collective-permute-start | bytes 49160 | tf_op jit(solution)/shard_map/ppermute | solution.py:299
  36.5 1.2 %collective-permute-start.5 = (f32[8,256]{1,0:T(8,128)S(1)}, f32[8,256]{1,0:T(8,128)S(1)}, u32[]{:S(2)}, u32[]{:S(2)}) collective-permute-start(f32[8,256]{1,0:T(8,128)S(1)} %get-tuple-element.34), channel_id=1, source_target_pairs={{0,16},{16,0},{32,48},{48,32},{64,80},{80,64},{96,112},{112,96},{1... | collective-permute-start | bytes 24584 | tf_op jit(solution)/shard_map/ppermute | solution.py:299
  40.2 5.6 %collective-permute-start.6 = (f32[8,256]{1,0:T(8,128)S(1)}, f32[8,256]{1,0:T(8,128)S(1)}, u32[]{:S(2)}, u32[]{:S(2)}) collective-permute-start(f32[8,256]{1,0:T(8,128)S(1)} %get-tuple-element.36.held_ref.own_ref), channel_id=1, source_target_pairs={{0,16},{16,0},{32,48},{48,32},{64,80},{80,64},{96,112},{112,96},{1... | collective-permute-start | bytes 24584 | tf_op jit(solution)/shard_map/ppermute | solution.py:299
  42.0 10.3 %all-to-all-start.2 = ((bf16[16,8,256]{2,1,0:T(8,128)(2,1)}), bf16[16,8,256]{2,1,0:T(8,128)(2,1)S(1)}, u32[]{:S(2)}, u32[]{:S(2)}) async-start(bf16[16,8,256]{2,1,0:T(8,128)(2,1)} %spread.3), calls=%async_computation.2 | async-start | bytes 131072 | tf_op jit(solution)/shard_map/all_to_all | solution.py:322
  45.9 3.3 %collective-permute-start.7 = (f32[16,256]{1,0:T(8,128)S(1)}, f32[16,256]{1,0:T(8,128)S(1)}, u32[]{:S(2)}, u32[]{:S(2)}) collective-permute-start(f32[16,256]{1,0:T(8,128)S(1)} %join.6.held_ref), channel_id=1, source_target_pairs={{0,48},{16,32},{32,16},{48,0},{64,112},{80,96},{96,80},{112,64},{1... | collective-permute-start | bytes 49160 | tf_op jit(solution)/shard_map/ppermute | solution.py:299
  49.2 11.7 %collective-permute-start.8 = (f32[32,256]{1,0:T(8,128)S(1)}, f32[32,256]{1,0:T(8,128)S(1)}, u32[]{:S(2)}, u32[]{:S(2)}) collective-permute-start(f32[32,256]{1,0:T(8,128)S(1)} %join.7.line_ref), channel_id=1, source_target_pairs={{0,112},{16,96},{32,80},{48,64},{64,48},{80,32},{96,16},{112,0},{1... | collective-permute-start | bytes 98312 | tf_op jit(solution)/shard_map/ppermute | solution.py:299
  56.6 10.7 %collective-permute-start.9 = (f32[32,256]{1,0:T(8,128)S(1)}, f32[32,256]{1,0:T(8,128)S(1)}, u32[]{:S(2)}, u32[]{:S(2)}) collective-permute-start(f32[32,256]{1,0:T(8,128)S(1)} %get-tuple-element.40), channel_id=1, source_target_pairs={{0,112},{16,96},{32,80},{48,64},{64,48},{80,32},{96,16},{112,0},{1... | collective-permute-start | bytes 98312 | tf_op jit(solution)/shard_map/ppermute | solution.py:299
  63.9 10.0 %all-to-all-start.3 = ((bf16[16,8,256]{2,1,0:T(8,128)(2,1)}), bf16[16,8,256]{2,1,0:T(8,128)(2,1)S(1)}, u32[]{:S(2)}, u32[]{:S(2)}) async-start(bf16[16,8,256]{2,1,0:T(8,128)(2,1)} %bitcast.7), calls=%async_computation.3 | async-start | bytes 131072 | tf_op jit(solution)/shard_map/all_to_all | solution.py:331
  67.4 3.3 %collective-permute-start.10 = (f32[16,256]{1,0:T(8,128)S(1)}, f32[16,256]{1,0:T(8,128)S(1)}, u32[]{:S(2)}, u32[]{:S(2)}) collective-permute-start(f32[16,256]{1,0:T(8,128)S(1)} %get-tuple-element.42), channel_id=1, source_target_pairs={{0,48},{16,32},{32,16},{48,0},{64,112},{80,96},{96,80},{112,64},{1... | collective-permute-start | bytes 49160 | tf_op jit(solution)/shard_map/ppermute | solution.py:299
  70.7 1.2 %collective-permute-start.11 = (f32[8,256]{1,0:T(8,128)S(1)}, f32[8,256]{1,0:T(8,128)S(1)}, u32[]{:S(2)}, u32[]{:S(2)}) collective-permute-start(f32[8,256]{1,0:T(8,128)S(1)} %get-tuple-element.44), channel_id=1, source_target_pairs={{0,16},{16,0},{32,48},{48,32},{64,80},{80,64},{96,112},{112,96},{1... | collective-permute-start | bytes 24584 | tf_op jit(solution)/shard_map/ppermute | solution.py:299

commit v4 on v3

--- a/solution.py
+++ b/solution.py
@@ -16,6 +16,7 @@
 bf16 = jnp.bfloat16
 LANES = 128
 PAIRS = 16
+HEAD = 2048
 VMEM = pl.BlockSpec(memory_space=pltpu.VMEM)
 
 
@@ -102,8 +103,8 @@
 
 def collect(mask, terms):
     hot = one_hot(mask)
-    high, mid, low = split3(terms)
-    return mxu(hot, high) + (mxu(hot, mid) + mxu(hot, low))
+    high = terms.astype(bf16)
+    return mxu(hot, high) + mxu(hot, (terms - high.astype(f32)).astype(bf16))
 
 
 def picked(at, values):
@@ -111,48 +112,71 @@
     return mxu(hot, values).astype(bf16)
 
 
-def pair_terms(at, ranks, values, taken, given, wait=lambda row: None):
-    pairs = at.shape[0]
-    width = taken.shape[0] // pairs
+def pair_terms(at, ranks, values, taken, given):
     x = picked(at, values)
-    shape = (PAIRS, PAIRS * width)
-    rank = lax.broadcasted_iota(jnp.int32, shape, 1) - width * lax.broadcasted_iota(jnp.int32, shape, 0)
-    terms = []
-    for k in range(pairs // PAIRS):
-        wait(k * shape[1])
+    groups = at.shape[0] // PAIRS
+    coefs = []
+    for k in range(groups):
+        factor = taken(k)
+        shape = (PAIRS, factor.shape[0])
+        rank = lax.broadcasted_iota(jnp.int32, shape, 1) - shape[1] // PAIRS * lax.broadcasted_iota(jnp.int32, shape, 0)
         rows = slice(k * PAIRS, (k + 1) * PAIRS)
-        part = pl.ds(k * shape[1], shape[1])
         within = (rank >= 0) & (rank < ranks[rows])
-        coef = jnp.where(within, mxu_nt(x[rows], taken[part]), 0.0).astype(bf16)
-        terms.append(mxu(coef, given[part]))
-    return jnp.concatenate(terms, axis=0)
-
-
-def terms_to_second(chunk, everyone_ref, near_0_ref, near_1_ref, info_ref, col_ref, left_hbm, right_hbm, kept_ref, sent_ref,
-                    left, right, sem):
-    copies = []
-    for k in range(left.shape[0] // chunk):
-        part = pl.ds(k * chunk, chunk)
-        copies.append((pltpu.make_async_copy(left_hbm.at[part], left.at[part], sem.at[0, k]),
-                       pltpu.make_async_copy(right_hbm.at[part], right.at[part], sem.at[1, k])))
-        for copy in copies[k]:
+        coefs.append(jnp.where(within, mxu_nt(x[rows], factor), 0.0).astype(bf16))
+    return jnp.concatenate([mxu(coefs[k], given(k)) for k in range(groups)], axis=0)
+
+
+def part_of(k, rows, head, tail):
+    first = head.shape[0] // rows
+    return head[pl.ds(k * rows, rows)] if k < first else tail[pl.ds((k - first) * rows, rows)]
+
+
+def second_sums(chunk, everyone_ref, near_0_ref, near_1_ref, info_ref, col_ref, sources, heads, tails, sem, load_heads,
+                kept_ref, sent_ref):
+    pairs = info_ref.shape[1]
+    rows = (heads[0].shape[0] + tails[0].shape[0]) // pairs * PAIRS
+    fetched = []
+    for which, (source, head, tail) in enumerate(zip(sources, heads, tails)):
+        start = head.shape[0]
+        copies = {}
+        if load_heads:
+            copies[0] = pltpu.make_async_copy(source.at[pl.ds(0, start)], head, sem.at[which, 0])
+        for k in range(tail.shape[0] // chunk):
+            part, at = pl.ds(k * chunk, chunk), start + k * chunk
+            copies[at] = pltpu.make_async_copy(source.at[pl.ds(at, chunk)], tail.at[part], sem.at[which, k + 1])
+        for copy in copies.values():
             copy.start()
 
-    def wait(row):
-        if row % chunk == 0:
-            for copy in copies[row // chunk]:
-                copy.wait()
-
-    terms = pair_terms(col_ref[:, 0:1], col_ref[:, 2:3], everyone_ref[...], left, right, wait)
+        def group(k, head=head, tail=tail, copies=copies):
+            if k * rows in copies:
+                copies[k * rows].wait()
+            return part_of(k, rows, head, tail)
+
+        fetched.append(group)
+    terms = pair_terms(col_ref[:, 0:1], col_ref[:, 2:3], everyone_ref[...], *fetched)
     halves(sums_at(info_ref, 1, 2 * kept_ref.shape[0], terms), kept_ref, sent_ref)
     half = near_0_ref.shape[0]
     kept_ref[0:half, :] += near_0_ref[...]
     kept_ref[half:2 * half, :] += near_1_ref[...]
 
 
-def terms_to_first(line_ref, more_ref, info_ref, col_ref, left, right, first_ref):
+def terms_to_second(chunk, everyone, near_0, near_1, info, col, left_hbm, right_hbm, kept, sent, left_head, right_head,
+                    left, right, sem):
+    second_sums(chunk, everyone, near_0, near_1, info, col, (left_hbm, right_hbm), (left_head, right_head), (left, right),
+                sem, True, kept, sent)
+
+
+def terms_to_second_again(chunk, everyone, near_0, near_1, info, col, left_head, right_head, left_hbm, right_hbm, kept, sent,
+                          left, right, sem):
+    second_sums(chunk, everyone, near_0, near_1, info, col, (left_hbm, right_hbm), (left_head, right_head), (left, right),
+                sem, False, kept, sent)
+
+
+def terms_to_first(line_ref, more_ref, info_ref, col_ref, left_head, right_head, left, right, first_ref):
     line = jnp.concatenate([line_ref[...], more_ref[...]], axis=0).astype(bf16)
-    terms = pair_terms(col_ref[:, 1:2], col_ref[:, 2:3], line, right, left)
+    rows = (left_head.shape[0] + left.shape[0]) // info_ref.shape[1] * PAIRS
+    terms = pair_terms(col_ref[:, 1:2], col_ref[:, 2:3], line, lambda k: part_of(k, rows, right_head, right),
+                       lambda k: part_of(k, rows, left_head, left))
     first_ref[...] = sums_at(info_ref, 0, first_ref.shape[0], terms).astype(bf16)
 
 
@@ -211,11 +235,10 @@
     info_ref[...] = jnp.transpose(columns_of)[:info_ref.shape[0]]
 
 
-def near_terms(which, own_ref, near, out_ref):
-    own = own_ref[...]
-    half = own.shape[0] // 2
-    row_own = lax.broadcasted_iota(jnp.int32, (half, own.shape[1]), 0)
-    mine = own.astype(bf16)
+def near_terms(which, two_ref, near, out_ref):
+    half = out_ref.shape[0]
+    row_own = lax.broadcasted_iota(jnp.int32, out_ref.shape, 0)
+    mine = two_ref[0:2 * half, :].astype(bf16)
     total = jnp.zeros(row_own.shape, f32)
     for k in range(half):
         product = mxu(mine, near[which * half + k])[which * half:(which + 1) * half]
@@ -223,7 +246,7 @@
     out_ref[...] = total
 
 
-def prepare(own_count, columns, pairs_ref, ranks_ref, state_ref, friction_ref, perm_ref, info_ref, col_ref, fields_ref):
+def prepare(own_count, columns, _, pairs_ref, ranks_ref, state_ref, friction_ref, perm_ref, info_ref, col_ref, fields_ref):
     pair_info(own_count, columns, pairs_ref, ranks_ref, info_ref, col_ref)
     to_order(state_ref, friction_ref, perm_ref, fields_ref)
 
@@ -299,10 +322,6 @@
         return lax.ppermute(x, axis, [(r, r ^ distance) for r in range(size)])
 
     own = call(first_deficit, block, [in_hbm(state), in_hbm(perm_row)], 6)
-    info, info_col, fields = call(
-        functools.partial(prepare, own_count, columns),
-        [sds((8, count), jnp.int32), sds((count, LANES), jnp.int32), sds((4, own_count, cluster), f32)],
-        [pairs, ranks.reshape(1, -1), state, friction, perm_row], 0.7)
     near = near_blocks
     left = in_hbm(left_factor.reshape(count * width, cluster))
     right = in_hbm(right_factor.reshape(count * width, cluster))
@@ -310,31 +329,48 @@
     def block_of(blocks, dtype):
         return sds((blocks * own_count, cluster), dtype)
 
-    chunk = 2048
-    scratch = [pltpu.SemaphoreType.DMA((2, count * width // chunk))]
-    loaded = [pltpu.VMEM(x.shape, bf16) for x in (left, right)]
-
-    def exchange(own):
+    chunk, head = 2048, HEAD
+    tail = count * width - head
+    scratch = [pltpu.SemaphoreType.DMA((2, tail // chunk + 1))]
+    kept_there = [pltpu.VMEM((head, cluster), bf16)] * 2
+    loaded = [pltpu.VMEM((tail, cluster), bf16)] * 2
+
+    def exchange(own, prepared=None, heads=None):
         copies = call(spread, sds((columns, own_count, cluster), bf16), [own], 0.6)
         two = call(join, block_of(2, f32), [own, swap(own, "row", HOPS[0])], 0.1)
+        if prepared is None:
+            prepared = call(
+                functools.partial(prepare, own_count, columns),
+                [sds((8, count), jnp.int32), sds((count, LANES), jnp.int32), sds((4, own_count, cluster), f32)],
+                [two, pairs, ranks.reshape(1, -1), state, friction, perm_row], 0.7)
+        info, info_col, _ = prepared
         four = call(join, block_of(4, f32), [two, swap(two, "row", HOPS[1])], 0.1)
         more = swap(four, "row", HOPS[2])
         everyone = lax.all_to_all(copies, "col", 0, 0).reshape(span, cluster)
-        near_term = [call(functools.partial(near_terms, k), sds((own_count // 2, cluster), f32), [own, near], 0.3)
+        near_term = [call(functools.partial(near_terms, k), sds((own_count // 2, cluster), f32), [two, near], 0.3)
                      for k in range(2)]
-        kept, sent, *factors = call(
-            functools.partial(terms_to_second, chunk), [block_of(4, f32)] * 2 + loaded,
-            [everyone, *near_term, info, info_col, left, right], 5, scratch, (left, right))
-        first = call(terms_to_first, block_of(columns, bf16), [four, more, info, info_col, *factors], 2.5)
+        if heads is None:
+            kept, sent, *factors = call(
+                functools.partial(terms_to_second, chunk), [block_of(4, f32)] * 2 + kept_there + loaded,
+                [everyone, *near_term, info, info_col, left, right], 5, scratch, (left, right))
+            heads, factors = factors[:2], factors[2:]
+        else:
+            kept, sent, *factors = call(
+                functools.partial(terms_to_second_again, chunk), [block_of(4, f32)] * 2 + loaded,
+                [everyone, *near_term, info, info_col, *heads, left, right], 5, scratch, (left, right))
+        first = call(terms_to_first, block_of(columns, bf16), [four, more, info, info_col, *heads, *factors], 2.5)
         for blocks, hop in ((2, HOPS[2]), (1, HOPS[1])):
             kept, sent = call(add, [block_of(blocks, f32)] * 2, [kept, swap(sent, "row", hop)], 0.1)
         from_first = lax.all_to_all(first.reshape(columns, own_count, cluster), "col", 0, 0)
-        return [from_first, kept, swap(sent, "row", HOPS[0])]
-
-    slope, own = call(half_step, [sds((2, own_count, cluster), f32), block], [*exchange(own), fields], 0.1)
+        return [from_first, kept, swap(sent, "row", HOPS[0])], prepared, heads
+
+    received, prepared, heads = exchange(own)
+    fields = prepared[2]
+    slope, own = call(half_step, [sds((2, own_count, cluster), f32), block], [*received, fields], 0.1)
+    received, _, _ = exchange(own, prepared, heads)
     devices = rows * columns
     new_state, squares = call(last_step, [sds(state.shape, f32), sds((devices, LANES), f32)],
-                              [*exchange(own), fields, slope, perm_row], 1.3)
+                              [*received, fields, slope, perm_row], 1.3)
     everywhere = lax.all_to_all(squares, ("row", "col"), 0, 0, tiled=True)
     entries = 2.0 * state.shape[1] * devices
     return new_state, jnp.sqrt(jnp.sum(everywhere[:, 0]) / entries)

time: 94.4 us -> 91.9 us (0.974)
  starting transfers between devices: 38.5 us -> 36.5 us
  Pallas kernels: 19.2 us -> 17.5 us
  waiting for transfers between devices: 16.1 us -> 17.4 us
    ppermute x12, starting transfers between devices: 20.1 us -> 17.8 us  [swap(): return lax.ppermute(x, axis, [(r, r ^ distance) for r in range(size)])]
    pallas_call x22, Pallas kernels: 19.2 us -> 17.5 us  [call(): pl.pallas_call(kernel, out_shape=out_shape, in_specs=[pl.BlockSpec(memory...]
  transfers between devices with their start and end apart: 16 -> 16, of which waited for: 8 -> 10; matrix products, arithmetic and copies ran while one was open for 0% -> 0% of each run, Pallas kernels for 18% -> 17%
where the time goes in v4:
time: 91.9 us; the launch traced here: 91.4 us
  starting transfers between devices  36.5 us (40%)
  Pallas kernels  17.5 us (19%)
  waiting for transfers between devices  17.4 us (19%)
  blocking collectives  16.5 us (18%)
  between operations  2.68 us (3%)
    ppermute x12, starting transfers between devices, swap(): return lax.ppermute(x, axis, [(r, r ^ distance) for r in range(size)])  17.8 us
    pallas_call x22, Pallas kernels, call(): pl.pallas_call(kernel, out_shape=out_shape, in_specs=[pl.BlockSpec(memory...  17.5 us
    all_to_all x1, blocking collectives, shards(): everywhere = lax.all_to_all(squares, ('row', 'col'), 0, 0, tiled=True)  16.5 us
    ppermute x12, waiting for transfers between devices, swap(): return lax.ppermute(x, axis, [(r, r ^ distance) for r in range(size)])  12.8 us
    all_to_all x2, starting transfers between devices, exchange(): everyone = lax.all_to_all(copies, 'col', 0, 0).reshape(span, cluster)  11.7 us
    all_to_all x2, starting transfers between devices, exchange(): lax.all_to_all(first.reshape(columns, own_count, cluster), 'col', 0, 0)  6.97 us
    all_to_all x2, waiting for transfers between devices, exchange(): lax.all_to_all(first.reshape(columns, own_count, cluster), 'col', 0, 0)  3.99 us
  transfers between devices with their start and end apart: 16, of which 10 were waited for; matrix products, arithmetic and copies ran while one was open for 0% of the time, Pallas kernels for 17%

profile of v4, /device:TPU:1, one launch (start us, length us, event | category | flops | bytes accessed | tf_op | source)
XLA Modules:
  0.0 91.4 jit_solution(15199450400830747042)
XLA Ops:
  0.6 0.0 copy-start.5
  0.6 0.0 copy-start.1
  0.7 0.0 copy-start.2
  0.7 0.0 copy-start.3
  0.7 0.0 copy-start.4
  0.7 1.0 %first_deficit.1.held_ref.own_ref = f32[8,256]{1,0:T(8,128)S(1)} custom-call(f32[2,2048]{1,0:T(2,128)} %state_ref.3, s32[1,2048]{1,0:T(1,128)} %bitcast.15), custom_call_target="tpu_custom_call" | custom-call | flops 6600000000 | tf_op jit(solution)/shard_map/first_deficit/pallas_call | solution.py:300
  1.7 0.0 copy-start
  1.7 1.5 %collective-permute-start = (f32[8,256]{1,0:T(8,128)S(1)}, f32[8,256]{1,0:T(8,128)S(1)}, u32[]{:S(2)}, u32[]{:S(2)}) collective-permute-start(f32[8,256]{1,0:T(8,128)S(1)} %first_deficit.1.held_ref.own_ref), channel_id=1, source_target_pairs={{0,16},{16,0},{32,48},{48,32},{64,80},{80,64},{96,112},{112,96},{1... | collective-permute-start | bytes 24584 | tf_op jit(solution)/shard_map/ppermute | solution.py:322
  3.2 0.6 spread.2
  3.8 7.7 %all-to-all-start = ((bf16[16,8,256]{2,1,0:T(8,128)(2,1)}), bf16[16,8,256]{2,1,0:T(8,128)(2,1)S(1)}, u32[]{:S(2)}, u32[]{:S(2)}) async-start(bf16[16,8,256]{2,1,0:T(8,128)(2,1)} %spread.2), calls=%async_computation | async-start | bytes 131072 | tf_op jit(solution)/shard_map/all_to_all | solution.py:349
  11.5 0.0 copy-done.5
  11.5 0.1 copy.11.pairs_ref
  11.6 0.0 collective-permute-done.received_ref
  11.6 1.6 %collective-permute-start.1 = (f32[16,256]{1,0:T(8,128)S(1)}, f32[16,256]{1,0:T(8,128)S(1)}, u32[]{:S(2)}, u32[]{:S(2)}) collective-permute-start(f32[16,256]{1,0:T(8,128)S(1)} %join.4.held_ref._.two_ref), channel_id=1, source_target_pairs={{0,48},{16,32},{32,16},{48,0},{64,112},{80,96},{96,80},{112,64},{1... | collective-permute-start | bytes 49160 | tf_op jit(solution)/shard_map/ppermute | solution.py:322
  13.2 0.0 copy-done.1
  13.2 0.0 copy-done.2
  13.2 0.0 copy-done.3
  13.2 0.0 copy-done.4
  13.2 0.5 prepare.1
  13.7 0.0 copy-done
  13.8 0.2 near_terms.4.near_0
  13.9 0.2 near_terms.5.near_1
  14.1 1.0 %collective-permute-done.1.received_ref = f32[16,256]{1,0:T(8,128)S(1)} collective-permute-done((f32[16,256]{1,0:T(8,128)S(1)}, f32[16,256]{1,0:T(8,128)S(1)}, u32[]{:S(2)}, u32[]{:S(2)}) %collective-permute-start.1) | collective-permute-done | bytes 16416 | tf_op jit(solution)/shard_map/ppermute | solution.py:322
  15.2 2.6 %collective-permute-start.2 = (f32[32,256]{1,0:T(8,128)S(1)}, f32[32,256]{1,0:T(8,128)S(1)}, u32[]{:S(2)}, u32[]{:S(2)}) collective-permute-start(f32[32,256]{1,0:T(8,128)S(1)} %join.5.line_ref), channel_id=1, source_target_pairs={{0,112},{16,96},{32,80},{48,64},{64,48},{80,32},{96,16},{112,0},{1... | collective-permute-start | bytes 98312 | tf_op jit(solution)/shard_map/ppermute | solution.py:322
  17.8 0.2 all-to-all-done
  18.0 4.0 %terms_to_second.1 = (f32[32,256]{1,0:T(8,128)S(1)}, f32[32,256]{1,0:T(8,128)S(1)}, bf16[2048,256]{1,0:T(8,128)(2,1)S(1)}, bf16[2048,256]{1,0:T(8,128)(2,1)S(1)}...) custom-call(bf16[128,256]{1,0:T(8,128)(2,1)S(1)} %bitcast.12, f32[4,256]{1,0:T(4,128)S(1)} %near_terms.4.near_0, ...), custom_call_target="tpu_custom_call" | custom-call | flops 5500000256 | tf_op jit(solution)/shard_map/terms_to_second/pallas_call | solution.py:300
  22.0 4.1 %collective-permute-start.3 = (f32[32,256]{1,0:T(8,128)S(1)}, f32[32,256]{1,0:T(8,128)S(1)}, u32[]{:S(2)}, u32[]{:S(2)}) collective-permute-start(f32[32,256]{1,0:T(8,128)S(1)} %get-tuple-element.34), channel_id=1, source_target_pairs={{0,112},{16,96},{32,80},{48,64},{64,48},{80,32},{96,16},{112,0},{1... | collective-permute-start | bytes 98312 | tf_op jit(solution)/shard_map/ppermute | solution.py:322
  26.2 0.0 collective-permute-done.2.more_ref
  26.2 2.7 %terms_to_first.2 = bf16[128,256]{1,0:T(8,128)(2,1)} custom-call(f32[32,256]{1,0:T(8,128)S(1)} %join.5.line_ref, f32[32,256]{1,0:T(8,128)S(1)} %collective-permute-done.2.more_ref, s32[8,128]{1,0:T(8,128)S(1)} %get-tuple-element.27.info.info_ref, s32[128,128]{1,0:T(8,128)S(1)} %get-tuple-element.28.col.col_ref, ...), custom_call_target="tpu_custom_call" | custom-call | flops 2750000128 | tf_op jit(solution)/shard_map/terms_to_first/pallas_call | solution.py:300
  28.9 3.5 %all-to-all-start.1 = ((bf16[16,8,256]{2,1,0:T(8,128)(2,1)}), bf16[16,8,256]{2,1,0:T(8,128)(2,1)S(1)}, u32[]{:S(2)}, u32[]{:S(2)}) async-start(bf16[16,8,256]{2,1,0:T(8,128)(2,1)} %bitcast.5), calls=%async_computation.1 | async-start | bytes 131072 | tf_op jit(solution)/shard_map/all_to_all | solution.py:364
  32.4 0.0 collective-permute-done.3.received_ref
  32.5 0.1 collective-permute-start.4
  32.5 3.3 %collective-permute-done.4.received_ref = f32[16,256]{1,0:T(8,128)S(1)} collective-permute-done((f32[16,256]{1,0:T(8,128)S(1)}, f32[16,256]{1,0:T(8,128)S(1)}, u32[]{:S(2)}, u32[]{:S(2)}) %collective-permute-start.4) | collective-permute-done | bytes 16416 | tf_op jit(solution)/shard_map/ppermute | solution.py:322
  35.8 0.0 collective-permute-start.5
  35.8 1.2 %collective-permute-done.5.refs_2_ = f32[8,256]{1,0:T(8,128)S(1)} collective-permute-done((f32[8,256]{1,0:T(8,128)S(1)}, f32[8,256]{1,0:T(8,128)S(1)}, u32[]{:S(2)}, u32[]{:S(2)}) %collective-permute-start.5) | collective-permute-done | bytes 8224 | tf_op jit(solution)/shard_map/ppermute | solution.py:322
  37.0 2.2 %all-to-all-done.1.refs_0_ = bf16[16,8,256]{2,1,0:T(8,128)(2,1)S(1)} async-done(((bf16[16,8,256]{2,1,0:T(8,128)(2,1)}), bf16[16,8,256]{2,1,0:T(8,128)(2,1)S(1)}, u32[]{:S(2)}, u32[]{:S(2)}) %all-to-all-start.1) | async-done | bytes 65568 | tf_op jit(solution)/shard_map/all_to_all | solution.py:364
  39.2 0.8 collective-permute-start.6
  40.0 0.6 spread.3
  40.7 4.0 %all-to-all-start.2 = ((bf16[16,8,256]{2,1,0:T(8,128)(2,1)}), bf16[16,8,256]{2,1,0:T(8,128)(2,1)S(1)}, u32[]{:S(2)}, u32[]{:S(2)}) async-start(bf16[16,8,256]{2,1,0:T(8,128)(2,1)} %spread.3), calls=%async_computation.2 | async-start | bytes 131072 | tf_op jit(solution)/shard_map/all_to_all | solution.py:349
  44.7 0.0 collective-permute-done.6.received_ref
  44.7 0.4 collective-permute-start.7
  45.2 0.2 near_terms.6.near_0
  45.3 0.2 near_terms.7.near_1
  45.5 2.8 %collective-permute-done.7.received_ref = f32[16,256]{1,0:T(8,128)S(1)} collective-permute-done((f32[16,256]{1,0:T(8,128)S(1)}, f32[16,256]{1,0:T(8,128)S(1)}, u32[]{:S(2)}, u32[]{:S(2)}) %collective-permute-start.7) | collective-permute-done | bytes 16416 | tf_op jit(solution)/shard_map/ppermute | solution.py:322
  48.3 2.5 %collective-permute-start.8 = (f32[32,256]{1,0:T(8,128)S(1)}, f32[32,256]{1,0:T(8,128)S(1)}, u32[]{:S(2)}, u32[]{:S(2)}) collective-permute-start(f32[32,256]{1,0:T(8,128)S(1)} %join.7.line_ref), channel_id=1, source_target_pairs={{0,112},{16,96},{32,80},{48,64},{64,48},{80,32},{96,16},{112,0},{1... | collective-permute-start | bytes 98312 | tf_op jit(solution)/shard_map/ppermute | solution.py:322
  50.8 0.4 all-to-all-done.2
  51.2 3.5 %terms_to_second_again.1 = (f32[32,256]{1,0:T(8,128)S(1)}, f32[32,256]{1,0:T(8,128)S(1)}, bf16[6144,256]{1,0:T(8,128)(2,1)S(1)}, bf16[6144,256]{1,0:T(8,128)(2,1)S(1)}) custom-call(bf16[128,256]{1,0:T(8,128)(2,1)S(1)} %bitcast.13, f32[4,256]{1,0:T(4,128)S(1)} %near_terms.6.near_0, f32[4,256]{1,0:T(4,128)S(1)} %near_terms.7.near_1, ...), custom_call_target="tpu_custom_call" | custom-call | flops 5500000256 | tf_op jit(solution)/shard_map/terms_to_second_again/pallas_call | solution.py:300
  54.7 4.0 %collective-permute-start.9 = (f32[32,256]{1,0:T(8,128)S(1)}, f32[32,256]{1,0:T(8,128)S(1)}, u32[]{:S(2)}, u32[]{:S(2)}) collective-permute-start(f32[32,256]{1,0:T(8,128)S(1)} %get-tuple-element.44), channel_id=1, source_target_pairs={{0,112},{16,96},{32,80},{48,64},{64,48},{80,32},{96,16},{112,0},{1... | collective-permute-start | bytes 98312 | tf_op jit(solution)/shard_map/ppermute | solution.py:322
  58.8 0.0 collective-permute-done.8.more_ref
  58.8 2.7 %terms_to_first.3 = bf16[128,256]{1,0:T(8,128)(2,1)} custom-call(f32[32,256]{1,0:T(8,128)S(1)} %join.7.line_ref, f32[32,256]{1,0:T(8,128)S(1)} %collective-permute-done.8.more_ref, s32[8,128]{1,0:T(8,128)S(1)} %get-tuple-element.27.info.info_ref, s32[128,128]{1,0:T(8,128)S(1)} %get-tuple-element.28.col.col_ref, ...), custom_call_target="tpu_custom_call" | custom-call | flops 2750000128 | tf_op jit(solution)/shard_map/terms_to_first/pallas_call | solution.py:300
  61.5 3.5 %all-to-all-start.3 = ((bf16[16,8,256]{2,1,0:T(8,128)(2,1)}), bf16[16,8,256]{2,1,0:T(8,128)(2,1)S(1)}, u32[]{:S(2)}, u32[]{:S(2)}) async-start(bf16[16,8,256]{2,1,0:T(8,128)(2,1)} %bitcast.7), calls=%async_computation.3 | async-start | bytes 131072 | tf_op jit(solution)/shard_map/all_to_all | solution.py:364
  65.0 0.0 collective-permute-done.9.received_ref
  65.0 0.1 collective-permute-start.10
  65.1 3.3 %collective-permute-done.10.received_ref = f32[16,256]{1,0:T(8,128)S(1)} collective-permute-done((f32[16,256]{1,0:T(8,128)S(1)}, f32[16,256]{1,0:T(8,128)S(1)}, u32[]{:S(2)}, u32[]{:S(2)}) %collective-permute-start.10) | collective-permute-done | bytes 16416 | tf_op jit(solution)/shard_map/ppermute | solution.py:322
  68.5 0.0 collective-permute-start.11
  68.5 1.2 %collective-permute-done.11.refs_2_ = f32[8,256]{1,0:T(8,128)S(1)} collective-permute-done((f32[8,256]{1,0:T(8,128)S(1)}, f32[8,256]{1,0:T(8,128)S(1)}, u32[]{:S(2)}, u32[]{:S(2)}) %collective-permute-start.11) | collective-permute-done | bytes 8224 | tf_op jit(solution)/shard_map/ppermute | solution.py:322
  69.7 1.8 %all-to-all-done.3.refs_0_ = bf16[16,8,256]{2,1,0:T(8,128)(2,1)S(1)} async-done(((bf16[16,8,256]{2,1,0:T(8,128)(2,1)}), bf16[16,8,256]{2,1,0:T(8,128)(2,1)S(1)}, u32[]{:S(2)}, u32[]{:S(2)}) %all-to-all-start.3) | async-done | bytes 65568 | tf_op jit(solution)/shard_map/all_to_all | solution.py:364
  71.5 0.9 %last_step.1 = (f32[2,2048]{1,0:T(2,128)}, f32[128,128]{1,0:T(8,128)S(1)}) custom-call(bf16[16,8,256]{2,1,0:T(8,128)(2,1)S(1)} %all-to-all-done.3.refs_0_, f32[8,256]{1,0:T(8,128)S(1)} %get-tuple-element.47.refs_1_, f32[8,256]{1,0:T(8,128)S(1)} %collective-permute-done.11.refs_2_, f32[4,8,256]{2,1,0:T(8,128)S(1)} %get-tuple-element.39.refs_3_, ...), custom_call_target="tpu_custom_call" | custom-call | flops 1430000000 | tf_op jit(solution)/shard_map/last_step/pallas_call | solution.py:300
  72.4 16.5 %all_to_all.32 = f32[128,1,128]{2,1,0:T(1,128)S(1)} all-to-all(f32[128,1,128]{2,1,0:T(1,128)S(1)} %bitcast.14), channel_id=1, replica_groups=mesh['row'=8,'col'=16] {'row','col'}, dimensions={0} | all-to-all | bytes 131072 | tf_op jit(solution)/shard_map/all_to_all | solution.py:374
  89.0 0.6 slice_reduce_fusion
  (9 shorter events, 0.1 us)
Async XLA Ops:
  0.6 10.9 %copy-start.5 = (s32[128,2]{0,1:T(2,128)S(1)}, s32[128,2]{0,1:T(2,128)}, u32[]{:S(2)}) copy-start(s32[128,2]{0,1:T(2,128)} %param.13) | copy-start | bytes 3076
  0.6 12.6 %copy-start.1 = (f32[3,2048]{1,0:T(4,128)S(1)}, f32[3,2048]{1,0:T(4,128)}, u32[]{:S(2)}) copy-start(f32[3,2048]{1,0:T(4,128)} %friction_ref.1) | copy-start | bytes 73732
  0.7 12.6 %copy-start.2 = (f32[2,2048]{1,0:T(2,128)S(1)}, f32[2,2048]{1,0:T(2,128)}, u32[]{:S(2)}) copy-start(f32[2,2048]{1,0:T(2,128)} %state_ref.3) | copy-start | bytes 49156
  0.7 12.5 %copy-start.3 = (s32[2048]{0:T(1024)S(1)}, s32[2048]{0:T(1024)}, u32[]{:S(2)}) copy-start(s32[2048]{0:T(1024)} %param.15) | copy-start | bytes 24580
  0.7 12.5 %copy-start.4 = (s32[128]{0:T(128)S(1)}, s32[128]{0:T(128)}, u32[]{:S(2)}) copy-start(s32[128]{0:T(128)} %param.14) | copy-start | bytes 1540
  1.7 12.1 %copy-start = (bf16[8,256,256]{2,1,0:T(8,128)(2,1)S(1)}, bf16[8,256,256]{2,1,0:T(8,128)(2,1)}, u32[]{:S(2)}) copy-start(bf16[8,256,256]{2,1,0:T(8,128)(2,1)} %near.7) | copy-start | bytes 3145732
  1.7 10.0 %collective-permute-start = (f32[8,256]{1,0:T(8,128)S(1)}, f32[8,256]{1,0:T(8,128)S(1)}, u32[]{:S(2)}, u32[]{:S(2)}) collective-permute-start(f32[8,256]{1,0:T(8,128)S(1)} %first_deficit.1.held_ref.own_ref), channel_id=1, source_target_pairs={{0,16},{16,0},{32,48},{48,32},{64,80},{80,64},{96,112},{112,96},{1... | collective-permute-start | bytes 24584 | tf_op jit(solution)/shard_map/ppermute | solution.py:322
  3.8 14.2 %all-to-all-start = ((bf16[16,8,256]{2,1,0:T(8,128)(2,1)}), bf16[16,8,256]{2,1,0:T(8,128)(2,1)S(1)}, u32[]{:S(2)}, u32[]{:S(2)}) async-start(bf16[16,8,256]{2,1,0:T(8,128)(2,1)} %spread.2), calls=%async_computation | async-start | bytes 131072 | tf_op jit(solution)/shard_map/all_to_all | solution.py:349
  11.6 3.5 %collective-permute-start.1 = (f32[16,256]{1,0:T(8,128)S(1)}, f32[16,256]{1,0:T(8,128)S(1)}, u32[]{:S(2)}, u32[]{:S(2)}) collective-permute-start(f32[16,256]{1,0:T(8,128)S(1)} %join.4.held_ref._.two_ref), channel_id=1, source_target_pairs={{0,48},{16,32},{32,16},{48,0},{64,112},{80,96},{96,80},{112,64},{1... | collective-permute-start | bytes 49160 | tf_op jit(solution)/shard_map/ppermute | solution.py:322
  15.2 11.0 %collective-permute-start.2 = (f32[32,256]{1,0:T(8,128)S(1)}, f32[32,256]{1,0:T(8,128)S(1)}, u32[]{:S(2)}, u32[]{:S(2)}) collective-permute-start(f32[32,256]{1,0:T(8,128)S(1)} %join.5.line_ref), channel_id=1, source_target_pairs={{0,112},{16,96},{32,80},{48,64},{64,48},{80,32},{96,16},{112,0},{1... | collective-permute-start | bytes 98312 | tf_op jit(solution)/shard_map/ppermute | solution.py:322
  22.0 10.4 %collective-permute-start.3 = (f32[32,256]{1,0:T(8,128)S(1)}, f32[32,256]{1,0:T(8,128)S(1)}, u32[]{:S(2)}, u32[]{:S(2)}) collective-permute-start(f32[32,256]{1,0:T(8,128)S(1)} %get-tuple-element.34), channel_id=1, source_target_pairs={{0,112},{16,96},{32,80},{48,64},{64,48},{80,32},{96,16},{112,0},{1... | collective-permute-start | bytes 98312 | tf_op jit(solution)/shard_map/ppermute | solution.py:322
  28.9 10.3 %all-to-all-start.1 = ((bf16[16,8,256]{2,1,0:T(8,128)(2,1)}), bf16[16,8,256]{2,1,0:T(8,128)(2,1)S(1)}, u32[]{:S(2)}, u32[]{:S(2)}) async-start(bf16[16,8,256]{2,1,0:T(8,128)(2,1)} %bitcast.5), calls=%async_computation.1 | async-start | bytes 131072 | tf_op jit(solution)/shard_map/all_to_all | solution.py:364
  32.5 3.4 %collective-permute-start.4 = (f32[16,256]{1,0:T(8,128)S(1)}, f32[16,256]{1,0:T(8,128)S(1)}, u32[]{:S(2)}, u32[]{:S(2)}) collective-permute-start(f32[16,256]{1,0:T(8,128)S(1)} %get-tuple-element.36), channel_id=1, source_target_pairs={{0,48},{16,32},{32,16},{48,0},{64,112},{80,96},{96,80},{112,64},{1... | collective-permute-start | bytes 49160 | tf_op jit(solution)/shard_map/ppermute | solution.py:322
  35.8 1.2 %collective-permute-start.5 = (f32[8,256]{1,0:T(8,128)S(1)}, f32[8,256]{1,0:T(8,128)S(1)}, u32[]{:S(2)}, u32[]{:S(2)}) collective-permute-start(f32[8,256]{1,0:T(8,128)S(1)} %get-tuple-element.38), channel_id=1, source_target_pairs={{0,16},{16,0},{32,48},{48,32},{64,80},{80,64},{96,112},{112,96},{1... | collective-permute-start | bytes 24584 | tf_op jit(solution)/shard_map/ppermute | solution.py:322
  39.2 5.5 %collective-permute-start.6 = (f32[8,256]{1,0:T(8,128)S(1)}, f32[8,256]{1,0:T(8,128)S(1)}, u32[]{:S(2)}, u32[]{:S(2)}) collective-permute-start(f32[8,256]{1,0:T(8,128)S(1)} %get-tuple-element.40.held_ref.own_ref), channel_id=1, source_target_pairs={{0,16},{16,0},{32,48},{48,32},{64,80},{80,64},{96,112},{112,96},{1... | collective-permute-start | bytes 24584 | tf_op jit(solution)/shard_map/ppermute | solution.py:322
  40.7 10.5 %all-to-all-start.2 = ((bf16[16,8,256]{2,1,0:T(8,128)(2,1)}), bf16[16,8,256]{2,1,0:T(8,128)(2,1)S(1)}, u32[]{:S(2)}, u32[]{:S(2)}) async-start(bf16[16,8,256]{2,1,0:T(8,128)(2,1)} %spread.3), calls=%async_computation.2 | async-start | bytes 131072 | tf_op jit(solution)/shard_map/all_to_all | solution.py:349
  44.7 3.6 %collective-permute-start.7 = (f32[16,256]{1,0:T(8,128)S(1)}, f32[16,256]{1,0:T(8,128)S(1)}, u32[]{:S(2)}, u32[]{:S(2)}) collective-permute-start(f32[16,256]{1,0:T(8,128)S(1)} %join.6.held_ref.two_ref), channel_id=1, source_target_pairs={{0,48},{16,32},{32,16},{48,0},{64,112},{80,96},{96,80},{112,64},{1... | collective-permute-start | bytes 49160 | tf_op jit(solution)/shard_map/ppermute | solution.py:322
  48.3 10.5 %collective-permute-start.8 = (f32[32,256]{1,0:T(8,128)S(1)}, f32[32,256]{1,0:T(8,128)S(1)}, u32[]{:S(2)}, u32[]{:S(2)}) collective-permute-start(f32[32,256]{1,0:T(8,128)S(1)} %join.7.line_ref), channel_id=1, source_target_pairs={{0,112},{16,96},{32,80},{48,64},{64,48},{80,32},{96,16},{112,0},{1... | collective-permute-start | bytes 98312 | tf_op jit(solution)/shard_map/ppermute | solution.py:322
  54.7 10.3 %collective-permute-start.9 = (f32[32,256]{1,0:T(8,128)S(1)}, f32[32,256]{1,0:T(8,128)S(1)}, u32[]{:S(2)}, u32[]{:S(2)}) collective-permute-start(f32[32,256]{1,0:T(8,128)S(1)} %get-tuple-element.44), channel_id=1, source_target_pairs={{0,112},{16,96},{32,80},{48,64},{64,48},{80,32},{96,16},{112,0},{1... | collective-permute-start | bytes 98312 | tf_op jit(solution)/shard_map/ppermute | solution.py:322
  61.5 9.9 %all-to-all-start.3 = ((bf16[16,8,256]{2,1,0:T(8,128)(2,1)}), bf16[16,8,256]{2,1,0:T(8,128)(2,1)S(1)}, u32[]{:S(2)}, u32[]{:S(2)}) async-start(bf16[16,8,256]{2,1,0:T(8,128)(2,1)} %bitcast.7), calls=%async_computation.3 | async-start | bytes 131072 | tf_op jit(solution)/shard_map/all_to_all | solution.py:364
  65.0 3.4 %collective-permute-start.10 = (f32[16,256]{1,0:T(8,128)S(1)}, f32[16,256]{1,0:T(8,128)S(1)}, u32[]{:S(2)}, u32[]{:S(2)}) collective-permute-start(f32[16,256]{1,0:T(8,128)S(1)} %get-tuple-element.46), channel_id=1, source_target_pairs={{0,48},{16,32},{32,16},{48,0},{64,112},{80,96},{96,80},{112,64},{1... | collective-permute-start | bytes 49160 | tf_op jit(solution)/shard_map/ppermute | solution.py:322
  68.5 1.2 %collective-permute-start.11 = (f32[8,256]{1,0:T(8,128)S(1)}, f32[8,256]{1,0:T(8,128)S(1)}, u32[]{:S(2)}, u32[]{:S(2)}) collective-permute-start(f32[8,256]{1,0:T(8,128)S(1)} %get-tuple-element.48), channel_id=1, source_target_pairs={{0,16},{16,0},{32,48},{48,32},{64,80},{80,64},{96,112},{112,96},{1... | collective-permute-start | bytes 24584 | tf_op jit(solution)/shard_map/ppermute | solution.py:322

commit v5 on v4

--- a/solution.py
+++ b/solution.py
@@ -275,19 +275,22 @@
 
 
 def last_step(*refs):
-    *stress_refs, fields_ref, slope_ref, perm_ref, out_ref, sum_ref = refs
+    *stress_refs, fields_ref, slope_ref, new_ref, sum_ref = refs
     lv, lt, a_sigma, b_sigma = (fields_ref[k] for k in range(4))
     first = (slope_ref[0], slope_ref[1])
     second = slopes(lv + step_size * first[0], lt + step_size * first[1], a_sigma, b_sigma, total_stress(stress_refs))
     squares = jnp.zeros(lv.shape, f32)
-    news = []
     for k, base in enumerate((lv, lt)):
         new = base + 0.5 * step_size * (first[k] + second[k])
-        news.append(new)
+        new_ref[k] = new
         scaled = 0.5 * step_size * (second[k] - first[k]) / (abs_tol + rel_tol * jnp.abs(new))
         squares += scaled * scaled
     sum_ref[...] = jnp.full(sum_ref.shape, jnp.sum(squares), f32)
-    from_order(news, perm_ref[...], out_ref)
+
+
+def finish(entries, everywhere_ref, new_ref, perm_ref, out_ref, norm_ref):
+    norm_ref[...] = jnp.sqrt(jnp.sum(everywhere_ref[...], axis=0, keepdims=True)[:, 0:1] / entries)
+    from_order([new_ref[0], new_ref[1]], perm_ref[...], out_ref)
 
 
 def in_hbm(x):
@@ -369,11 +372,13 @@
     slope, own = call(half_step, [sds((2, own_count, cluster), f32), block], [*received, fields], 0.1)
     received, _, _ = exchange(own, prepared, heads)
     devices = rows * columns
-    new_state, squares = call(last_step, [sds(state.shape, f32), sds((devices, LANES), f32)],
-                              [*received, fields, slope, perm_row], 1.3)
+    new, squares = call(last_step, [sds((2, own_count, cluster), f32), sds((devices, LANES), f32)],
+                        [*received, fields, slope], 0.2)
     everywhere = lax.all_to_all(squares, ("row", "col"), 0, 0, tiled=True)
     entries = 2.0 * state.shape[1] * devices
-    return new_state, jnp.sqrt(jnp.sum(everywhere[:, 0]) / entries)
+    new_state, norm = call(functools.partial(finish, entries), [sds(state.shape, f32), sds((1, 1), f32)],
+                           [everywhere, new, perm_row], 1)
+    return new_state, norm.reshape(())
 
 
 def solution(mesh):

time: 91.9 us -> 89.5 us (0.974)
  between operations: 2.68 us -> 0.87 us
    pallas_call x22 -> x23, Pallas kernels: 17.5 us -> 17.6 us  [call(): pl.pallas_call(kernel, out_shape=out_shape, in_specs=[pl.BlockSpec(memory...]
where the time goes in v5:
time: 89.5 us; the launch traced here: 89.1 us
  starting transfers between devices  36.5 us (41%)
  Pallas kernels  17.6 us (20%)
  waiting for transfers between devices  17.4 us (19%)
  blocking collectives  16.5 us (18%)
    ppermute x12, starting transfers between devices, swap(): return lax.ppermute(x, axis, [(r, r ^ distance) for r in range(size)])  17.8 us
    pallas_call x23, Pallas kernels, call(): pl.pallas_call(kernel, out_shape=out_shape, in_specs=[pl.BlockSpec(memory...  17.6 us
    all_to_all x1, blocking collectives, shards(): everywhere = lax.all_to_all(squares, ('row', 'col'), 0, 0, tiled=True)  16.5 us
    ppermute x12, waiting for transfers between devices, swap(): return lax.ppermute(x, axis, [(r, r ^ distance) for r in range(size)])  12.8 us
    all_to_all x2, starting transfers between devices, exchange(): everyone = lax.all_to_all(copies, 'col', 0, 0).reshape(span, cluster)  11.7 us
    all_to_all x2, starting transfers between devices, exchange(): lax.all_to_all(first.reshape(columns, own_count, cluster), 'col', 0, 0)  7 us
    all_to_all x2, waiting for transfers between devices, exchange(): lax.all_to_all(first.reshape(columns, own_count, cluster), 'col', 0, 0)  4.01 us
  transfers between devices with their start and end apart: 16, of which 10 were waited for; matrix products, arithmetic and copies ran while one was open for 0% of the time, Pallas kernels for 17%

profile of v5, /device:TPU:1, one launch (start us, length us, event | category | flops | bytes accessed | tf_op | source)
XLA Modules:
  0.0 89.1 jit_solution(5043840922606356116)
XLA Ops:
  0.6 0.0 copy-start.5
  0.6 0.0 copy-start.1
  0.7 0.0 copy-start.2
  0.7 0.0 copy-start.3
  0.7 0.0 copy-start.4
  0.7 1.0 %first_deficit.1.held_ref.own_ref = f32[8,256]{1,0:T(8,128)S(1)} custom-call(f32[2,2048]{1,0:T(2,128)} %state_ref.3, s32[1,2048]{1,0:T(1,128)} %bitcast.17), custom_call_target="tpu_custom_call" | custom-call | flops 6600000000 | tf_op jit(solution)/shard_map/first_deficit/pallas_call | solution.py:303
  1.7 0.0 copy-start
  1.7 1.5 %collective-permute-start = (f32[8,256]{1,0:T(8,128)S(1)}, f32[8,256]{1,0:T(8,128)S(1)}, u32[]{:S(2)}, u32[]{:S(2)}) collective-permute-start(f32[8,256]{1,0:T(8,128)S(1)} %first_deficit.1.held_ref.own_ref), channel_id=1, source_target_pairs={{0,16},{16,0},{32,48},{48,32},{64,80},{80,64},{96,112},{112,96},{1... | collective-permute-start | bytes 24584 | tf_op jit(solution)/shard_map/ppermute | solution.py:325
  3.2 0.6 spread.2
  3.8 7.7 %all-to-all-start = ((bf16[16,8,256]{2,1,0:T(8,128)(2,1)}), bf16[16,8,256]{2,1,0:T(8,128)(2,1)S(1)}, u32[]{:S(2)}, u32[]{:S(2)}) async-start(bf16[16,8,256]{2,1,0:T(8,128)(2,1)} %spread.2), calls=%async_computation | async-start | bytes 131072 | tf_op jit(solution)/shard_map/all_to_all | solution.py:352
  11.5 0.0 copy-done.5
  11.5 0.1 copy.11.pairs_ref
  11.6 0.0 collective-permute-done.received_ref
  11.6 1.6 %collective-permute-start.1 = (f32[16,256]{1,0:T(8,128)S(1)}, f32[16,256]{1,0:T(8,128)S(1)}, u32[]{:S(2)}, u32[]{:S(2)}) collective-permute-start(f32[16,256]{1,0:T(8,128)S(1)} %join.4.held_ref._.two_ref), channel_id=1, source_target_pairs={{0,48},{16,32},{32,16},{48,0},{64,112},{80,96},{96,80},{112,64},{1... | collective-permute-start | bytes 49160 | tf_op jit(solution)/shard_map/ppermute | solution.py:325
  13.2 0.0 copy-done.1
  13.2 0.0 copy-done.2
  13.2 0.0 copy-done.3
  13.2 0.0 copy-done.4
  13.2 0.5 prepare.1
  13.7 0.0 copy-done
  13.7 0.2 near_terms.4.near_0
  13.9 0.2 near_terms.5.near_1
  14.1 1.0 %collective-permute-done.1.received_ref = f32[16,256]{1,0:T(8,128)S(1)} collective-permute-done((f32[16,256]{1,0:T(8,128)S(1)}, f32[16,256]{1,0:T(8,128)S(1)}, u32[]{:S(2)}, u32[]{:S(2)}) %collective-permute-start.1) | collective-permute-done | bytes 16416 | tf_op jit(solution)/shard_map/ppermute | solution.py:325
  15.1 2.6 %collective-permute-start.2 = (f32[32,256]{1,0:T(8,128)S(1)}, f32[32,256]{1,0:T(8,128)S(1)}, u32[]{:S(2)}, u32[]{:S(2)}) collective-permute-start(f32[32,256]{1,0:T(8,128)S(1)} %join.5.line_ref), channel_id=1, source_target_pairs={{0,112},{16,96},{32,80},{48,64},{64,48},{80,32},{96,16},{112,0},{1... | collective-permute-start | bytes 98312 | tf_op jit(solution)/shard_map/ppermute | solution.py:325
  17.8 0.2 all-to-all-done
  18.0 4.0 %terms_to_second.1 = (f32[32,256]{1,0:T(8,128)S(1)}, f32[32,256]{1,0:T(8,128)S(1)}, bf16[2048,256]{1,0:T(8,128)(2,1)S(1)}, bf16[2048,256]{1,0:T(8,128)(2,1)S(1)}...) custom-call(bf16[128,256]{1,0:T(8,128)(2,1)S(1)} %bitcast.13, f32[4,256]{1,0:T(4,128)S(1)} %near_terms.4.near_0, ...), custom_call_target="tpu_custom_call" | custom-call | flops 5500000256 | tf_op jit(solution)/shard_map/terms_to_second/pallas_call | solution.py:303
  22.0 4.1 %collective-permute-start.3 = (f32[32,256]{1,0:T(8,128)S(1)}, f32[32,256]{1,0:T(8,128)S(1)}, u32[]{:S(2)}, u32[]{:S(2)}) collective-permute-start(f32[32,256]{1,0:T(8,128)S(1)} %get-tuple-element.36), channel_id=1, source_target_pairs={{0,112},{16,96},{32,80},{48,64},{64,48},{80,32},{96,16},{112,0},{1... | collective-permute-start | bytes 98312 | tf_op jit(solution)/shard_map/ppermute | solution.py:325
  26.2 0.0 collective-permute-done.2.more_ref
  26.2 2.7 %terms_to_first.2 = bf16[128,256]{1,0:T(8,128)(2,1)} custom-call(f32[32,256]{1,0:T(8,128)S(1)} %join.5.line_ref, f32[32,256]{1,0:T(8,128)S(1)} %collective-permute-done.2.more_ref, s32[8,128]{1,0:T(8,128)S(1)} %get-tuple-element.29.info.info_ref, s32[128,128]{1,0:T(8,128)S(1)} %get-tuple-element.30.col.col_ref, ...), custom_call_target="tpu_custom_call" | custom-call | flops 2750000128 | tf_op jit(solution)/shard_map/terms_to_first/pallas_call | solution.py:303
  28.9 3.5 %all-to-all-start.1 = ((bf16[16,8,256]{2,1,0:T(8,128)(2,1)}), bf16[16,8,256]{2,1,0:T(8,128)(2,1)S(1)}, u32[]{:S(2)}, u32[]{:S(2)}) async-start(bf16[16,8,256]{2,1,0:T(8,128)(2,1)} %bitcast.5), calls=%async_computation.1 | async-start | bytes 131072 | tf_op jit(solution)/shard_map/all_to_all | solution.py:367
  32.4 0.0 collective-permute-done.3.received_ref
  32.4 0.1 collective-permute-start.4
  32.5 3.3 %collective-permute-done.4.received_ref = f32[16,256]{1,0:T(8,128)S(1)} collective-permute-done((f32[16,256]{1,0:T(8,128)S(1)}, f32[16,256]{1,0:T(8,128)S(1)}, u32[]{:S(2)}, u32[]{:S(2)}) %collective-permute-start.4) | collective-permute-done | bytes 16416 | tf_op jit(solution)/shard_map/ppermute | solution.py:325
  35.8 0.0 collective-permute-start.5
  35.8 1.2 %collective-permute-done.5.refs_2_ = f32[8,256]{1,0:T(8,128)S(1)} collective-permute-done((f32[8,256]{1,0:T(8,128)S(1)}, f32[8,256]{1,0:T(8,128)S(1)}, u32[]{:S(2)}, u32[]{:S(2)}) %collective-permute-start.5) | collective-permute-done | bytes 8224 | tf_op jit(solution)/shard_map/ppermute | solution.py:325
  37.0 2.2 %all-to-all-done.1.refs_0_ = bf16[16,8,256]{2,1,0:T(8,128)(2,1)S(1)} async-done(((bf16[16,8,256]{2,1,0:T(8,128)(2,1)}), bf16[16,8,256]{2,1,0:T(8,128)(2,1)S(1)}, u32[]{:S(2)}, u32[]{:S(2)}) %all-to-all-start.1) | async-done | bytes 65568 | tf_op jit(solution)/shard_map/all_to_all | solution.py:367
  39.2 0.8 collective-permute-start.6
  40.0 0.6 spread.3
  40.6 4.0 %all-to-all-start.2 = ((bf16[16,8,256]{2,1,0:T(8,128)(2,1)}), bf16[16,8,256]{2,1,0:T(8,128)(2,1)S(1)}, u32[]{:S(2)}, u32[]{:S(2)}) async-start(bf16[16,8,256]{2,1,0:T(8,128)(2,1)} %spread.3), calls=%async_computation.2 | async-start | bytes 131072 | tf_op jit(solution)/shard_map/all_to_all | solution.py:352
  44.6 0.0 collective-permute-done.6.received_ref
  44.7 0.5 collective-permute-start.7
  45.1 0.2 near_terms.6.near_0
  45.3 0.2 near_terms.7.near_1
  45.5 2.8 %collective-permute-done.7.received_ref = f32[16,256]{1,0:T(8,128)S(1)} collective-permute-done((f32[16,256]{1,0:T(8,128)S(1)}, f32[16,256]{1,0:T(8,128)S(1)}, u32[]{:S(2)}, u32[]{:S(2)}) %collective-permute-start.7) | collective-permute-done | bytes 16416 | tf_op jit(solution)/shard_map/ppermute | solution.py:325
  48.3 2.5 %collective-permute-start.8 = (f32[32,256]{1,0:T(8,128)S(1)}, f32[32,256]{1,0:T(8,128)S(1)}, u32[]{:S(2)}, u32[]{:S(2)}) collective-permute-start(f32[32,256]{1,0:T(8,128)S(1)} %join.7.line_ref), channel_id=1, source_target_pairs={{0,112},{16,96},{32,80},{48,64},{64,48},{80,32},{96,16},{112,0},{1... | collective-permute-start | bytes 98312 | tf_op jit(solution)/shard_map/ppermute | solution.py:325
  50.7 0.4 all-to-all-done.2
  51.2 3.5 %terms_to_second_again.1 = (f32[32,256]{1,0:T(8,128)S(1)}, f32[32,256]{1,0:T(8,128)S(1)}, bf16[6144,256]{1,0:T(8,128)(2,1)S(1)}, bf16[6144,256]{1,0:T(8,128)(2,1)S(1)}) custom-call(bf16[128,256]{1,0:T(8,128)(2,1)S(1)} %bitcast.14, f32[4,256]{1,0:T(4,128)S(1)} %near_terms.6.near_0, f32[4,256]{1,0:T(4,128)S(1)} %near_terms.7.near_1, ...), custom_call_target="tpu_custom_call" | custom-call | flops 5500000256 | tf_op jit(solution)/shard_map/terms_to_second_again/pallas_call | solution.py:303
  54.7 4.0 %collective-permute-start.9 = (f32[32,256]{1,0:T(8,128)S(1)}, f32[32,256]{1,0:T(8,128)S(1)}, u32[]{:S(2)}, u32[]{:S(2)}) collective-permute-start(f32[32,256]{1,0:T(8,128)S(1)} %get-tuple-element.46), channel_id=1, source_target_pairs={{0,112},{16,96},{32,80},{48,64},{64,48},{80,32},{96,16},{112,0},{1... | collective-permute-start | bytes 98312 | tf_op jit(solution)/shard_map/ppermute | solution.py:325
  58.7 0.0 collective-permute-done.8.more_ref
  58.7 2.7 %terms_to_first.3 = bf16[128,256]{1,0:T(8,128)(2,1)} custom-call(f32[32,256]{1,0:T(8,128)S(1)} %join.7.line_ref, f32[32,256]{1,0:T(8,128)S(1)} %collective-permute-done.8.more_ref, s32[8,128]{1,0:T(8,128)S(1)} %get-tuple-element.29.info.info_ref, s32[128,128]{1,0:T(8,128)S(1)} %get-tuple-element.30.col.col_ref, ...), custom_call_target="tpu_custom_call" | custom-call | flops 2750000128 | tf_op jit(solution)/shard_map/terms_to_first/pallas_call | solution.py:303
  61.4 3.5 %all-to-all-start.3 = ((bf16[16,8,256]{2,1,0:T(8,128)(2,1)}), bf16[16,8,256]{2,1,0:T(8,128)(2,1)S(1)}, u32[]{:S(2)}, u32[]{:S(2)}) async-start(bf16[16,8,256]{2,1,0:T(8,128)(2,1)} %bitcast.7), calls=%async_computation.3 | async-start | bytes 131072 | tf_op jit(solution)/shard_map/all_to_all | solution.py:367
  65.0 0.0 collective-permute-done.9.received_ref
  65.0 0.1 collective-permute-start.10
  65.1 3.3 %collective-permute-done.10.received_ref = f32[16,256]{1,0:T(8,128)S(1)} collective-permute-done((f32[16,256]{1,0:T(8,128)S(1)}, f32[16,256]{1,0:T(8,128)S(1)}, u32[]{:S(2)}, u32[]{:S(2)}) %collective-permute-start.10) | collective-permute-done | bytes 16416 | tf_op jit(solution)/shard_map/ppermute | solution.py:325
  68.4 0.0 collective-permute-start.11
  68.4 1.2 %collective-permute-done.11.refs_2_ = f32[8,256]{1,0:T(8,128)S(1)} collective-permute-done((f32[8,256]{1,0:T(8,128)S(1)}, f32[8,256]{1,0:T(8,128)S(1)}, u32[]{:S(2)}, u32[]{:S(2)}) %collective-permute-start.11) | collective-permute-done | bytes 8224 | tf_op jit(solution)/shard_map/ppermute | solution.py:325
  69.6 1.8 %all-to-all-done.3.refs_0_ = bf16[16,8,256]{2,1,0:T(8,128)(2,1)S(1)} async-done(((bf16[16,8,256]{2,1,0:T(8,128)(2,1)}), bf16[16,8,256]{2,1,0:T(8,128)(2,1)S(1)}, u32[]{:S(2)}, u32[]{:S(2)}) %all-to-all-start.3) | async-done | bytes 65568 | tf_op jit(solution)/shard_map/all_to_all | solution.py:367
  71.4 0.2 last_step.1
  71.6 16.5 %all_to_all.31 = f32[128,1,128]{2,1,0:T(1,128)S(1)} all-to-all(f32[128,1,128]{2,1,0:T(1,128)S(1)} %bitcast.15), channel_id=1, replica_groups=mesh['row'=8,'col'=16] {'row','col'}, dimensions={0} | all-to-all | bytes 131072 | tf_op jit(solution)/shard_map/all_to_all | solution.py:377
  88.1 0.9 %finish.1 = (f32[2,2048]{1,0:T(2,128)}, f32[1,1]{1,0:T(1,128)}) custom-call(f32[128,128]{1,0:T(8,128)S(1)} %bitcast.16, f32[2,8,256]{2,1,0:T(8,128)S(1)} %get-tuple-element.53.new_ref, s32[1,2048]{1,0:T(1,128)S(1)} %bitcast.19), custom_call_target="tpu_custom_call" | custom-call | flops 1100000000 | tf_op jit(solution)/shard_map/finish/pallas_call | solution.py:303
  (9 shorter events, 0.1 us)
Async XLA Ops:
  0.6 10.9 %copy-start.5 = (s32[128,2]{0,1:T(2,128)S(1)}, s32[128,2]{0,1:T(2,128)}, u32[]{:S(2)}) copy-start(s32[128,2]{0,1:T(2,128)} %param.13) | copy-start | bytes 3076
  0.6 12.5 %copy-start.1 = (f32[3,2048]{1,0:T(4,128)S(1)}, f32[3,2048]{1,0:T(4,128)}, u32[]{:S(2)}) copy-start(f32[3,2048]{1,0:T(4,128)} %friction_ref.1) | copy-start | bytes 73732
  0.7 12.5 %copy-start.2 = (f32[2,2048]{1,0:T(2,128)S(1)}, f32[2,2048]{1,0:T(2,128)}, u32[]{:S(2)}) copy-start(f32[2,2048]{1,0:T(2,128)} %state_ref.3) | copy-start | bytes 49156
  0.7 12.5 %copy-start.3 = (s32[2048]{0:T(1024)S(1)}, s32[2048]{0:T(1024)}, u32[]{:S(2)}) copy-start(s32[2048]{0:T(1024)} %param.15) | copy-start | bytes 24580
  0.7 12.5 %copy-start.4 = (s32[128]{0:T(128)S(1)}, s32[128]{0:T(128)}, u32[]{:S(2)}) copy-start(s32[128]{0:T(128)} %param.14) | copy-start | bytes 1540
  1.7 12.1 %copy-start = (bf16[8,256,256]{2,1,0:T(8,128)(2,1)S(1)}, bf16[8,256,256]{2,1,0:T(8,128)(2,1)}, u32[]{:S(2)}) copy-start(bf16[8,256,256]{2,1,0:T(8,128)(2,1)} %near.7) | copy-start | bytes 3145732
  1.7 9.9 %collective-permute-start = (f32[8,256]{1,0:T(8,128)S(1)}, f32[8,256]{1,0:T(8,128)S(1)}, u32[]{:S(2)}, u32[]{:S(2)}) collective-permute-start(f32[8,256]{1,0:T(8,128)S(1)} %first_deficit.1.held_ref.own_ref), channel_id=1, source_target_pairs={{0,16},{16,0},{32,48},{48,32},{64,80},{80,64},{96,112},{112,96},{1... | collective-permute-start | bytes 24584 | tf_op jit(solution)/shard_map/ppermute | solution.py:325
  3.8 14.2 %all-to-all-start = ((bf16[16,8,256]{2,1,0:T(8,128)(2,1)}), bf16[16,8,256]{2,1,0:T(8,128)(2,1)S(1)}, u32[]{:S(2)}, u32[]{:S(2)}) async-start(bf16[16,8,256]{2,1,0:T(8,128)(2,1)} %spread.2), calls=%async_computation | async-start | bytes 131072 | tf_op jit(solution)/shard_map/all_to_all | solution.py:352
  11.6 3.5 %collective-permute-start.1 = (f32[16,256]{1,0:T(8,128)S(1)}, f32[16,256]{1,0:T(8,128)S(1)}, u32[]{:S(2)}, u32[]{:S(2)}) collective-permute-start(f32[16,256]{1,0:T(8,128)S(1)} %join.4.held_ref._.two_ref), channel_id=1, source_target_pairs={{0,48},{16,32},{32,16},{48,0},{64,112},{80,96},{96,80},{112,64},{1... | collective-permute-start | bytes 49160 | tf_op jit(solution)/shard_map/ppermute | solution.py:325
  15.1 11.0 %collective-permute-start.2 = (f32[32,256]{1,0:T(8,128)S(1)}, f32[32,256]{1,0:T(8,128)S(1)}, u32[]{:S(2)}, u32[]{:S(2)}) collective-permute-start(f32[32,256]{1,0:T(8,128)S(1)} %join.5.line_ref), channel_id=1, source_target_pairs={{0,112},{16,96},{32,80},{48,64},{64,48},{80,32},{96,16},{112,0},{1... | collective-permute-start | bytes 98312 | tf_op jit(solution)/shard_map/ppermute | solution.py:325
  22.0 10.4 %collective-permute-start.3 = (f32[32,256]{1,0:T(8,128)S(1)}, f32[32,256]{1,0:T(8,128)S(1)}, u32[]{:S(2)}, u32[]{:S(2)}) collective-permute-start(f32[32,256]{1,0:T(8,128)S(1)} %get-tuple-element.36), channel_id=1, source_target_pairs={{0,112},{16,96},{32,80},{48,64},{64,48},{80,32},{96,16},{112,0},{1... | collective-permute-start | bytes 98312 | tf_op jit(solution)/shard_map/ppermute | solution.py:325
  28.9 10.3 %all-to-all-start.1 = ((bf16[16,8,256]{2,1,0:T(8,128)(2,1)}), bf16[16,8,256]{2,1,0:T(8,128)(2,1)S(1)}, u32[]{:S(2)}, u32[]{:S(2)}) async-start(bf16[16,8,256]{2,1,0:T(8,128)(2,1)} %bitcast.5), calls=%async_computation.1 | async-start | bytes 131072 | tf_op jit(solution)/shard_map/all_to_all | solution.py:367
  32.4 3.4 %collective-permute-start.4 = (f32[16,256]{1,0:T(8,128)S(1)}, f32[16,256]{1,0:T(8,128)S(1)}, u32[]{:S(2)}, u32[]{:S(2)}) collective-permute-start(f32[16,256]{1,0:T(8,128)S(1)} %get-tuple-element.38), channel_id=1, source_target_pairs={{0,48},{16,32},{32,16},{48,0},{64,112},{80,96},{96,80},{112,64},{1... | collective-permute-start | bytes 49160 | tf_op jit(solution)/shard_map/ppermute | solution.py:325
  35.8 1.2 %collective-permute-start.5 = (f32[8,256]{1,0:T(8,128)S(1)}, f32[8,256]{1,0:T(8,128)S(1)}, u32[]{:S(2)}, u32[]{:S(2)}) collective-permute-start(f32[8,256]{1,0:T(8,128)S(1)} %get-tuple-element.40), channel_id=1, source_target_pairs={{0,16},{16,0},{32,48},{48,32},{64,80},{80,64},{96,112},{112,96},{1... | collective-permute-start | bytes 24584 | tf_op jit(solution)/shard_map/ppermute | solution.py:325
  39.2 5.4 %collective-permute-start.6 = (f32[8,256]{1,0:T(8,128)S(1)}, f32[8,256]{1,0:T(8,128)S(1)}, u32[]{:S(2)}, u32[]{:S(2)}) collective-permute-start(f32[8,256]{1,0:T(8,128)S(1)} %get-tuple-element.42.held_ref.own_ref), channel_id=1, source_target_pairs={{0,16},{16,0},{32,48},{48,32},{64,80},{80,64},{96,112},{112,96},{1... | collective-permute-start | bytes 24584 | tf_op jit(solution)/shard_map/ppermute | solution.py:325
  40.6 10.5 %all-to-all-start.2 = ((bf16[16,8,256]{2,1,0:T(8,128)(2,1)}), bf16[16,8,256]{2,1,0:T(8,128)(2,1)S(1)}, u32[]{:S(2)}, u32[]{:S(2)}) async-start(bf16[16,8,256]{2,1,0:T(8,128)(2,1)} %spread.3), calls=%async_computation.2 | async-start | bytes 131072 | tf_op jit(solution)/shard_map/all_to_all | solution.py:352
  44.7 3.6 %collective-permute-start.7 = (f32[16,256]{1,0:T(8,128)S(1)}, f32[16,256]{1,0:T(8,128)S(1)}, u32[]{:S(2)}, u32[]{:S(2)}) collective-permute-start(f32[16,256]{1,0:T(8,128)S(1)} %join.6.held_ref.two_ref), channel_id=1, source_target_pairs={{0,48},{16,32},{32,16},{48,0},{64,112},{80,96},{96,80},{112,64},{1... | collective-permute-start | bytes 49160 | tf_op jit(solution)/shard_map/ppermute | solution.py:325
  48.3 10.5 %collective-permute-start.8 = (f32[32,256]{1,0:T(8,128)S(1)}, f32[32,256]{1,0:T(8,128)S(1)}, u32[]{:S(2)}, u32[]{:S(2)}) collective-permute-start(f32[32,256]{1,0:T(8,128)S(1)} %join.7.line_ref), channel_id=1, source_target_pairs={{0,112},{16,96},{32,80},{48,64},{64,48},{80,32},{96,16},{112,0},{1... | collective-permute-start | bytes 98312 | tf_op jit(solution)/shard_map/ppermute | solution.py:325
  54.7 10.3 %collective-permute-start.9 = (f32[32,256]{1,0:T(8,128)S(1)}, f32[32,256]{1,0:T(8,128)S(1)}, u32[]{:S(2)}, u32[]{:S(2)}) collective-permute-start(f32[32,256]{1,0:T(8,128)S(1)} %get-tuple-element.46), channel_id=1, source_target_pairs={{0,112},{16,96},{32,80},{48,64},{64,48},{80,32},{96,16},{112,0},{1... | collective-permute-start | bytes 98312 | tf_op jit(solution)/shard_map/ppermute | solution.py:325
  61.4 10.0 %all-to-all-start.3 = ((bf16[16,8,256]{2,1,0:T(8,128)(2,1)}), bf16[16,8,256]{2,1,0:T(8,128)(2,1)S(1)}, u32[]{:S(2)}, u32[]{:S(2)}) async-start(bf16[16,8,256]{2,1,0:T(8,128)(2,1)} %bitcast.7), calls=%async_computation.3 | async-start | bytes 131072 | tf_op jit(solution)/shard_map/all_to_all | solution.py:367
  65.0 3.4 %collective-permute-start.10 = (f32[16,256]{1,0:T(8,128)S(1)}, f32[16,256]{1,0:T(8,128)S(1)}, u32[]{:S(2)}, u32[]{:S(2)}) collective-permute-start(f32[16,256]{1,0:T(8,128)S(1)} %get-tuple-element.48), channel_id=1, source_target_pairs={{0,48},{16,32},{32,16},{48,0},{64,112},{80,96},{96,80},{112,64},{1... | collective-permute-start | bytes 49160 | tf_op jit(solution)/shard_map/ppermute | solution.py:325
  68.4 1.2 %collective-permute-start.11 = (f32[8,256]{1,0:T(8,128)S(1)}, f32[8,256]{1,0:T(8,128)S(1)}, u32[]{:S(2)}, u32[]{:S(2)}) collective-permute-start(f32[8,256]{1,0:T(8,128)S(1)} %get-tuple-element.50), channel_id=1, source_target_pairs={{0,16},{16,0},{32,48},{48,32},{64,80},{80,64},{96,112},{112,96},{1... | collective-permute-start | bytes 24584 | tf_op jit(solution)/shard_map/ppermute | solution.py:325

commit v6 on v5

--- a/solution.py
+++ b/solution.py
@@ -177,7 +177,7 @@
     rows = (left_head.shape[0] + left.shape[0]) // info_ref.shape[1] * PAIRS
     terms = pair_terms(col_ref[:, 1:2], col_ref[:, 2:3], line, lambda k: part_of(k, rows, right_head, right),
                        lambda k: part_of(k, rows, left_head, left))
-    first_ref[...] = sums_at(info_ref, 0, first_ref.shape[0], terms).astype(bf16)
+    first_ref[...] = sums_at(info_ref, 0, first_ref.shape[0], terms)
 
 
 def sums_at(info_ref, side, rows, terms):
@@ -259,7 +259,7 @@
 
 def total_stress(refs):
     from_first_ref, kept_ref, received_ref = refs
-    parts = [from_first_ref[k].astype(f32) for k in range(from_first_ref.shape[0])]
+    parts = [from_first_ref[k] for k in range(from_first_ref.shape[0])]
     while len(parts) > 1:
         parts = [parts[k] + parts[k + 1] for k in range(0, len(parts), 2)]
     return parts[0] + (kept_ref[...] + received_ref[...])
@@ -361,9 +361,9 @@
             kept, sent, *factors = call(
                 functools.partial(terms_to_second_again, chunk), [block_of(4, f32)] * 2 + loaded,
                 [everyone, *near_term, info, info_col, *heads, left, right], 5, scratch, (left, right))
-        first = call(terms_to_first, block_of(columns, bf16), [four, more, info, info_col, *heads, *factors], 2.5)
-        for blocks, hop in ((2, HOPS[2]), (1, HOPS[1])):
-            kept, sent = call(add, [block_of(blocks, f32)] * 2, [kept, swap(sent, "row", hop)], 0.1)
+        first = call(terms_to_first, block_of(columns, f32), [four, more, info, info_col, *heads, *factors], 2.5)
+        for blocks, hop, cost in ((2, HOPS[2], 1.0), (1, HOPS[1], 0.1)):
+            kept, sent = call(add, [block_of(blocks, f32)] * 2, [kept, swap(sent, "row", hop)], cost)
         from_first = lax.all_to_all(first.reshape(columns, own_count, cluster), "col", 0, 0)
         return [from_first, kept, swap(sent, "row", HOPS[0])], prepared, heads
 

time: 89.5 us -> 89.6 us (level)
  waiting for transfers between devices: 17.4 us -> 18.7 us
    all_to_all x2, waiting for transfers between devices: 4.01 us -> 5.32 us  [exchange(): lax.all_to_all(first.reshape(columns, own_count, cluster), 'col', 0, 0)]
where the time goes in v6:
time: 89.6 us; the launch traced here: 89.1 us
  starting transfers between devices  35.9 us (40%)
  waiting for transfers between devices  18.7 us (21%)
  Pallas kernels  17.6 us (20%)
  blocking collectives  15.8 us (18%)
    ppermute x12, starting transfers between devices, swap(): return lax.ppermute(x, axis, [(r, r ^ distance) for r in range(size)])  17.7 us
    pallas_call x23, Pallas kernels, call(): pl.pallas_call(kernel, out_shape=out_shape, in_specs=[pl.BlockSpec(memory...  17.6 us
    all_to_all x1, blocking collectives, shards(): everywhere = lax.all_to_all(squares, ('row', 'col'), 0, 0, tiled=True)  15.8 us
    ppermute x12, waiting for transfers between devices, swap(): return lax.ppermute(x, axis, [(r, r ^ distance) for r in range(size)])  12.6 us
    all_to_all x2, starting transfers between devices, exchange(): everyone = lax.all_to_all(copies, 'col', 0, 0).reshape(span, cluster)  11.2 us
    all_to_all x2, starting transfers between devices, exchange(): lax.all_to_all(first.reshape(columns, own_count, cluster), 'col', 0, 0)  7.02 us
    all_to_all x2, waiting for transfers between devices, exchange(): lax.all_to_all(first.reshape(columns, own_count, cluster), 'col', 0, 0)  5.32 us
  transfers between devices with their start and end apart: 16, of which 10 were waited for; matrix products, arithmetic and copies ran while one was open for 0% of the time, Pallas kernels for 17%

profile of v6, /device:TPU:1, one launch (start us, length us, event | category | flops | bytes accessed | tf_op | source)
XLA Modules:
  0.0 89.1 jit_solution(8015073552984818221)
XLA Ops:
  0.6 0.0 copy-start.5
  0.6 0.0 copy-start.1
  0.7 0.0 copy-start.2
  0.7 0.0 copy-start.3
  0.7 0.0 copy-start.4
  0.7 1.0 %first_deficit.1.held_ref.own_ref = f32[8,256]{1,0:T(8,128)S(1)} custom-call(f32[2,2048]{1,0:T(2,128)} %state_ref.3, s32[1,2048]{1,0:T(1,128)} %bitcast.17), custom_call_target="tpu_custom_call" | custom-call | flops 6600000000 | tf_op jit(solution)/shard_map/first_deficit/pallas_call | solution.py:303
  1.7 0.0 copy-start
  1.7 1.5 %collective-permute-start = (f32[8,256]{1,0:T(8,128)S(1)}, f32[8,256]{1,0:T(8,128)S(1)}, u32[]{:S(2)}, u32[]{:S(2)}) collective-permute-start(f32[8,256]{1,0:T(8,128)S(1)} %first_deficit.1.held_ref.own_ref), channel_id=1, source_target_pairs={{0,16},{16,0},{32,48},{48,32},{64,80},{80,64},{96,112},{112,96},{1... | collective-permute-start | bytes 24584 | tf_op jit(solution)/shard_map/ppermute | solution.py:325
  3.2 0.6 spread.2
  3.8 7.7 %all-to-all-start = ((bf16[16,8,256]{2,1,0:T(8,128)(2,1)}), bf16[16,8,256]{2,1,0:T(8,128)(2,1)S(1)}, u32[]{:S(2)}, u32[]{:S(2)}) async-start(bf16[16,8,256]{2,1,0:T(8,128)(2,1)} %spread.2), calls=%async_computation | async-start | bytes 131072 | tf_op jit(solution)/shard_map/all_to_all | solution.py:352
  11.5 0.0 copy-done.5
  11.5 0.1 copy.11.pairs_ref
  11.6 0.0 collective-permute-done.received_ref
  11.6 1.6 %collective-permute-start.1 = (f32[16,256]{1,0:T(8,128)S(1)}, f32[16,256]{1,0:T(8,128)S(1)}, u32[]{:S(2)}, u32[]{:S(2)}) collective-permute-start(f32[16,256]{1,0:T(8,128)S(1)} %join.4.held_ref._.two_ref), channel_id=1, source_target_pairs={{0,48},{16,32},{32,16},{48,0},{64,112},{80,96},{96,80},{112,64},{1... | collective-permute-start | bytes 49160 | tf_op jit(solution)/shard_map/ppermute | solution.py:325
  13.2 0.0 copy-done.1
  13.2 0.0 copy-done.2
  13.2 0.0 copy-done.3
  13.2 0.0 copy-done.4
  13.2 0.5 prepare.1
  13.7 0.0 copy-done
  13.7 0.2 near_terms.4.near_0
  13.9 0.2 near_terms.5.near_1
  14.1 1.0 %collective-permute-done.1.received_ref = f32[16,256]{1,0:T(8,128)S(1)} collective-permute-done((f32[16,256]{1,0:T(8,128)S(1)}, f32[16,256]{1,0:T(8,128)S(1)}, u32[]{:S(2)}, u32[]{:S(2)}) %collective-permute-start.1) | collective-permute-done | bytes 16416 | tf_op jit(solution)/shard_map/ppermute | solution.py:325
  15.1 2.6 %collective-permute-start.2 = (f32[32,256]{1,0:T(8,128)S(1)}, f32[32,256]{1,0:T(8,128)S(1)}, u32[]{:S(2)}, u32[]{:S(2)}) collective-permute-start(f32[32,256]{1,0:T(8,128)S(1)} %join.5.line_ref), channel_id=1, source_target_pairs={{0,112},{16,96},{32,80},{48,64},{64,48},{80,32},{96,16},{112,0},{1... | collective-permute-start | bytes 98312 | tf_op jit(solution)/shard_map/ppermute | solution.py:325
  17.8 0.2 all-to-all-done
  18.0 4.0 %terms_to_second.1 = (f32[32,256]{1,0:T(8,128)S(1)}, f32[32,256]{1,0:T(8,128)S(1)}, bf16[2048,256]{1,0:T(8,128)(2,1)S(1)}, bf16[2048,256]{1,0:T(8,128)(2,1)S(1)}...) custom-call(bf16[128,256]{1,0:T(8,128)(2,1)S(1)} %bitcast.13, f32[4,256]{1,0:T(4,128)S(1)} %near_terms.4.near_0, ...), custom_call_target="tpu_custom_call" | custom-call | flops 5500000256 | tf_op jit(solution)/shard_map/terms_to_second/pallas_call | solution.py:303
  22.0 4.1 %collective-permute-start.3 = (f32[32,256]{1,0:T(8,128)S(1)}, f32[32,256]{1,0:T(8,128)S(1)}, u32[]{:S(2)}, u32[]{:S(2)}) collective-permute-start(f32[32,256]{1,0:T(8,128)S(1)} %get-tuple-element.36), channel_id=1, source_target_pairs={{0,112},{16,96},{32,80},{48,64},{64,48},{80,32},{96,16},{112,0},{1... | collective-permute-start | bytes 98312 | tf_op jit(solution)/shard_map/ppermute | solution.py:325
  26.2 0.0 collective-permute-done.2.more_ref
  26.2 2.7 %terms_to_first.2 = f32[128,256]{1,0:T(8,128)} custom-call(f32[32,256]{1,0:T(8,128)S(1)} %join.5.line_ref, f32[32,256]{1,0:T(8,128)S(1)} %collective-permute-done.2.more_ref, s32[8,128]{1,0:T(8,128)S(1)} %get-tuple-element.29.info.info_ref, s32[128,128]{1,0:T(8,128)S(1)} %get-tuple-element.30.col.col_ref, bf16[2048,256]{1,0:T(8,128)(2,1)S(1)} %get-tuple-element.31.left_head, ...), custom_call_target="tpu_custom_call" | custom-call | flops 2750000128 | tf_op jit(solution)/shard_map/terms_to_first/pallas_call | solution.py:303
  28.9 3.5 %all-to-all-start.1 = ((f32[16,8,256]{2,1,0:T(8,128)}), f32[16,8,256]{2,1,0:T(8,128)S(1)}, u32[]{:S(2)}, u32[]{:S(2)}) async-start(f32[16,8,256]{2,1,0:T(8,128)} %bitcast.5), calls=%async_computation.1 | async-start | bytes 262144 | tf_op jit(solution)/shard_map/all_to_all | solution.py:367
  32.4 0.0 collective-permute-done.3.received_ref
  32.5 0.1 collective-permute-start.4
  32.5 3.2 %collective-permute-done.4.received_ref = f32[16,256]{1,0:T(8,128)S(1)} collective-permute-done((f32[16,256]{1,0:T(8,128)S(1)}, f32[16,256]{1,0:T(8,128)S(1)}, u32[]{:S(2)}, u32[]{:S(2)}) %collective-permute-start.4) | collective-permute-done | bytes 16416 | tf_op jit(solution)/shard_map/ppermute | solution.py:325
  35.7 0.0 collective-permute-start.5
  35.7 1.2 %collective-permute-done.5.refs_2_ = f32[8,256]{1,0:T(8,128)S(1)} collective-permute-done((f32[8,256]{1,0:T(8,128)S(1)}, f32[8,256]{1,0:T(8,128)S(1)}, u32[]{:S(2)}, u32[]{:S(2)}) %collective-permute-start.5) | collective-permute-done | bytes 8224 | tf_op jit(solution)/shard_map/ppermute | solution.py:325
  36.9 2.9 %all-to-all-done.1.refs_0_ = f32[16,8,256]{2,1,0:T(8,128)S(1)} async-done(((f32[16,8,256]{2,1,0:T(8,128)}), f32[16,8,256]{2,1,0:T(8,128)S(1)}, u32[]{:S(2)}, u32[]{:S(2)}) %all-to-all-start.1) | async-done | bytes 131104 | tf_op jit(solution)/shard_map/all_to_all | solution.py:367
  39.8 0.9 %collective-permute-start.6 = (f32[8,256]{1,0:T(8,128)S(1)}, f32[8,256]{1,0:T(8,128)S(1)}, u32[]{:S(2)}, u32[]{:S(2)}) collective-permute-start(f32[8,256]{1,0:T(8,128)S(1)} %get-tuple-element.42.held_ref.own_ref), channel_id=1, source_target_pairs={{0,16},{16,0},{32,48},{48,32},{64,80},{80,64},{96,112},{112,96},{1... | collective-permute-start | bytes 24584 | tf_op jit(solution)/shard_map/ppermute | solution.py:325
  40.7 0.6 spread.3
  41.4 3.5 %all-to-all-start.2 = ((bf16[16,8,256]{2,1,0:T(8,128)(2,1)}), bf16[16,8,256]{2,1,0:T(8,128)(2,1)S(1)}, u32[]{:S(2)}, u32[]{:S(2)}) async-start(bf16[16,8,256]{2,1,0:T(8,128)(2,1)} %spread.3), calls=%async_computation.2 | async-start | bytes 131072 | tf_op jit(solution)/shard_map/all_to_all | solution.py:352
  44.9 0.0 collective-permute-done.6.received_ref
  44.9 0.3 collective-permute-start.7
  45.1 0.2 near_terms.6.near_0
  45.3 0.2 near_terms.7.near_1
  45.5 2.7 %collective-permute-done.7.received_ref = f32[16,256]{1,0:T(8,128)S(1)} collective-permute-done((f32[16,256]{1,0:T(8,128)S(1)}, f32[16,256]{1,0:T(8,128)S(1)}, u32[]{:S(2)}, u32[]{:S(2)}) %collective-permute-start.7) | collective-permute-done | bytes 16416 | tf_op jit(solution)/shard_map/ppermute | solution.py:325
  48.2 2.6 %collective-permute-start.8 = (f32[32,256]{1,0:T(8,128)S(1)}, f32[32,256]{1,0:T(8,128)S(1)}, u32[]{:S(2)}, u32[]{:S(2)}) collective-permute-start(f32[32,256]{1,0:T(8,128)S(1)} %join.7.line_ref), channel_id=1, source_target_pairs={{0,112},{16,96},{32,80},{48,64},{64,48},{80,32},{96,16},{112,0},{1... | collective-permute-start | bytes 98312 | tf_op jit(solution)/shard_map/ppermute | solution.py:325
  50.7 0.6 all-to-all-done.2
  51.3 3.5 %terms_to_second_again.1 = (f32[32,256]{1,0:T(8,128)S(1)}, f32[32,256]{1,0:T(8,128)S(1)}, bf16[6144,256]{1,0:T(8,128)(2,1)S(1)}, bf16[6144,256]{1,0:T(8,128)(2,1)S(1)}) custom-call(bf16[128,256]{1,0:T(8,128)(2,1)S(1)} %bitcast.14, f32[4,256]{1,0:T(4,128)S(1)} %near_terms.6.near_0, f32[4,256]{1,0:T(4,128)S(1)} %near_terms.7.near_1, ...), custom_call_target="tpu_custom_call" | custom-call | flops 5500000256 | tf_op jit(solution)/shard_map/terms_to_second_again/pallas_call | solution.py:303
  54.8 3.9 %collective-permute-start.9 = (f32[32,256]{1,0:T(8,128)S(1)}, f32[32,256]{1,0:T(8,128)S(1)}, u32[]{:S(2)}, u32[]{:S(2)}) collective-permute-start(f32[32,256]{1,0:T(8,128)S(1)} %get-tuple-element.46), channel_id=1, source_target_pairs={{0,112},{16,96},{32,80},{48,64},{64,48},{80,32},{96,16},{112,0},{1... | collective-permute-start | bytes 98312 | tf_op jit(solution)/shard_map/ppermute | solution.py:325
  58.7 0.0 collective-permute-done.8.more_ref
  58.8 2.7 %terms_to_first.3 = f32[128,256]{1,0:T(8,128)} custom-call(f32[32,256]{1,0:T(8,128)S(1)} %join.7.line_ref, f32[32,256]{1,0:T(8,128)S(1)} %collective-permute-done.8.more_ref, s32[8,128]{1,0:T(8,128)S(1)} %get-tuple-element.29.info.info_ref, s32[128,128]{1,0:T(8,128)S(1)} %get-tuple-element.30.col.col_ref, bf16[2048,256]{1,0:T(8,128)(2,1)S(1)} %get-tuple-element.31.left_head, ...), custom_call_target="tpu_custom_call" | custom-call | flops 2750000128 | tf_op jit(solution)/shard_map/terms_to_first/pallas_call | solution.py:303
  61.5 3.5 %all-to-all-start.3 = ((f32[16,8,256]{2,1,0:T(8,128)}), f32[16,8,256]{2,1,0:T(8,128)S(1)}, u32[]{:S(2)}, u32[]{:S(2)}) async-start(f32[16,8,256]{2,1,0:T(8,128)} %bitcast.7), calls=%async_computation.3 | async-start | bytes 262144 | tf_op jit(solution)/shard_map/all_to_all | solution.py:367
  65.0 0.0 collective-permute-done.9.received_ref
  65.0 0.1 collective-permute-start.10
  65.1 3.4 %collective-permute-done.10.received_ref = f32[16,256]{1,0:T(8,128)S(1)} collective-permute-done((f32[16,256]{1,0:T(8,128)S(1)}, f32[16,256]{1,0:T(8,128)S(1)}, u32[]{:S(2)}, u32[]{:S(2)}) %collective-permute-start.10) | collective-permute-done | bytes 16416 | tf_op jit(solution)/shard_map/ppermute | solution.py:325
  68.6 0.0 collective-permute-start.11
  68.6 1.2 %collective-permute-done.11.refs_2_ = f32[8,256]{1,0:T(8,128)S(1)} collective-permute-done((f32[8,256]{1,0:T(8,128)S(1)}, f32[8,256]{1,0:T(8,128)S(1)}, u32[]{:S(2)}, u32[]{:S(2)}) %collective-permute-start.11) | collective-permute-done | bytes 8224 | tf_op jit(solution)/shard_map/ppermute | solution.py:325
  69.7 2.4 %all-to-all-done.3.refs_0_ = f32[16,8,256]{2,1,0:T(8,128)S(1)} async-done(((f32[16,8,256]{2,1,0:T(8,128)}), f32[16,8,256]{2,1,0:T(8,128)S(1)}, u32[]{:S(2)}, u32[]{:S(2)}) %all-to-all-start.3) | async-done | bytes 131104 | tf_op jit(solution)/shard_map/all_to_all | solution.py:367
  72.2 0.2 last_step.1
  72.3 15.8 %all_to_all.31 = f32[128,1,128]{2,1,0:T(1,128)S(1)} all-to-all(f32[128,1,128]{2,1,0:T(1,128)S(1)} %bitcast.15), channel_id=1, replica_groups=mesh['row'=8,'col'=16] {'row','col'}, dimensions={0} | all-to-all | bytes 131072 | tf_op jit(solution)/shard_map/all_to_all | solution.py:377
  88.2 0.9 %finish.1 = (f32[2,2048]{1,0:T(2,128)}, f32[1,1]{1,0:T(1,128)}) custom-call(f32[128,128]{1,0:T(8,128)S(1)} %bitcast.16, f32[2,8,256]{2,1,0:T(8,128)S(1)} %get-tuple-element.53.new_ref, s32[1,2048]{1,0:T(1,128)S(1)} %bitcast.19), custom_call_target="tpu_custom_call" | custom-call | flops 1100000000 | tf_op jit(solution)/shard_map/finish/pallas_call | solution.py:303
  (9 shorter events, 0.1 us)
Async XLA Ops:
  0.6 10.9 %copy-start.5 = (s32[128,2]{0,1:T(2,128)S(1)}, s32[128,2]{0,1:T(2,128)}, u32[]{:S(2)}) copy-start(s32[128,2]{0,1:T(2,128)} %param.13) | copy-start | bytes 3076
  0.6 12.5 %copy-start.1 = (f32[3,2048]{1,0:T(4,128)S(1)}, f32[3,2048]{1,0:T(4,128)}, u32[]{:S(2)}) copy-start(f32[3,2048]{1,0:T(4,128)} %friction_ref.1) | copy-start | bytes 73732
  0.7 12.5 %copy-start.2 = (f32[2,2048]{1,0:T(2,128)S(1)}, f32[2,2048]{1,0:T(2,128)}, u32[]{:S(2)}) copy-start(f32[2,2048]{1,0:T(2,128)} %state_ref.3) | copy-start | bytes 49156
  0.7 12.5 %copy-start.3 = (s32[2048]{0:T(1024)S(1)}, s32[2048]{0:T(1024)}, u32[]{:S(2)}) copy-start(s32[2048]{0:T(1024)} %param.15) | copy-start | bytes 24580
  0.7 12.5 %copy-start.4 = (s32[128]{0:T(128)S(1)}, s32[128]{0:T(128)}, u32[]{:S(2)}) copy-start(s32[128]{0:T(128)} %param.14) | copy-start | bytes 1540
  1.7 12.1 %copy-start = (bf16[8,256,256]{2,1,0:T(8,128)(2,1)S(1)}, bf16[8,256,256]{2,1,0:T(8,128)(2,1)}, u32[]{:S(2)}) copy-start(bf16[8,256,256]{2,1,0:T(8,128)(2,1)} %near.7) | copy-start | bytes 3145732
  1.7 9.9 %collective-permute-start = (f32[8,256]{1,0:T(8,128)S(1)}, f32[8,256]{1,0:T(8,128)S(1)}, u32[]{:S(2)}, u32[]{:S(2)}) collective-permute-start(f32[8,256]{1,0:T(8,128)S(1)} %first_deficit.1.held_ref.own_ref), channel_id=1, source_target_pairs={{0,16},{16,0},{32,48},{48,32},{64,80},{80,64},{96,112},{112,96},{1... | collective-permute-start | bytes 24584 | tf_op jit(solution)/shard_map/ppermute | solution.py:325
  3.8 14.2 %all-to-all-start = ((bf16[16,8,256]{2,1,0:T(8,128)(2,1)}), bf16[16,8,256]{2,1,0:T(8,128)(2,1)S(1)}, u32[]{:S(2)}, u32[]{:S(2)}) async-start(bf16[16,8,256]{2,1,0:T(8,128)(2,1)} %spread.2), calls=%async_computation | async-start | bytes 131072 | tf_op jit(solution)/shard_map/all_to_all | solution.py:352
  11.6 3.5 %collective-permute-start.1 = (f32[16,256]{1,0:T(8,128)S(1)}, f32[16,256]{1,0:T(8,128)S(1)}, u32[]{:S(2)}, u32[]{:S(2)}) collective-permute-start(f32[16,256]{1,0:T(8,128)S(1)} %join.4.held_ref._.two_ref), channel_id=1, source_target_pairs={{0,48},{16,32},{32,16},{48,0},{64,112},{80,96},{96,80},{112,64},{1... | collective-permute-start | bytes 49160 | tf_op jit(solution)/shard_map/ppermute | solution.py:325
  15.1 11.0 %collective-permute-start.2 = (f32[32,256]{1,0:T(8,128)S(1)}, f32[32,256]{1,0:T(8,128)S(1)}, u32[]{:S(2)}, u32[]{:S(2)}) collective-permute-start(f32[32,256]{1,0:T(8,128)S(1)} %join.5.line_ref), channel_id=1, source_target_pairs={{0,112},{16,96},{32,80},{48,64},{64,48},{80,32},{96,16},{112,0},{1... | collective-permute-start | bytes 98312 | tf_op jit(solution)/shard_map/ppermute | solution.py:325
  22.0 10.4 %collective-permute-start.3 = (f32[32,256]{1,0:T(8,128)S(1)}, f32[32,256]{1,0:T(8,128)S(1)}, u32[]{:S(2)}, u32[]{:S(2)}) collective-permute-start(f32[32,256]{1,0:T(8,128)S(1)} %get-tuple-element.36), channel_id=1, source_target_pairs={{0,112},{16,96},{32,80},{48,64},{64,48},{80,32},{96,16},{112,0},{1... | collective-permute-start | bytes 98312 | tf_op jit(solution)/shard_map/ppermute | solution.py:325
  28.9 10.9 %all-to-all-start.1 = ((f32[16,8,256]{2,1,0:T(8,128)}), f32[16,8,256]{2,1,0:T(8,128)S(1)}, u32[]{:S(2)}, u32[]{:S(2)}) async-start(f32[16,8,256]{2,1,0:T(8,128)} %bitcast.5), calls=%async_computation.1 | async-start | bytes 262144 | tf_op jit(solution)/shard_map/all_to_all | solution.py:367
  32.5 3.2 %collective-permute-start.4 = (f32[16,256]{1,0:T(8,128)S(1)}, f32[16,256]{1,0:T(8,128)S(1)}, u32[]{:S(2)}, u32[]{:S(2)}) collective-permute-start(f32[16,256]{1,0:T(8,128)S(1)} %get-tuple-element.38), channel_id=1, source_target_pairs={{0,48},{16,32},{32,16},{48,0},{64,112},{80,96},{96,80},{112,64},{1... | collective-permute-start | bytes 49160 | tf_op jit(solution)/shard_map/ppermute | solution.py:325
  35.7 1.2 %collective-permute-start.5 = (f32[8,256]{1,0:T(8,128)S(1)}, f32[8,256]{1,0:T(8,128)S(1)}, u32[]{:S(2)}, u32[]{:S(2)}) collective-permute-start(f32[8,256]{1,0:T(8,128)S(1)} %get-tuple-element.40), channel_id=1, source_target_pairs={{0,16},{16,0},{32,48},{48,32},{64,80},{80,64},{96,112},{112,96},{1... | collective-permute-start | bytes 24584 | tf_op jit(solution)/shard_map/ppermute | solution.py:325
  39.8 5.1 %collective-permute-start.6 = (f32[8,256]{1,0:T(8,128)S(1)}, f32[8,256]{1,0:T(8,128)S(1)}, u32[]{:S(2)}, u32[]{:S(2)}) collective-permute-start(f32[8,256]{1,0:T(8,128)S(1)} %get-tuple-element.42.held_ref.own_ref), channel_id=1, source_target_pairs={{0,16},{16,0},{32,48},{48,32},{64,80},{80,64},{96,112},{112,96},{1... | collective-permute-start | bytes 24584 | tf_op jit(solution)/shard_map/ppermute | solution.py:325
  41.4 10.0 %all-to-all-start.2 = ((bf16[16,8,256]{2,1,0:T(8,128)(2,1)}), bf16[16,8,256]{2,1,0:T(8,128)(2,1)S(1)}, u32[]{:S(2)}, u32[]{:S(2)}) async-start(bf16[16,8,256]{2,1,0:T(8,128)(2,1)} %spread.3), calls=%async_computation.2 | async-start | bytes 131072 | tf_op jit(solution)/shard_map/all_to_all | solution.py:352
  44.9 3.3 %collective-permute-start.7 = (f32[16,256]{1,0:T(8,128)S(1)}, f32[16,256]{1,0:T(8,128)S(1)}, u32[]{:S(2)}, u32[]{:S(2)}) collective-permute-start(f32[16,256]{1,0:T(8,128)S(1)} %join.6.held_ref.two_ref), channel_id=1, source_target_pairs={{0,48},{16,32},{32,16},{48,0},{64,112},{80,96},{96,80},{112,64},{1... | collective-permute-start | bytes 49160 | tf_op jit(solution)/shard_map/ppermute | solution.py:325
  48.2 10.6 %collective-permute-start.8 = (f32[32,256]{1,0:T(8,128)S(1)}, f32[32,256]{1,0:T(8,128)S(1)}, u32[]{:S(2)}, u32[]{:S(2)}) collective-permute-start(f32[32,256]{1,0:T(8,128)S(1)} %join.7.line_ref), channel_id=1, source_target_pairs={{0,112},{16,96},{32,80},{48,64},{64,48},{80,32},{96,16},{112,0},{1... | collective-permute-start | bytes 98312 | tf_op jit(solution)/shard_map/ppermute | solution.py:325
  54.8 10.2 %collective-permute-start.9 = (f32[32,256]{1,0:T(8,128)S(1)}, f32[32,256]{1,0:T(8,128)S(1)}, u32[]{:S(2)}, u32[]{:S(2)}) collective-permute-start(f32[32,256]{1,0:T(8,128)S(1)} %get-tuple-element.46), channel_id=1, source_target_pairs={{0,112},{16,96},{32,80},{48,64},{64,48},{80,32},{96,16},{112,0},{1... | collective-permute-start | bytes 98312 | tf_op jit(solution)/shard_map/ppermute | solution.py:325
  61.5 10.7 %all-to-all-start.3 = ((f32[16,8,256]{2,1,0:T(8,128)}), f32[16,8,256]{2,1,0:T(8,128)S(1)}, u32[]{:S(2)}, u32[]{:S(2)}) async-start(f32[16,8,256]{2,1,0:T(8,128)} %bitcast.7), calls=%async_computation.3 | async-start | bytes 262144 | tf_op jit(solution)/shard_map/all_to_all | solution.py:367
  65.0 3.5 %collective-permute-start.10 = (f32[16,256]{1,0:T(8,128)S(1)}, f32[16,256]{1,0:T(8,128)S(1)}, u32[]{:S(2)}, u32[]{:S(2)}) collective-permute-start(f32[16,256]{1,0:T(8,128)S(1)} %get-tuple-element.48), channel_id=1, source_target_pairs={{0,48},{16,32},{32,16},{48,0},{64,112},{80,96},{96,80},{112,64},{1... | collective-permute-start | bytes 49160 | tf_op jit(solution)/shard_map/ppermute | solution.py:325
  68.6 1.2 %collective-permute-start.11 = (f32[8,256]{1,0:T(8,128)S(1)}, f32[8,256]{1,0:T(8,128)S(1)}, u32[]{:S(2)}, u32[]{:S(2)}) collective-permute-start(f32[8,256]{1,0:T(8,128)S(1)} %get-tuple-element.50), channel_id=1, source_target_pairs={{0,16},{16,0},{32,48},{48,32},{64,80},{80,64},{96,112},{112,96},{1... | collective-permute-start | bytes 24584 | tf_op jit(solution)/shard_map/ppermute | solution.py:325

commit v7 on v6

--- a/solution.py
+++ b/solution.py
@@ -112,17 +112,17 @@
     return mxu(hot, values).astype(bf16)
 
 
-def pair_terms(at, ranks, values, taken, given):
+def pair_terms(at, ranks, values, product, given):
     x = picked(at, values)
     groups = at.shape[0] // PAIRS
     coefs = []
     for k in range(groups):
-        factor = taken(k)
-        shape = (PAIRS, factor.shape[0])
+        rows = slice(k * PAIRS, (k + 1) * PAIRS)
+        coef = product(x[rows], k)
+        shape = coef.shape
         rank = lax.broadcasted_iota(jnp.int32, shape, 1) - shape[1] // PAIRS * lax.broadcasted_iota(jnp.int32, shape, 0)
-        rows = slice(k * PAIRS, (k + 1) * PAIRS)
         within = (rank >= 0) & (rank < ranks[rows])
-        coefs.append(jnp.where(within, mxu_nt(x[rows], factor), 0.0).astype(bf16))
+        coefs.append(jnp.where(within, coef, 0.0).astype(bf16))
     return jnp.concatenate([mxu(coefs[k], given(k)) for k in range(groups)], axis=0)
 
 
@@ -132,7 +132,7 @@
 
 
 def second_sums(chunk, everyone_ref, near_0_ref, near_1_ref, info_ref, col_ref, sources, heads, tails, sem, load_heads,
-                kept_ref, sent_ref):
+                kept_ref, sent_ref, right_t):
     pairs = info_ref.shape[1]
     rows = (heads[0].shape[0] + tails[0].shape[0]) // pairs * PAIRS
     fetched = []
@@ -153,7 +153,14 @@
             return part_of(k, rows, head, tail)
 
         fetched.append(group)
-    terms = pair_terms(col_ref[:, 0:1], col_ref[:, 2:3], everyone_ref[...], *fetched)
+    left_rows, right_rows = fetched
+
+    def transposing(k):
+        right = right_rows(k)
+        right_t[:, pl.ds(k * rows, rows)] = jnp.transpose(right)
+        return right
+
+    terms = pair_terms(col_ref[:, 0:1], col_ref[:, 2:3], everyone_ref[...], lambda x, k: mxu_nt(x, left_rows(k)), transposing)
     halves(sums_at(info_ref, 1, 2 * kept_ref.shape[0], terms), kept_ref, sent_ref)
     half = near_0_ref.shape[0]
     kept_ref[0:half, :] += near_0_ref[...]
@@ -161,21 +168,21 @@
 
 
 def terms_to_second(chunk, everyone, near_0, near_1, info, col, left_hbm, right_hbm, kept, sent, left_head, right_head,
-                    left, right, sem):
+                    left, right_t, right, sem):
     second_sums(chunk, everyone, near_0, near_1, info, col, (left_hbm, right_hbm), (left_head, right_head), (left, right),
-                sem, True, kept, sent)
+                sem, True, kept, sent, right_t)
 
 
 def terms_to_second_again(chunk, everyone, near_0, near_1, info, col, left_head, right_head, left_hbm, right_hbm, kept, sent,
-                          left, right, sem):
+                          left, right_t, right, sem):
     second_sums(chunk, everyone, near_0, near_1, info, col, (left_hbm, right_hbm), (left_head, right_head), (left, right),
-                sem, False, kept, sent)
-
-
-def terms_to_first(line_ref, more_ref, info_ref, col_ref, left_head, right_head, left, right, first_ref):
+                sem, False, kept, sent, right_t)
+
+
+def terms_to_first(line_ref, more_ref, info_ref, col_ref, left_head, left, right_t, first_ref):
     line = jnp.concatenate([line_ref[...], more_ref[...]], axis=0).astype(bf16)
-    rows = (left_head.shape[0] + left.shape[0]) // info_ref.shape[1] * PAIRS
-    terms = pair_terms(col_ref[:, 1:2], col_ref[:, 2:3], line, lambda k: part_of(k, rows, right_head, right),
+    rows = right_t.shape[1] // info_ref.shape[1] * PAIRS
+    terms = pair_terms(col_ref[:, 1:2], col_ref[:, 2:3], line, lambda x, k: mxu(x, right_t[:, pl.ds(k * rows, rows)]),
                        lambda k: part_of(k, rows, left_head, left))
     first_ref[...] = sums_at(info_ref, 0, first_ref.shape[0], terms)
 
@@ -334,9 +341,9 @@
 
     chunk, head = 2048, HEAD
     tail = count * width - head
-    scratch = [pltpu.SemaphoreType.DMA((2, tail // chunk + 1))]
+    scratch = [pltpu.VMEM((tail, cluster), bf16), pltpu.SemaphoreType.DMA((2, tail // chunk + 1))]
     kept_there = [pltpu.VMEM((head, cluster), bf16)] * 2
-    loaded = [pltpu.VMEM((tail, cluster), bf16)] * 2
+    loaded = [pltpu.VMEM((tail, cluster), bf16), pltpu.VMEM((cluster, count * width), bf16)]
 
     def exchange(own, prepared=None, heads=None):
         copies = call(spread, sds((columns, own_count, cluster), bf16), [own], 0.6)
@@ -361,7 +368,7 @@
             kept, sent, *factors = call(
                 functools.partial(terms_to_second_again, chunk), [block_of(4, f32)] * 2 + loaded,
                 [everyone, *near_term, info, info_col, *heads, left, right], 5, scratch, (left, right))
-        first = call(terms_to_first, block_of(columns, f32), [four, more, info, info_col, *heads, *factors], 2.5)
+        first = call(terms_to_first, block_of(columns, f32), [four, more, info, info_col, heads[0], *factors], 2.5)
         for blocks, hop, cost in ((2, HOPS[2], 1.0), (1, HOPS[1], 0.1)):
             kept, sent = call(add, [block_of(blocks, f32)] * 2, [kept, swap(sent, "row", hop)], cost)
         from_first = lax.all_to_all(first.reshape(columns, own_count, cluster), "col", 0, 0)

time: 89.6 us -> 89.1 us (level)
  no operation moved by 1% of the time
where the time goes in v7:
time: 89.1 us; the launch traced here: 88.6 us
  starting transfers between devices  35.9 us (40%)
  waiting for transfers between devices  18.7 us (21%)
  Pallas kernels  17.2 us (19%)
  blocking collectives  15.8 us (18%)
    ppermute x12, starting transfers between devices, swap(): return lax.ppermute(x, axis, [(r, r ^ distance) for r in range(size)])  17.7 us
    pallas_call x23, Pallas kernels, call(): pl.pallas_call(kernel, out_shape=out_shape, in_specs=[pl.BlockSpec(memory...  17.2 us
    all_to_all x1, blocking collectives, shards(): everywhere = lax.all_to_all(squares, ('row', 'col'), 0, 0, tiled=True)  15.8 us
    ppermute x12, waiting for transfers between devices, swap(): return lax.ppermute(x, axis, [(r, r ^ distance) for r in range(size)])  12.6 us
    all_to_all x2, starting transfers between devices, exchange(): everyone = lax.all_to_all(copies, 'col', 0, 0).reshape(span, cluster)  11.2 us
    all_to_all x2, starting transfers between devices, exchange(): lax.all_to_all(first.reshape(columns, own_count, cluster), 'col', 0, 0)  7.02 us
    all_to_all x2, waiting for transfers between devices, exchange(): lax.all_to_all(first.reshape(columns, own_count, cluster), 'col', 0, 0)  5.32 us
  transfers between devices with their start and end apart: 16, of which 10 were waited for; matrix products, arithmetic and copies ran while one was open for 0% of the time, Pallas kernels for 17%

profile of v7, /device:TPU:1, one launch (start us, length us, event | category | flops | bytes accessed | tf_op | source)
XLA Modules:
  0.0 88.6 jit_solution(438651236604462848)
XLA Ops:
  0.6 0.0 copy-start.5
  0.6 0.0 copy-start.1
  0.7 0.0 copy-start.2
  0.7 0.0 copy-start.3
  0.7 0.0 copy-start.4
  0.7 1.0 %first_deficit.1.held_ref.own_ref = f32[8,256]{1,0:T(8,128)S(1)} custom-call(f32[2,2048]{1,0:T(2,128)} %state_ref.3, s32[1,2048]{1,0:T(1,128)} %bitcast.17), custom_call_target="tpu_custom_call" | custom-call | flops 6600000000 | tf_op jit(solution)/shard_map/first_deficit/pallas_call | solution.py:310
  1.7 0.0 copy-start
  1.7 1.5 %collective-permute-start = (f32[8,256]{1,0:T(8,128)S(1)}, f32[8,256]{1,0:T(8,128)S(1)}, u32[]{:S(2)}, u32[]{:S(2)}) collective-permute-start(f32[8,256]{1,0:T(8,128)S(1)} %first_deficit.1.held_ref.own_ref), channel_id=1, source_target_pairs={{0,16},{16,0},{32,48},{48,32},{64,80},{80,64},{96,112},{112,96},{1... | collective-permute-start | bytes 24584 | tf_op jit(solution)/shard_map/ppermute | solution.py:332
  3.2 0.6 spread.2
  3.8 7.7 %all-to-all-start = ((bf16[16,8,256]{2,1,0:T(8,128)(2,1)}), bf16[16,8,256]{2,1,0:T(8,128)(2,1)S(1)}, u32[]{:S(2)}, u32[]{:S(2)}) async-start(bf16[16,8,256]{2,1,0:T(8,128)(2,1)} %spread.2), calls=%async_computation | async-start | bytes 131072 | tf_op jit(solution)/shard_map/all_to_all | solution.py:359
  11.5 0.0 copy-done.5
  11.5 0.1 copy.11.pairs_ref
  11.6 0.0 collective-permute-done.received_ref
  11.6 1.6 %collective-permute-start.1 = (f32[16,256]{1,0:T(8,128)S(1)}, f32[16,256]{1,0:T(8,128)S(1)}, u32[]{:S(2)}, u32[]{:S(2)}) collective-permute-start(f32[16,256]{1,0:T(8,128)S(1)} %join.4.held_ref._.two_ref), channel_id=1, source_target_pairs={{0,48},{16,32},{32,16},{48,0},{64,112},{80,96},{96,80},{112,64},{1... | collective-permute-start | bytes 49160 | tf_op jit(solution)/shard_map/ppermute | solution.py:332
  13.2 0.0 copy-done.1
  13.2 0.0 copy-done.2
  13.2 0.0 copy-done.3
  13.2 0.0 copy-done.4
  13.2 0.5 prepare.1
  13.7 0.0 copy-done
  13.7 0.2 near_terms.4.near_0
  13.9 0.2 near_terms.5.near_1
  14.1 1.0 %collective-permute-done.1.received_ref = f32[16,256]{1,0:T(8,128)S(1)} collective-permute-done((f32[16,256]{1,0:T(8,128)S(1)}, f32[16,256]{1,0:T(8,128)S(1)}, u32[]{:S(2)}, u32[]{:S(2)}) %collective-permute-start.1) | collective-permute-done | bytes 16416 | tf_op jit(solution)/shard_map/ppermute | solution.py:332
  15.1 2.6 %collective-permute-start.2 = (f32[32,256]{1,0:T(8,128)S(1)}, f32[32,256]{1,0:T(8,128)S(1)}, u32[]{:S(2)}, u32[]{:S(2)}) collective-permute-start(f32[32,256]{1,0:T(8,128)S(1)} %join.5.line_ref), channel_id=1, source_target_pairs={{0,112},{16,96},{32,80},{48,64},{64,48},{80,32},{96,16},{112,0},{1... | collective-permute-start | bytes 98312 | tf_op jit(solution)/shard_map/ppermute | solution.py:332
  17.8 0.2 all-to-all-done
  18.0 4.3 %terms_to_second.1 = (f32[32,256]{1,0:T(8,128)S(1)}, f32[32,256]{1,0:T(8,128)S(1)}, bf16[2048,256]{1,0:T(8,128)(2,1)S(1)}, bf16[2048,256]{1,0:T(8,128)(2,1)S(1)}...) custom-call(bf16[128,256]{1,0:T(8,128)(2,1)S(1)} %bitcast.13, f32[4,256]{1,0:T(4,128)S(1)} %near_terms.4.near_0, ...), custom_call_target="tpu_custom_call" | custom-call | flops 5500000256 | tf_op jit(solution)/shard_map/terms_to_second/pallas_call | solution.py:310
  22.3 4.1 %collective-permute-start.3 = (f32[32,256]{1,0:T(8,128)S(1)}, f32[32,256]{1,0:T(8,128)S(1)}, u32[]{:S(2)}, u32[]{:S(2)}) collective-permute-start(f32[32,256]{1,0:T(8,128)S(1)} %get-tuple-element.35), channel_id=1, source_target_pairs={{0,112},{16,96},{32,80},{48,64},{64,48},{80,32},{96,16},{112,0},{1... | collective-permute-start | bytes 98312 | tf_op jit(solution)/shard_map/ppermute | solution.py:332
  26.5 0.0 collective-permute-done.2.more_ref
  26.5 2.2 %terms_to_first.2 = f32[128,256]{1,0:T(8,128)} custom-call(f32[32,256]{1,0:T(8,128)S(1)} %join.5.line_ref, f32[32,256]{1,0:T(8,128)S(1)} %collective-permute-done.2.more_ref, s32[8,128]{1,0:T(8,128)S(1)} %get-tuple-element.29.info.info_ref, s32[128,128]{1,0:T(8,128)S(1)} %get-tuple-element.30.col.col_ref, bf16[2048,256]{1,0:T(8,128)(2,1)S(1)} %get-tuple-element.31.left_head, ...), custom_call_target="tpu_custom_call" | custom-call | flops 2750000128 | tf_op jit(solution)/shard_map/terms_to_first/pallas_call | solution.py:310
  28.7 3.5 %all-to-all-start.1 = ((f32[16,8,256]{2,1,0:T(8,128)}), f32[16,8,256]{2,1,0:T(8,128)S(1)}, u32[]{:S(2)}, u32[]{:S(2)}) async-start(f32[16,8,256]{2,1,0:T(8,128)} %bitcast.5), calls=%async_computation.1 | async-start | bytes 262144 | tf_op jit(solution)/shard_map/all_to_all | solution.py:374
  32.2 0.0 collective-permute-done.3.received_ref
  32.2 0.1 collective-permute-start.4
  32.3 3.2 %collective-permute-done.4.received_ref = f32[16,256]{1,0:T(8,128)S(1)} collective-permute-done((f32[16,256]{1,0:T(8,128)S(1)}, f32[16,256]{1,0:T(8,128)S(1)}, u32[]{:S(2)}, u32[]{:S(2)}) %collective-permute-start.4) | collective-permute-done | bytes 16416 | tf_op jit(solution)/shard_map/ppermute | solution.py:332
  35.5 0.0 collective-permute-start.5
  35.5 1.2 %collective-permute-done.5.refs_2_ = f32[8,256]{1,0:T(8,128)S(1)} collective-permute-done((f32[8,256]{1,0:T(8,128)S(1)}, f32[8,256]{1,0:T(8,128)S(1)}, u32[]{:S(2)}, u32[]{:S(2)}) %collective-permute-start.5) | collective-permute-done | bytes 8224 | tf_op jit(solution)/shard_map/ppermute | solution.py:332
  36.7 2.9 %all-to-all-done.1.refs_0_ = f32[16,8,256]{2,1,0:T(8,128)S(1)} async-done(((f32[16,8,256]{2,1,0:T(8,128)}), f32[16,8,256]{2,1,0:T(8,128)S(1)}, u32[]{:S(2)}, u32[]{:S(2)}) %all-to-all-start.1) | async-done | bytes 131104 | tf_op jit(solution)/shard_map/all_to_all | solution.py:374
  39.6 0.9 %collective-permute-start.6 = (f32[8,256]{1,0:T(8,128)S(1)}, f32[8,256]{1,0:T(8,128)S(1)}, u32[]{:S(2)}, u32[]{:S(2)}) collective-permute-start(f32[8,256]{1,0:T(8,128)S(1)} %get-tuple-element.41.held_ref.own_ref), channel_id=1, source_target_pairs={{0,16},{16,0},{32,48},{48,32},{64,80},{80,64},{96,112},{112,96},{1... | collective-permute-start | bytes 24584 | tf_op jit(solution)/shard_map/ppermute | solution.py:332
  40.5 0.6 spread.3
  41.2 3.5 %all-to-all-start.2 = ((bf16[16,8,256]{2,1,0:T(8,128)(2,1)}), bf16[16,8,256]{2,1,0:T(8,128)(2,1)S(1)}, u32[]{:S(2)}, u32[]{:S(2)}) async-start(bf16[16,8,256]{2,1,0:T(8,128)(2,1)} %spread.3), calls=%async_computation.2 | async-start | bytes 131072 | tf_op jit(solution)/shard_map/all_to_all | solution.py:359
  44.7 0.0 collective-permute-done.6.received_ref
  44.7 0.3 collective-permute-start.7
  44.9 0.2 near_terms.6.near_0
  45.1 0.2 near_terms.7.near_1
  45.3 2.7 %collective-permute-done.7.received_ref = f32[16,256]{1,0:T(8,128)S(1)} collective-permute-done((f32[16,256]{1,0:T(8,128)S(1)}, f32[16,256]{1,0:T(8,128)S(1)}, u32[]{:S(2)}, u32[]{:S(2)}) %collective-permute-start.7) | collective-permute-done | bytes 16416 | tf_op jit(solution)/shard_map/ppermute | solution.py:332
  48.0 2.6 %collective-permute-start.8 = (f32[32,256]{1,0:T(8,128)S(1)}, f32[32,256]{1,0:T(8,128)S(1)}, u32[]{:S(2)}, u32[]{:S(2)}) collective-permute-start(f32[32,256]{1,0:T(8,128)S(1)} %join.7.line_ref), channel_id=1, source_target_pairs={{0,112},{16,96},{32,80},{48,64},{64,48},{80,32},{96,16},{112,0},{1... | collective-permute-start | bytes 98312 | tf_op jit(solution)/shard_map/ppermute | solution.py:332
  50.5 0.6 all-to-all-done.2
  51.1 3.7 %terms_to_second_again.1 = (f32[32,256]{1,0:T(8,128)S(1)}, f32[32,256]{1,0:T(8,128)S(1)}, bf16[6144,256]{1,0:T(8,128)(2,1)S(1)}, bf16[256,8192]{1,0:T(8,128)(2,1)S(1)}) custom-call(bf16[128,256]{1,0:T(8,128)(2,1)S(1)} %bitcast.14, f32[4,256]{1,0:T(4,128)S(1)} %near_terms.6.near_0, f32[4,256]{1,0:T(4,128)S(1)} %near_terms.7.near_1, ...), custom_call_target="tpu_custom_call" | custom-call | flops 5500000256 | tf_op jit(solution)/shard_map/terms_to_second_again/pallas_call | solution.py:310
  54.9 3.9 %collective-permute-start.9 = (f32[32,256]{1,0:T(8,128)S(1)}, f32[32,256]{1,0:T(8,128)S(1)}, u32[]{:S(2)}, u32[]{:S(2)}) collective-permute-start(f32[32,256]{1,0:T(8,128)S(1)} %get-tuple-element.46), channel_id=1, source_target_pairs={{0,112},{16,96},{32,80},{48,64},{64,48},{80,32},{96,16},{112,0},{1... | collective-permute-start | bytes 98312 | tf_op jit(solution)/shard_map/ppermute | solution.py:332
  58.8 0.0 collective-permute-done.8.more_ref
  58.8 2.2 %terms_to_first.3 = f32[128,256]{1,0:T(8,128)} custom-call(f32[32,256]{1,0:T(8,128)S(1)} %join.7.line_ref, f32[32,256]{1,0:T(8,128)S(1)} %collective-permute-done.8.more_ref, s32[8,128]{1,0:T(8,128)S(1)} %get-tuple-element.29.info.info_ref, s32[128,128]{1,0:T(8,128)S(1)} %get-tuple-element.30.col.col_ref, bf16[2048,256]{1,0:T(8,128)(2,1)S(1)} %get-tuple-element.31.left_head, ...), custom_call_target="tpu_custom_call" | custom-call | flops 2750000128 | tf_op jit(solution)/shard_map/terms_to_first/pallas_call | solution.py:310
  61.0 3.5 %all-to-all-start.3 = ((f32[16,8,256]{2,1,0:T(8,128)}), f32[16,8,256]{2,1,0:T(8,128)S(1)}, u32[]{:S(2)}, u32[]{:S(2)}) async-start(f32[16,8,256]{2,1,0:T(8,128)} %bitcast.7), calls=%async_computation.3 | async-start | bytes 262144 | tf_op jit(solution)/shard_map/all_to_all | solution.py:374
  64.5 0.0 collective-permute-done.9.received_ref
  64.5 0.1 collective-permute-start.10
  64.6 3.4 %collective-permute-done.10.received_ref = f32[16,256]{1,0:T(8,128)S(1)} collective-permute-done((f32[16,256]{1,0:T(8,128)S(1)}, f32[16,256]{1,0:T(8,128)S(1)}, u32[]{:S(2)}, u32[]{:S(2)}) %collective-permute-start.10) | collective-permute-done | bytes 16416 | tf_op jit(solution)/shard_map/ppermute | solution.py:332
  68.1 0.0 collective-permute-start.11
  68.1 1.2 %collective-permute-done.11.refs_2_ = f32[8,256]{1,0:T(8,128)S(1)} collective-permute-done((f32[8,256]{1,0:T(8,128)S(1)}, f32[8,256]{1,0:T(8,128)S(1)}, u32[]{:S(2)}, u32[]{:S(2)}) %collective-permute-start.11) | collective-permute-done | bytes 8224 | tf_op jit(solution)/shard_map/ppermute | solution.py:332
  69.3 2.4 %all-to-all-done.3.refs_0_ = f32[16,8,256]{2,1,0:T(8,128)S(1)} async-done(((f32[16,8,256]{2,1,0:T(8,128)}), f32[16,8,256]{2,1,0:T(8,128)S(1)}, u32[]{:S(2)}, u32[]{:S(2)}) %all-to-all-start.3) | async-done | bytes 131104 | tf_op jit(solution)/shard_map/all_to_all | solution.py:374
  71.7 0.2 last_step.1
  71.9 15.8 %all_to_all.31 = f32[128,1,128]{2,1,0:T(1,128)S(1)} all-to-all(f32[128,1,128]{2,1,0:T(1,128)S(1)} %bitcast.15), channel_id=1, replica_groups=mesh['row'=8,'col'=16] {'row','col'}, dimensions={0} | all-to-all | bytes 131072 | tf_op jit(solution)/shard_map/all_to_all | solution.py:384
  87.7 0.9 %finish.1 = (f32[2,2048]{1,0:T(2,128)}, f32[1,1]{1,0:T(1,128)}) custom-call(f32[128,128]{1,0:T(8,128)S(1)} %bitcast.16, f32[2,8,256]{2,1,0:T(8,128)S(1)} %get-tuple-element.53.new_ref, s32[1,2048]{1,0:T(1,128)S(1)} %bitcast.19), custom_call_target="tpu_custom_call" | custom-call | flops 1100000000 | tf_op jit(solution)/shard_map/finish/pallas_call | solution.py:310
  (9 shorter events, 0.1 us)
Async XLA Ops:
  0.6 10.9 %copy-start.5 = (s32[128,2]{0,1:T(2,128)S(1)}, s32[128,2]{0,1:T(2,128)}, u32[]{:S(2)}) copy-start(s32[128,2]{0,1:T(2,128)} %param.13) | copy-start | bytes 3076
  0.6 12.5 %copy-start.1 = (f32[3,2048]{1,0:T(4,128)S(1)}, f32[3,2048]{1,0:T(4,128)}, u32[]{:S(2)}) copy-start(f32[3,2048]{1,0:T(4,128)} %friction_ref.1) | copy-start | bytes 73732
  0.7 12.5 %copy-start.2 = (f32[2,2048]{1,0:T(2,128)S(1)}, f32[2,2048]{1,0:T(2,128)}, u32[]{:S(2)}) copy-start(f32[2,2048]{1,0:T(2,128)} %state_ref.3) | copy-start | bytes 49156
  0.7 12.5 %copy-start.3 = (s32[2048]{0:T(1024)S(1)}, s32[2048]{0:T(1024)}, u32[]{:S(2)}) copy-start(s32[2048]{0:T(1024)} %param.15) | copy-start | bytes 24580
  0.7 12.5 %copy-start.4 = (s32[128]{0:T(128)S(1)}, s32[128]{0:T(128)}, u32[]{:S(2)}) copy-start(s32[128]{0:T(128)} %param.14) | copy-start | bytes 1540
  1.7 12.1 %copy-start = (bf16[8,256,256]{2,1,0:T(8,128)(2,1)S(1)}, bf16[8,256,256]{2,1,0:T(8,128)(2,1)}, u32[]{:S(2)}) copy-start(bf16[8,256,256]{2,1,0:T(8,128)(2,1)} %near.7) | copy-start | bytes 3145732
  1.7 9.9 %collective-permute-start = (f32[8,256]{1,0:T(8,128)S(1)}, f32[8,256]{1,0:T(8,128)S(1)}, u32[]{:S(2)}, u32[]{:S(2)}) collective-permute-start(f32[8,256]{1,0:T(8,128)S(1)} %first_deficit.1.held_ref.own_ref), channel_id=1, source_target_pairs={{0,16},{16,0},{32,48},{48,32},{64,80},{80,64},{96,112},{112,96},{1... | collective-permute-start | bytes 24584 | tf_op jit(solution)/shard_map/ppermute | solution.py:332
  3.8 14.2 %all-to-all-start = ((bf16[16,8,256]{2,1,0:T(8,128)(2,1)}), bf16[16,8,256]{2,1,0:T(8,128)(2,1)S(1)}, u32[]{:S(2)}, u32[]{:S(2)}) async-start(bf16[16,8,256]{2,1,0:T(8,128)(2,1)} %spread.2), calls=%async_computation | async-start | bytes 131072 | tf_op jit(solution)/shard_map/all_to_all | solution.py:359
  11.6 3.5 %collective-permute-start.1 = (f32[16,256]{1,0:T(8,128)S(1)}, f32[16,256]{1,0:T(8,128)S(1)}, u32[]{:S(2)}, u32[]{:S(2)}) collective-permute-start(f32[16,256]{1,0:T(8,128)S(1)} %join.4.held_ref._.two_ref), channel_id=1, source_target_pairs={{0,48},{16,32},{32,16},{48,0},{64,112},{80,96},{96,80},{112,64},{1... | collective-permute-start | bytes 49160 | tf_op jit(solution)/shard_map/ppermute | solution.py:332
  15.1 11.3 %collective-permute-start.2 = (f32[32,256]{1,0:T(8,128)S(1)}, f32[32,256]{1,0:T(8,128)S(1)}, u32[]{:S(2)}, u32[]{:S(2)}) collective-permute-start(f32[32,256]{1,0:T(8,128)S(1)} %join.5.line_ref), channel_id=1, source_target_pairs={{0,112},{16,96},{32,80},{48,64},{64,48},{80,32},{96,16},{112,0},{1... | collective-permute-start | bytes 98312 | tf_op jit(solution)/shard_map/ppermute | solution.py:332
  22.3 9.9 %collective-permute-start.3 = (f32[32,256]{1,0:T(8,128)S(1)}, f32[32,256]{1,0:T(8,128)S(1)}, u32[]{:S(2)}, u32[]{:S(2)}) collective-permute-start(f32[32,256]{1,0:T(8,128)S(1)} %get-tuple-element.35), channel_id=1, source_target_pairs={{0,112},{16,96},{32,80},{48,64},{64,48},{80,32},{96,16},{112,0},{1... | collective-permute-start | bytes 98312 | tf_op jit(solution)/shard_map/ppermute | solution.py:332
  28.7 10.9 %all-to-all-start.1 = ((f32[16,8,256]{2,1,0:T(8,128)}), f32[16,8,256]{2,1,0:T(8,128)S(1)}, u32[]{:S(2)}, u32[]{:S(2)}) async-start(f32[16,8,256]{2,1,0:T(8,128)} %bitcast.5), calls=%async_computation.1 | async-start | bytes 262144 | tf_op jit(solution)/shard_map/all_to_all | solution.py:374
  32.2 3.2 %collective-permute-start.4 = (f32[16,256]{1,0:T(8,128)S(1)}, f32[16,256]{1,0:T(8,128)S(1)}, u32[]{:S(2)}, u32[]{:S(2)}) collective-permute-start(f32[16,256]{1,0:T(8,128)S(1)} %get-tuple-element.37), channel_id=1, source_target_pairs={{0,48},{16,32},{32,16},{48,0},{64,112},{80,96},{96,80},{112,64},{1... | collective-permute-start | bytes 49160 | tf_op jit(solution)/shard_map/ppermute | solution.py:332
  35.5 1.2 %collective-permute-start.5 = (f32[8,256]{1,0:T(8,128)S(1)}, f32[8,256]{1,0:T(8,128)S(1)}, u32[]{:S(2)}, u32[]{:S(2)}) collective-permute-start(f32[8,256]{1,0:T(8,128)S(1)} %get-tuple-element.39), channel_id=1, source_target_pairs={{0,16},{16,0},{32,48},{48,32},{64,80},{80,64},{96,112},{112,96},{1... | collective-permute-start | bytes 24584 | tf_op jit(solution)/shard_map/ppermute | solution.py:332
  39.6 5.1 %collective-permute-start.6 = (f32[8,256]{1,0:T(8,128)S(1)}, f32[8,256]{1,0:T(8,128)S(1)}, u32[]{:S(2)}, u32[]{:S(2)}) collective-permute-start(f32[8,256]{1,0:T(8,128)S(1)} %get-tuple-element.41.held_ref.own_ref), channel_id=1, source_target_pairs={{0,16},{16,0},{32,48},{48,32},{64,80},{80,64},{96,112},{112,96},{1... | collective-permute-start | bytes 24584 | tf_op jit(solution)/shard_map/ppermute | solution.py:332
  41.2 10.0 %all-to-all-start.2 = ((bf16[16,8,256]{2,1,0:T(8,128)(2,1)}), bf16[16,8,256]{2,1,0:T(8,128)(2,1)S(1)}, u32[]{:S(2)}, u32[]{:S(2)}) async-start(bf16[16,8,256]{2,1,0:T(8,128)(2,1)} %spread.3), calls=%async_computation.2 | async-start | bytes 131072 | tf_op jit(solution)/shard_map/all_to_all | solution.py:359
  44.7 3.3 %collective-permute-start.7 = (f32[16,256]{1,0:T(8,128)S(1)}, f32[16,256]{1,0:T(8,128)S(1)}, u32[]{:S(2)}, u32[]{:S(2)}) collective-permute-start(f32[16,256]{1,0:T(8,128)S(1)} %join.6.held_ref.two_ref), channel_id=1, source_target_pairs={{0,48},{16,32},{32,16},{48,0},{64,112},{80,96},{96,80},{112,64},{1... | collective-permute-start | bytes 49160 | tf_op jit(solution)/shard_map/ppermute | solution.py:332
  48.0 10.8 %collective-permute-start.8 = (f32[32,256]{1,0:T(8,128)S(1)}, f32[32,256]{1,0:T(8,128)S(1)}, u32[]{:S(2)}, u32[]{:S(2)}) collective-permute-start(f32[32,256]{1,0:T(8,128)S(1)} %join.7.line_ref), channel_id=1, source_target_pairs={{0,112},{16,96},{32,80},{48,64},{64,48},{80,32},{96,16},{112,0},{1... | collective-permute-start | bytes 98312 | tf_op jit(solution)/shard_map/ppermute | solution.py:332
  54.9 9.7 %collective-permute-start.9 = (f32[32,256]{1,0:T(8,128)S(1)}, f32[32,256]{1,0:T(8,128)S(1)}, u32[]{:S(2)}, u32[]{:S(2)}) collective-permute-start(f32[32,256]{1,0:T(8,128)S(1)} %get-tuple-element.46), channel_id=1, source_target_pairs={{0,112},{16,96},{32,80},{48,64},{64,48},{80,32},{96,16},{112,0},{1... | collective-permute-start | bytes 98312 | tf_op jit(solution)/shard_map/ppermute | solution.py:332
  61.0 10.7 %all-to-all-start.3 = ((f32[16,8,256]{2,1,0:T(8,128)}), f32[16,8,256]{2,1,0:T(8,128)S(1)}, u32[]{:S(2)}, u32[]{:S(2)}) async-start(f32[16,8,256]{2,1,0:T(8,128)} %bitcast.7), calls=%async_computation.3 | async-start | bytes 262144 | tf_op jit(solution)/shard_map/all_to_all | solution.py:374
  64.5 3.5 %collective-permute-start.10 = (f32[16,256]{1,0:T(8,128)S(1)}, f32[16,256]{1,0:T(8,128)S(1)}, u32[]{:S(2)}, u32[]{:S(2)}) collective-permute-start(f32[16,256]{1,0:T(8,128)S(1)} %get-tuple-element.48), channel_id=1, source_target_pairs={{0,48},{16,32},{32,16},{48,0},{64,112},{80,96},{96,80},{112,64},{1... | collective-permute-start | bytes 49160 | tf_op jit(solution)/shard_map/ppermute | solution.py:332
  68.1 1.2 %collective-permute-start.11 = (f32[8,256]{1,0:T(8,128)S(1)}, f32[8,256]{1,0:T(8,128)S(1)}, u32[]{:S(2)}, u32[]{:S(2)}) collective-permute-start(f32[8,256]{1,0:T(8,128)S(1)} %get-tuple-element.50), channel_id=1, source_target_pairs={{0,16},{16,0},{32,48},{48,32},{64,80},{80,64},{96,112},{112,96},{1... | collective-permute-start | bytes 24584 | tf_op jit(solution)/shard_map/ppermute | solution.py:332

commit v8 on v7

--- a/solution.py
+++ b/solution.py
@@ -182,7 +182,7 @@
 def terms_to_first(line_ref, more_ref, info_ref, col_ref, left_head, left, right_t, first_ref):
     line = jnp.concatenate([line_ref[...], more_ref[...]], axis=0).astype(bf16)
     rows = right_t.shape[1] // info_ref.shape[1] * PAIRS
-    terms = pair_terms(col_ref[:, 1:2], col_ref[:, 2:3], line, lambda x, k: mxu(x, right_t[:, pl.ds(k * rows, rows)]),
+    terms = pair_terms(col_ref[:, 3:4], col_ref[:, 2:3], line, lambda x, k: mxu(x, right_t[:, pl.ds(k * rows, rows)]),
                        lambda k: part_of(k, rows, left_head, left))
     first_ref[...] = sums_at(info_ref, 0, first_ref.shape[0], terms)
 
@@ -213,13 +213,14 @@
 
 
 HOPS = (1, 3, 7)
-
-
-def place_of(difference):
+BACK = (1, 7, 3)
+
+
+def place_of(difference, hops):
     place = jnp.zeros_like(difference)
-    for k in range(2 ** len(HOPS)):
+    for k in range(2 ** len(hops)):
         reached = 0
-        for bit, hop in enumerate(HOPS):
+        for bit, hop in enumerate(hops):
             reached ^= hop * (k >> bit & 1)
         place = jnp.where(difference == reached, k, place)
     return place
@@ -232,12 +233,14 @@
     owner_row = lax.div(owner, columns)
     by_row = owner_row ^ row
     first_at = (owner - owner_row * columns) * own_count + inside
-    second_at = place_of(by_row) * own_count + inside
+    second_at = place_of(by_row, HOPS) * own_count + inside
+    second_sum_at = place_of(by_row, BACK) * own_count + inside
     count = ranks_ref.shape[1]
     sublane = lax.broadcasted_iota(jnp.int32, (count, LANES), 0)
     lane = lax.broadcasted_iota(jnp.int32, (count, LANES), 1)
     rank = jnp.sum(jnp.where(sublane == lane, jnp.broadcast_to(ranks_ref[...], (count, LANES)), 0), axis=1, keepdims=True)
-    columns_of = jnp.where(lane == 0, first_at[:, 0:1], jnp.where(lane == 1, second_at[:, 1:2], rank))
+    columns_of = jnp.where(lane == 0, first_at[:, 0:1], jnp.where(lane == 1, second_sum_at[:, 1:2], jnp.where(
+        lane == 2, rank, second_at[:, 1:2])))
     col_ref[...] = columns_of
     info_ref[...] = jnp.transpose(columns_of)[:info_ref.shape[0]]
 
@@ -339,7 +342,7 @@
     def block_of(blocks, dtype):
         return sds((blocks * own_count, cluster), dtype)
 
-    chunk, head = 2048, HEAD
+    chunk, head = 3072, HEAD
     tail = count * width - head
     scratch = [pltpu.VMEM((tail, cluster), bf16), pltpu.SemaphoreType.DMA((2, tail // chunk + 1))]
     kept_there = [pltpu.VMEM((head, cluster), bf16)] * 2
@@ -369,10 +372,10 @@
                 functools.partial(terms_to_second_again, chunk), [block_of(4, f32)] * 2 + loaded,
                 [everyone, *near_term, info, info_col, *heads, left, right], 5, scratch, (left, right))
         first = call(terms_to_first, block_of(columns, f32), [four, more, info, info_col, heads[0], *factors], 2.5)
-        for blocks, hop, cost in ((2, HOPS[2], 1.0), (1, HOPS[1], 0.1)):
+        for blocks, hop, cost in ((2, BACK[2], 1.0), (1, BACK[1], 0.1)):
             kept, sent = call(add, [block_of(blocks, f32)] * 2, [kept, swap(sent, "row", hop)], cost)
         from_first = lax.all_to_all(first.reshape(columns, own_count, cluster), "col", 0, 0)
-        return [from_first, kept, swap(sent, "row", HOPS[0])], prepared, heads
+        return [from_first, kept, swap(sent, "row", BACK[0])], prepared, heads
 
     received, prepared, heads = exchange(own)
     fields = prepared[2]

time: 89.1 us -> 88.6 us (level)
  waiting for transfers between devices: 18.7 us -> 16.1 us
  starting transfers between devices: 35.9 us -> 37.4 us
    all_to_all x2, waiting for transfers between devices: 5.32 us -> 2.38 us  [exchange(): lax.all_to_all(first.reshape(columns, own_count, cluster), 'col', 0, 0)]
    all_to_all x2, waiting for transfers between devices: 0.79 us -> 2.4 us  [exchange(): everyone = lax.all_to_all(copies, 'col', 0, 0).reshape(span, cluster)]
    ppermute x12, waiting for transfers between devices: 12.6 us -> 11.4 us  [swap(): return lax.ppermute(x, axis, [(r, r ^ distance) for r in range(size)])]
    all_to_all x2, starting transfers between devices: 11.2 us -> 12.4 us  [exchange(): everyone = lax.all_to_all(copies, 'col', 0, 0).reshape(span, cluster)]
where the time goes in v8:
time: 88.6 us; the launch traced here: 88.1 us
  starting transfers between devices  37.4 us (42%)
  Pallas kernels  17.1 us (19%)
  blocking collectives  16.5 us (19%)
  waiting for transfers between devices  16.1 us (18%)
    ppermute x12, starting transfers between devices, swap(): return lax.ppermute(x, axis, [(r, r ^ distance) for r in range(size)])  17.4 us
    pallas_call x23, Pallas kernels, call(): pl.pallas_call(kernel, out_shape=out_shape, in_specs=[pl.BlockSpec(memory...  17.1 us
    all_to_all x1, blocking collectives, shards(): everywhere = lax.all_to_all(squares, ('row', 'col'), 0, 0, tiled=True)  16.5 us
    all_to_all x2, starting transfers between devices, exchange(): everyone = lax.all_to_all(copies, 'col', 0, 0).reshape(span, cluster)  12.4 us
    ppermute x12, waiting for transfers between devices, swap(): return lax.ppermute(x, axis, [(r, r ^ distance) for r in range(size)])  11.4 us
    all_to_all x2, starting transfers between devices, exchange(): lax.all_to_all(first.reshape(columns, own_count, cluster), 'col', 0, 0)  7.69 us
    all_to_all x2, waiting for transfers between devices, exchange(): everyone = lax.all_to_all(copies, 'col', 0, 0).reshape(span, cluster)  2.4 us
    all_to_all x2, waiting for transfers between devices, exchange(): lax.all_to_all(first.reshape(columns, own_count, cluster), 'col', 0, 0)  2.38 us
  transfers between devices with their start and end apart: 16, of which 10 were waited for; matrix products, arithmetic and copies ran while one was open for 0% of the time, Pallas kernels for 17%

profile of v8, /device:TPU:1, one launch (start us, length us, event | category | flops | bytes accessed | tf_op | source)
XLA Modules:
  0.0 88.1 jit_solution(17172293673443036333)
XLA Ops:
  0.6 0.0 copy-start.5
  0.6 0.0 copy-start.1
  0.7 0.0 copy-start.2
  0.7 0.0 copy-start.3
  0.7 0.0 copy-start.4
  0.7 1.0 %first_deficit.1.held_ref.own_ref = f32[8,256]{1,0:T(8,128)S(1)} custom-call(f32[2,2048]{1,0:T(2,128)} %state_ref.3, s32[1,2048]{1,0:T(1,128)} %bitcast.17), custom_call_target="tpu_custom_call" | custom-call | flops 6600000000 | tf_op jit(solution)/shard_map/first_deficit/pallas_call | solution.py:313
  1.7 0.0 copy-start
  1.7 1.5 %collective-permute-start = (f32[8,256]{1,0:T(8,128)S(1)}, f32[8,256]{1,0:T(8,128)S(1)}, u32[]{:S(2)}, u32[]{:S(2)}) collective-permute-start(f32[8,256]{1,0:T(8,128)S(1)} %first_deficit.1.held_ref.own_ref), channel_id=1, source_target_pairs={{0,16},{16,0},{32,48},{48,32},{64,80},{80,64},{96,112},{112,96},{1... | collective-permute-start | bytes 24584 | tf_op jit(solution)/shard_map/ppermute | solution.py:335
  3.2 0.6 spread.2
  3.8 7.7 %all-to-all-start = ((bf16[16,8,256]{2,1,0:T(8,128)(2,1)}), bf16[16,8,256]{2,1,0:T(8,128)(2,1)S(1)}, u32[]{:S(2)}, u32[]{:S(2)}) async-start(bf16[16,8,256]{2,1,0:T(8,128)(2,1)} %spread.2), calls=%async_computation | async-start | bytes 131072 | tf_op jit(solution)/shard_map/all_to_all | solution.py:362
  11.5 0.0 copy-done.5
  11.5 0.1 copy.11.pairs_ref
  11.6 0.0 collective-permute-done.received_ref
  11.6 1.6 %collective-permute-start.1 = (f32[16,256]{1,0:T(8,128)S(1)}, f32[16,256]{1,0:T(8,128)S(1)}, u32[]{:S(2)}, u32[]{:S(2)}) collective-permute-start(f32[16,256]{1,0:T(8,128)S(1)} %join.4.held_ref._.two_ref), channel_id=1, source_target_pairs={{0,48},{16,32},{32,16},{48,0},{64,112},{80,96},{96,80},{112,64},{1... | collective-permute-start | bytes 49160 | tf_op jit(solution)/shard_map/ppermute | solution.py:335
  13.2 0.0 copy-done.1
  13.2 0.0 copy-done.2
  13.2 0.0 copy-done.3
  13.2 0.0 copy-done.4
  13.2 0.5 prepare.1
  13.7 0.0 copy-done
  13.7 0.2 near_terms.4.near_0
  13.9 0.2 near_terms.5.near_1
  14.1 1.0 %collective-permute-done.1.received_ref = f32[16,256]{1,0:T(8,128)S(1)} collective-permute-done((f32[16,256]{1,0:T(8,128)S(1)}, f32[16,256]{1,0:T(8,128)S(1)}, u32[]{:S(2)}, u32[]{:S(2)}) %collective-permute-start.1) | collective-permute-done | bytes 16416 | tf_op jit(solution)/shard_map/ppermute | solution.py:335
  15.1 2.6 %collective-permute-start.2 = (f32[32,256]{1,0:T(8,128)S(1)}, f32[32,256]{1,0:T(8,128)S(1)}, u32[]{:S(2)}, u32[]{:S(2)}) collective-permute-start(f32[32,256]{1,0:T(8,128)S(1)} %join.5.line_ref), channel_id=1, source_target_pairs={{0,112},{16,96},{32,80},{48,64},{64,48},{80,32},{96,16},{112,0},{1... | collective-permute-start | bytes 98312 | tf_op jit(solution)/shard_map/ppermute | solution.py:335
  17.8 0.2 all-to-all-done
  18.0 4.2 %terms_to_second.1 = (f32[32,256]{1,0:T(8,128)S(1)}, f32[32,256]{1,0:T(8,128)S(1)}, bf16[2048,256]{1,0:T(8,128)(2,1)S(1)}, bf16[2048,256]{1,0:T(8,128)(2,1)S(1)}...) custom-call(bf16[128,256]{1,0:T(8,128)(2,1)S(1)} %bitcast.13, f32[4,256]{1,0:T(4,128)S(1)} %near_terms.4.near_0, ...), custom_call_target="tpu_custom_call" | custom-call | flops 5500000256 | tf_op jit(solution)/shard_map/terms_to_second/pallas_call | solution.py:313
  22.2 2.7 %collective-permute-start.3 = (f32[32,256]{1,0:T(8,128)S(1)}, f32[32,256]{1,0:T(8,128)S(1)}, u32[]{:S(2)}, u32[]{:S(2)}) collective-permute-start(f32[32,256]{1,0:T(8,128)S(1)} %get-tuple-element.35), channel_id=1, source_target_pairs={{0,48},{16,32},{32,16},{48,0},{64,112},{80,96},{96,80},{112,64},{1... | collective-permute-start | bytes 98312 | tf_op jit(solution)/shard_map/ppermute | solution.py:335
  24.9 0.0 collective-permute-done.2.more_ref
  25.0 2.2 %terms_to_first.2 = f32[128,256]{1,0:T(8,128)} custom-call(f32[32,256]{1,0:T(8,128)S(1)} %join.5.line_ref, f32[32,256]{1,0:T(8,128)S(1)} %collective-permute-done.2.more_ref, s32[8,128]{1,0:T(8,128)S(1)} %get-tuple-element.29.info.info_ref, s32[128,128]{1,0:T(8,128)S(1)} %get-tuple-element.30.col.col_ref, bf16[2048,256]{1,0:T(8,128)(2,1)S(1)} %get-tuple-element.31.left_head, ...), custom_call_target="tpu_custom_call" | custom-call | flops 2750000128 | tf_op jit(solution)/shard_map/terms_to_first/pallas_call | solution.py:313
  27.2 4.2 %all-to-all-start.1 = ((f32[16,8,256]{2,1,0:T(8,128)}), f32[16,8,256]{2,1,0:T(8,128)S(1)}, u32[]{:S(2)}, u32[]{:S(2)}) async-start(f32[16,8,256]{2,1,0:T(8,128)} %bitcast.5), calls=%async_computation.1 | async-start | bytes 262144 | tf_op jit(solution)/shard_map/all_to_all | solution.py:377
  31.4 0.0 collective-permute-done.3.received_ref
  31.4 1.3 %collective-permute-start.4 = (f32[16,256]{1,0:T(8,128)S(1)}, f32[16,256]{1,0:T(8,128)S(1)}, u32[]{:S(2)}, u32[]{:S(2)}) collective-permute-start(f32[16,256]{1,0:T(8,128)S(1)} %get-tuple-element.37), channel_id=1, source_target_pairs={{0,112},{16,96},{32,80},{48,64},{64,48},{80,32},{96,16},{112,0},{1... | collective-permute-start | bytes 49160 | tf_op jit(solution)/shard_map/ppermute | solution.py:335
  32.7 3.3 %collective-permute-done.4.received_ref = f32[16,256]{1,0:T(8,128)S(1)} collective-permute-done((f32[16,256]{1,0:T(8,128)S(1)}, f32[16,256]{1,0:T(8,128)S(1)}, u32[]{:S(2)}, u32[]{:S(2)}) %collective-permute-start.4) | collective-permute-done | bytes 16416 | tf_op jit(solution)/shard_map/ppermute | solution.py:335
  36.0 0.4 collective-permute-start.5
  36.4 0.8 collective-permute-done.5.refs_2_
  37.2 1.0 %all-to-all-done.1.refs_0_ = f32[16,8,256]{2,1,0:T(8,128)S(1)} async-done(((f32[16,8,256]{2,1,0:T(8,128)}), f32[16,8,256]{2,1,0:T(8,128)S(1)}, u32[]{:S(2)}, u32[]{:S(2)}) %all-to-all-start.1) | async-done | bytes 131104 | tf_op jit(solution)/shard_map/all_to_all | solution.py:377
  38.2 1.7 %collective-permute-start.6 = (f32[8,256]{1,0:T(8,128)S(1)}, f32[8,256]{1,0:T(8,128)S(1)}, u32[]{:S(2)}, u32[]{:S(2)}) collective-permute-start(f32[8,256]{1,0:T(8,128)S(1)} %get-tuple-element.41.held_ref.own_ref), channel_id=1, source_target_pairs={{0,16},{16,0},{32,48},{48,32},{64,80},{80,64},{96,112},{112,96},{1... | collective-permute-start | bytes 24584 | tf_op jit(solution)/shard_map/ppermute | solution.py:335
  40.0 0.6 spread.3
  40.6 4.7 %all-to-all-start.2 = ((bf16[16,8,256]{2,1,0:T(8,128)(2,1)}), bf16[16,8,256]{2,1,0:T(8,128)(2,1)S(1)}, u32[]{:S(2)}, u32[]{:S(2)}) async-start(bf16[16,8,256]{2,1,0:T(8,128)(2,1)} %spread.3), calls=%async_computation.2 | async-start | bytes 131072 | tf_op jit(solution)/shard_map/all_to_all | solution.py:362
  45.3 0.0 collective-permute-done.6.received_ref
  45.3 0.8 collective-permute-start.7
  46.1 0.2 near_terms.6.near_0
  46.3 0.2 near_terms.7.near_1
  46.4 2.2 %collective-permute-done.7.received_ref = f32[16,256]{1,0:T(8,128)S(1)} collective-permute-done((f32[16,256]{1,0:T(8,128)S(1)}, f32[16,256]{1,0:T(8,128)S(1)}, u32[]{:S(2)}, u32[]{:S(2)}) %collective-permute-start.7) | collective-permute-done | bytes 16416 | tf_op jit(solution)/shard_map/ppermute | solution.py:335
  48.6 1.0 %collective-permute-start.8 = (f32[32,256]{1,0:T(8,128)S(1)}, f32[32,256]{1,0:T(8,128)S(1)}, u32[]{:S(2)}, u32[]{:S(2)}) collective-permute-start(f32[32,256]{1,0:T(8,128)S(1)} %join.7.line_ref), channel_id=1, source_target_pairs={{0,112},{16,96},{32,80},{48,64},{64,48},{80,32},{96,16},{112,0},{1... | collective-permute-start | bytes 98312 | tf_op jit(solution)/shard_map/ppermute | solution.py:335
  49.6 2.2 %all-to-all-done.2 = bf16[16,8,256]{2,1,0:T(8,128)(2,1)S(1)} async-done(((bf16[16,8,256]{2,1,0:T(8,128)(2,1)}), bf16[16,8,256]{2,1,0:T(8,128)(2,1)S(1)}, u32[]{:S(2)}, u32[]{:S(2)}) %all-to-all-start.2) | async-done | bytes 65568 | tf_op jit(solution)/shard_map/all_to_all | solution.py:362
  51.8 3.7 %terms_to_second_again.1 = (f32[32,256]{1,0:T(8,128)S(1)}, f32[32,256]{1,0:T(8,128)S(1)}, bf16[6144,256]{1,0:T(8,128)(2,1)S(1)}, bf16[256,8192]{1,0:T(8,128)(2,1)S(1)}) custom-call(bf16[128,256]{1,0:T(8,128)(2,1)S(1)} %bitcast.14, f32[4,256]{1,0:T(4,128)S(1)} %near_terms.6.near_0, f32[4,256]{1,0:T(4,128)S(1)} %near_terms.7.near_1, ...), custom_call_target="tpu_custom_call" | custom-call | flops 5500000256 | tf_op jit(solution)/shard_map/terms_to_second_again/pallas_call | solution.py:313
  55.6 1.9 %collective-permute-start.9 = (f32[32,256]{1,0:T(8,128)S(1)}, f32[32,256]{1,0:T(8,128)S(1)}, u32[]{:S(2)}, u32[]{:S(2)}) collective-permute-start(f32[32,256]{1,0:T(8,128)S(1)} %get-tuple-element.46), channel_id=1, source_target_pairs={{0,48},{16,32},{32,16},{48,0},{64,112},{80,96},{96,80},{112,64},{1... | collective-permute-start | bytes 98312 | tf_op jit(solution)/shard_map/ppermute | solution.py:335
  57.5 0.0 collective-permute-done.8.more_ref
  57.5 2.2 %terms_to_first.3 = f32[128,256]{1,0:T(8,128)} custom-call(f32[32,256]{1,0:T(8,128)S(1)} %join.7.line_ref, f32[32,256]{1,0:T(8,128)S(1)} %collective-permute-done.8.more_ref, s32[8,128]{1,0:T(8,128)S(1)} %get-tuple-element.29.info.info_ref, s32[128,128]{1,0:T(8,128)S(1)} %get-tuple-element.30.col.col_ref, bf16[2048,256]{1,0:T(8,128)(2,1)S(1)} %get-tuple-element.31.left_head, ...), custom_call_target="tpu_custom_call" | custom-call | flops 2750000128 | tf_op jit(solution)/shard_map/terms_to_first/pallas_call | solution.py:313
  59.7 3.5 %all-to-all-start.3 = ((f32[16,8,256]{2,1,0:T(8,128)}), f32[16,8,256]{2,1,0:T(8,128)S(1)}, u32[]{:S(2)}, u32[]{:S(2)}) async-start(f32[16,8,256]{2,1,0:T(8,128)} %bitcast.7), calls=%async_computation.3 | async-start | bytes 262144 | tf_op jit(solution)/shard_map/all_to_all | solution.py:377
  63.2 0.0 collective-permute-done.9.received_ref
  63.3 1.9 %collective-permute-start.10 = (f32[16,256]{1,0:T(8,128)S(1)}, f32[16,256]{1,0:T(8,128)S(1)}, u32[]{:S(2)}, u32[]{:S(2)}) collective-permute-start(f32[16,256]{1,0:T(8,128)S(1)} %get-tuple-element.48), channel_id=1, source_target_pairs={{0,112},{16,96},{32,80},{48,64},{64,48},{80,32},{96,16},{112,0},{1... | collective-permute-start | bytes 49160 | tf_op jit(solution)/shard_map/ppermute | solution.py:335
  65.2 2.8 %collective-permute-done.10.received_ref = f32[16,256]{1,0:T(8,128)S(1)} collective-permute-done((f32[16,256]{1,0:T(8,128)S(1)}, f32[16,256]{1,0:T(8,128)S(1)}, u32[]{:S(2)}, u32[]{:S(2)}) %collective-permute-start.10) | collective-permute-done | bytes 16416 | tf_op jit(solution)/shard_map/ppermute | solution.py:335
  68.0 0.0 collective-permute-start.11
  68.0 1.2 %collective-permute-done.11.refs_2_ = f32[8,256]{1,0:T(8,128)S(1)} collective-permute-done((f32[8,256]{1,0:T(8,128)S(1)}, f32[8,256]{1,0:T(8,128)S(1)}, u32[]{:S(2)}, u32[]{:S(2)}) %collective-permute-start.11) | collective-permute-done | bytes 8224 | tf_op jit(solution)/shard_map/ppermute | solution.py:335
  69.2 1.4 %all-to-all-done.3.refs_0_ = f32[16,8,256]{2,1,0:T(8,128)S(1)} async-done(((f32[16,8,256]{2,1,0:T(8,128)}), f32[16,8,256]{2,1,0:T(8,128)S(1)}, u32[]{:S(2)}, u32[]{:S(2)}) %all-to-all-start.3) | async-done | bytes 131104 | tf_op jit(solution)/shard_map/all_to_all | solution.py:377
  70.5 0.2 last_step.1
  70.7 16.5 %all_to_all.31 = f32[128,1,128]{2,1,0:T(1,128)S(1)} all-to-all(f32[128,1,128]{2,1,0:T(1,128)S(1)} %bitcast.15), channel_id=1, replica_groups=mesh['row'=8,'col'=16] {'row','col'}, dimensions={0} | all-to-all | bytes 131072 | tf_op jit(solution)/shard_map/all_to_all | solution.py:387
  87.2 0.9 %finish.1 = (f32[2,2048]{1,0:T(2,128)}, f32[1,1]{1,0:T(1,128)}) custom-call(f32[128,128]{1,0:T(8,128)S(1)} %bitcast.16, f32[2,8,256]{2,1,0:T(8,128)S(1)} %get-tuple-element.53.new_ref, s32[1,2048]{1,0:T(1,128)S(1)} %bitcast.19), custom_call_target="tpu_custom_call" | custom-call | flops 1100000000 | tf_op jit(solution)/shard_map/finish/pallas_call | solution.py:313
  (9 shorter events, 0.1 us)
Async XLA Ops:
  0.6 10.9 %copy-start.5 = (s32[128,2]{0,1:T(2,128)S(1)}, s32[128,2]{0,1:T(2,128)}, u32[]{:S(2)}) copy-start(s32[128,2]{0,1:T(2,128)} %param.13) | copy-start | bytes 3076
  0.6 12.5 %copy-start.1 = (f32[3,2048]{1,0:T(4,128)S(1)}, f32[3,2048]{1,0:T(4,128)}, u32[]{:S(2)}) copy-start(f32[3,2048]{1,0:T(4,128)} %friction_ref.1) | copy-start | bytes 73732
  0.7 12.5 %copy-start.2 = (f32[2,2048]{1,0:T(2,128)S(1)}, f32[2,2048]{1,0:T(2,128)}, u32[]{:S(2)}) copy-start(f32[2,2048]{1,0:T(2,128)} %state_ref.3) | copy-start | bytes 49156
  0.7 12.5 %copy-start.3 = (s32[2048]{0:T(1024)S(1)}, s32[2048]{0:T(1024)}, u32[]{:S(2)}) copy-start(s32[2048]{0:T(1024)} %param.15) | copy-start | bytes 24580
  0.7 12.5 %copy-start.4 = (s32[128]{0:T(128)S(1)}, s32[128]{0:T(128)}, u32[]{:S(2)}) copy-start(s32[128]{0:T(128)} %param.14) | copy-start | bytes 1540
  1.7 12.1 %copy-start = (bf16[8,256,256]{2,1,0:T(8,128)(2,1)S(1)}, bf16[8,256,256]{2,1,0:T(8,128)(2,1)}, u32[]{:S(2)}) copy-start(bf16[8,256,256]{2,1,0:T(8,128)(2,1)} %near.7) | copy-start | bytes 3145732
  1.7 9.9 %collective-permute-start = (f32[8,256]{1,0:T(8,128)S(1)}, f32[8,256]{1,0:T(8,128)S(1)}, u32[]{:S(2)}, u32[]{:S(2)}) collective-permute-start(f32[8,256]{1,0:T(8,128)S(1)} %first_deficit.1.held_ref.own_ref), channel_id=1, source_target_pairs={{0,16},{16,0},{32,48},{48,32},{64,80},{80,64},{96,112},{112,96},{1... | collective-permute-start | bytes 24584 | tf_op jit(solution)/shard_map/ppermute | solution.py:335
  3.8 14.2 %all-to-all-start = ((bf16[16,8,256]{2,1,0:T(8,128)(2,1)}), bf16[16,8,256]{2,1,0:T(8,128)(2,1)S(1)}, u32[]{:S(2)}, u32[]{:S(2)}) async-start(bf16[16,8,256]{2,1,0:T(8,128)(2,1)} %spread.2), calls=%async_computation | async-start | bytes 131072 | tf_op jit(solution)/shard_map/all_to_all | solution.py:362
  11.6 3.5 %collective-permute-start.1 = (f32[16,256]{1,0:T(8,128)S(1)}, f32[16,256]{1,0:T(8,128)S(1)}, u32[]{:S(2)}, u32[]{:S(2)}) collective-permute-start(f32[16,256]{1,0:T(8,128)S(1)} %join.4.held_ref._.two_ref), channel_id=1, source_target_pairs={{0,48},{16,32},{32,16},{48,0},{64,112},{80,96},{96,80},{112,64},{1... | collective-permute-start | bytes 49160 | tf_op jit(solution)/shard_map/ppermute | solution.py:335
  15.1 9.8 %collective-permute-start.2 = (f32[32,256]{1,0:T(8,128)S(1)}, f32[32,256]{1,0:T(8,128)S(1)}, u32[]{:S(2)}, u32[]{:S(2)}) collective-permute-start(f32[32,256]{1,0:T(8,128)S(1)} %join.5.line_ref), channel_id=1, source_target_pairs={{0,112},{16,96},{32,80},{48,64},{64,48},{80,32},{96,16},{112,0},{1... | collective-permute-start | bytes 98312 | tf_op jit(solution)/shard_map/ppermute | solution.py:335
  22.2 9.1 %collective-permute-start.3 = (f32[32,256]{1,0:T(8,128)S(1)}, f32[32,256]{1,0:T(8,128)S(1)}, u32[]{:S(2)}, u32[]{:S(2)}) collective-permute-start(f32[32,256]{1,0:T(8,128)S(1)} %get-tuple-element.35), channel_id=1, source_target_pairs={{0,48},{16,32},{32,16},{48,0},{64,112},{80,96},{96,80},{112,64},{1... | collective-permute-start | bytes 98312 | tf_op jit(solution)/shard_map/ppermute | solution.py:335
  27.2 11.0 %all-to-all-start.1 = ((f32[16,8,256]{2,1,0:T(8,128)}), f32[16,8,256]{2,1,0:T(8,128)S(1)}, u32[]{:S(2)}, u32[]{:S(2)}) async-start(f32[16,8,256]{2,1,0:T(8,128)} %bitcast.5), calls=%async_computation.1 | async-start | bytes 262144 | tf_op jit(solution)/shard_map/all_to_all | solution.py:377
  31.4 4.6 %collective-permute-start.4 = (f32[16,256]{1,0:T(8,128)S(1)}, f32[16,256]{1,0:T(8,128)S(1)}, u32[]{:S(2)}, u32[]{:S(2)}) collective-permute-start(f32[16,256]{1,0:T(8,128)S(1)} %get-tuple-element.37), channel_id=1, source_target_pairs={{0,112},{16,96},{32,80},{48,64},{64,48},{80,32},{96,16},{112,0},{1... | collective-permute-start | bytes 49160 | tf_op jit(solution)/shard_map/ppermute | solution.py:335
  36.0 1.2 %collective-permute-start.5 = (f32[8,256]{1,0:T(8,128)S(1)}, f32[8,256]{1,0:T(8,128)S(1)}, u32[]{:S(2)}, u32[]{:S(2)}) collective-permute-start(f32[8,256]{1,0:T(8,128)S(1)} %get-tuple-element.39), channel_id=1, source_target_pairs={{0,16},{16,0},{32,48},{48,32},{64,80},{80,64},{96,112},{112,96},{1... | collective-permute-start | bytes 24584 | tf_op jit(solution)/shard_map/ppermute | solution.py:335
  38.2 7.1 %collective-permute-start.6 = (f32[8,256]{1,0:T(8,128)S(1)}, f32[8,256]{1,0:T(8,128)S(1)}, u32[]{:S(2)}, u32[]{:S(2)}) collective-permute-start(f32[8,256]{1,0:T(8,128)S(1)} %get-tuple-element.41.held_ref.own_ref), channel_id=1, source_target_pairs={{0,16},{16,0},{32,48},{48,32},{64,80},{80,64},{96,112},{112,96},{1... | collective-permute-start | bytes 24584 | tf_op jit(solution)/shard_map/ppermute | solution.py:335
  40.6 11.2 %all-to-all-start.2 = ((bf16[16,8,256]{2,1,0:T(8,128)(2,1)}), bf16[16,8,256]{2,1,0:T(8,128)(2,1)S(1)}, u32[]{:S(2)}, u32[]{:S(2)}) async-start(bf16[16,8,256]{2,1,0:T(8,128)(2,1)} %spread.3), calls=%async_computation.2 | async-start | bytes 131072 | tf_op jit(solution)/shard_map/all_to_all | solution.py:362
  45.3 3.3 %collective-permute-start.7 = (f32[16,256]{1,0:T(8,128)S(1)}, f32[16,256]{1,0:T(8,128)S(1)}, u32[]{:S(2)}, u32[]{:S(2)}) collective-permute-start(f32[16,256]{1,0:T(8,128)S(1)} %join.6.held_ref.two_ref), channel_id=1, source_target_pairs={{0,48},{16,32},{32,16},{48,0},{64,112},{80,96},{96,80},{112,64},{1... | collective-permute-start | bytes 49160 | tf_op jit(solution)/shard_map/ppermute | solution.py:335
  48.6 8.9 %collective-permute-start.8 = (f32[32,256]{1,0:T(8,128)S(1)}, f32[32,256]{1,0:T(8,128)S(1)}, u32[]{:S(2)}, u32[]{:S(2)}) collective-permute-start(f32[32,256]{1,0:T(8,128)S(1)} %join.7.line_ref), channel_id=1, source_target_pairs={{0,112},{16,96},{32,80},{48,64},{64,48},{80,32},{96,16},{112,0},{1... | collective-permute-start | bytes 98312 | tf_op jit(solution)/shard_map/ppermute | solution.py:335
  55.6 7.7 %collective-permute-start.9 = (f32[32,256]{1,0:T(8,128)S(1)}, f32[32,256]{1,0:T(8,128)S(1)}, u32[]{:S(2)}, u32[]{:S(2)}) collective-permute-start(f32[32,256]{1,0:T(8,128)S(1)} %get-tuple-element.46), channel_id=1, source_target_pairs={{0,48},{16,32},{32,16},{48,0},{64,112},{80,96},{96,80},{112,64},{1... | collective-permute-start | bytes 98312 | tf_op jit(solution)/shard_map/ppermute | solution.py:335
  59.7 10.8 %all-to-all-start.3 = ((f32[16,8,256]{2,1,0:T(8,128)}), f32[16,8,256]{2,1,0:T(8,128)S(1)}, u32[]{:S(2)}, u32[]{:S(2)}) async-start(f32[16,8,256]{2,1,0:T(8,128)} %bitcast.7), calls=%async_computation.3 | async-start | bytes 262144 | tf_op jit(solution)/shard_map/all_to_all | solution.py:377
  63.3 4.7 %collective-permute-start.10 = (f32[16,256]{1,0:T(8,128)S(1)}, f32[16,256]{1,0:T(8,128)S(1)}, u32[]{:S(2)}, u32[]{:S(2)}) collective-permute-start(f32[16,256]{1,0:T(8,128)S(1)} %get-tuple-element.48), channel_id=1, source_target_pairs={{0,112},{16,96},{32,80},{48,64},{64,48},{80,32},{96,16},{112,0},{1... | collective-permute-start | bytes 49160 | tf_op jit(solution)/shard_map/ppermute | solution.py:335
  68.0 1.2 %collective-permute-start.11 = (f32[8,256]{1,0:T(8,128)S(1)}, f32[8,256]{1,0:T(8,128)S(1)}, u32[]{:S(2)}, u32[]{:S(2)}) collective-permute-start(f32[8,256]{1,0:T(8,128)S(1)} %get-tuple-element.50), channel_id=1, source_target_pairs={{0,16},{16,0},{32,48},{48,32},{64,80},{80,64},{96,112},{112,96},{1... | collective-permute-start | bytes 24584 | tf_op jit(solution)/shard_map/ppermute | solution.py:335

commit v9 on v7

--- a/solution.py
+++ b/solution.py
@@ -339,7 +339,7 @@
     def block_of(blocks, dtype):
         return sds((blocks * own_count, cluster), dtype)
 
-    chunk, head = 2048, HEAD
+    chunk, head = 3072, HEAD
     tail = count * width - head
     scratch = [pltpu.VMEM((tail, cluster), bf16), pltpu.SemaphoreType.DMA((2, tail // chunk + 1))]
     kept_there = [pltpu.VMEM((head, cluster), bf16)] * 2

time: 89.1 us -> 89 us (level)
  no operation moved by 1% of the time
where the time goes in v9:
time: 89 us; the launch traced here: 88.5 us
  starting transfers between devices  35.9 us (40%)
  waiting for transfers between devices  18.7 us (21%)
  Pallas kernels  17.1 us (19%)
  blocking collectives  15.8 us (18%)
    ppermute x12, starting transfers between devices, swap(): return lax.ppermute(x, axis, [(r, r ^ distance) for r in range(size)])  17.7 us
    pallas_call x23, Pallas kernels, call(): pl.pallas_call(kernel, out_shape=out_shape, in_specs=[pl.BlockSpec(memory...  17.1 us
    all_to_all x1, blocking collectives, shards(): everywhere = lax.all_to_all(squares, ('row', 'col'), 0, 0, tiled=True)  15.8 us
    ppermute x12, waiting for transfers between devices, swap(): return lax.ppermute(x, axis, [(r, r ^ distance) for r in range(size)])  12.6 us
    all_to_all x2, starting transfers between devices, exchange(): everyone = lax.all_to_all(copies, 'col', 0, 0).reshape(span, cluster)  11.2 us
    all_to_all x2, starting transfers between devices, exchange(): lax.all_to_all(first.reshape(columns, own_count, cluster), 'col', 0, 0)  7.02 us
    all_to_all x2, waiting for transfers between devices, exchange(): lax.all_to_all(first.reshape(columns, own_count, cluster), 'col', 0, 0)  5.32 us
  transfers between devices with their start and end apart: 16, of which 10 were waited for; matrix products, arithmetic and copies ran while one was open for 0% of the time, Pallas kernels for 17%

profile of v9, /device:TPU:1, one launch (start us, length us, event | category | flops | bytes accessed | tf_op | source)
XLA Modules:
  0.0 88.5 jit_solution(14454113366535812280)
XLA Ops:
  0.6 0.0 copy-start.5
  0.6 0.0 copy-start.1
  0.7 0.0 copy-start.2
  0.7 0.0 copy-start.3
  0.7 0.0 copy-start.4
  0.7 1.0 %first_deficit.1.held_ref.own_ref = f32[8,256]{1,0:T(8,128)S(1)} custom-call(f32[2,2048]{1,0:T(2,128)} %state_ref.3, s32[1,2048]{1,0:T(1,128)} %bitcast.17), custom_call_target="tpu_custom_call" | custom-call | flops 6600000000 | tf_op jit(solution)/shard_map/first_deficit/pallas_call | solution.py:310
  1.7 0.0 copy-start
  1.7 1.5 %collective-permute-start = (f32[8,256]{1,0:T(8,128)S(1)}, f32[8,256]{1,0:T(8,128)S(1)}, u32[]{:S(2)}, u32[]{:S(2)}) collective-permute-start(f32[8,256]{1,0:T(8,128)S(1)} %first_deficit.1.held_ref.own_ref), channel_id=1, source_target_pairs={{0,16},{16,0},{32,48},{48,32},{64,80},{80,64},{96,112},{112,96},{1... | collective-permute-start | bytes 24584 | tf_op jit(solution)/shard_map/ppermute | solution.py:332
  3.2 0.6 spread.2
  3.8 7.7 %all-to-all-start = ((bf16[16,8,256]{2,1,0:T(8,128)(2,1)}), bf16[16,8,256]{2,1,0:T(8,128)(2,1)S(1)}, u32[]{:S(2)}, u32[]{:S(2)}) async-start(bf16[16,8,256]{2,1,0:T(8,128)(2,1)} %spread.2), calls=%async_computation | async-start | bytes 131072 | tf_op jit(solution)/shard_map/all_to_all | solution.py:359
  11.5 0.0 copy-done.5
  11.5 0.1 copy.11.pairs_ref
  11.6 0.0 collective-permute-done.received_ref
  11.6 1.6 %collective-permute-start.1 = (f32[16,256]{1,0:T(8,128)S(1)}, f32[16,256]{1,0:T(8,128)S(1)}, u32[]{:S(2)}, u32[]{:S(2)}) collective-permute-start(f32[16,256]{1,0:T(8,128)S(1)} %join.4.held_ref._.two_ref), channel_id=1, source_target_pairs={{0,48},{16,32},{32,16},{48,0},{64,112},{80,96},{96,80},{112,64},{1... | collective-permute-start | bytes 49160 | tf_op jit(solution)/shard_map/ppermute | solution.py:332
  13.2 0.0 copy-done.1
  13.2 0.0 copy-done.2
  13.2 0.0 copy-done.3
  13.2 0.0 copy-done.4
  13.2 0.5 prepare.1
  13.7 0.0 copy-done
  13.7 0.2 near_terms.4.near_0
  13.9 0.2 near_terms.5.near_1
  14.1 1.0 %collective-permute-done.1.received_ref = f32[16,256]{1,0:T(8,128)S(1)} collective-permute-done((f32[16,256]{1,0:T(8,128)S(1)}, f32[16,256]{1,0:T(8,128)S(1)}, u32[]{:S(2)}, u32[]{:S(2)}) %collective-permute-start.1) | collective-permute-done | bytes 16416 | tf_op jit(solution)/shard_map/ppermute | solution.py:332
  15.1 2.6 %collective-permute-start.2 = (f32[32,256]{1,0:T(8,128)S(1)}, f32[32,256]{1,0:T(8,128)S(1)}, u32[]{:S(2)}, u32[]{:S(2)}) collective-permute-start(f32[32,256]{1,0:T(8,128)S(1)} %join.5.line_ref), channel_id=1, source_target_pairs={{0,112},{16,96},{32,80},{48,64},{64,48},{80,32},{96,16},{112,0},{1... | collective-permute-start | bytes 98312 | tf_op jit(solution)/shard_map/ppermute | solution.py:332
  17.8 0.2 all-to-all-done
  18.0 4.2 %terms_to_second.1 = (f32[32,256]{1,0:T(8,128)S(1)}, f32[32,256]{1,0:T(8,128)S(1)}, bf16[2048,256]{1,0:T(8,128)(2,1)S(1)}, bf16[2048,256]{1,0:T(8,128)(2,1)S(1)}...) custom-call(bf16[128,256]{1,0:T(8,128)(2,1)S(1)} %bitcast.13, f32[4,256]{1,0:T(4,128)S(1)} %near_terms.4.near_0, ...), custom_call_target="tpu_custom_call" | custom-call | flops 5500000256 | tf_op jit(solution)/shard_map/terms_to_second/pallas_call | solution.py:310
  22.2 4.1 %collective-permute-start.3 = (f32[32,256]{1,0:T(8,128)S(1)}, f32[32,256]{1,0:T(8,128)S(1)}, u32[]{:S(2)}, u32[]{:S(2)}) collective-permute-start(f32[32,256]{1,0:T(8,128)S(1)} %get-tuple-element.35), channel_id=1, source_target_pairs={{0,112},{16,96},{32,80},{48,64},{64,48},{80,32},{96,16},{112,0},{1... | collective-permute-start | bytes 98312 | tf_op jit(solution)/shard_map/ppermute | solution.py:332
  26.4 0.0 collective-permute-done.2.more_ref
  26.4 2.2 %terms_to_first.2 = f32[128,256]{1,0:T(8,128)} custom-call(f32[32,256]{1,0:T(8,128)S(1)} %join.5.line_ref, f32[32,256]{1,0:T(8,128)S(1)} %collective-permute-done.2.more_ref, s32[8,128]{1,0:T(8,128)S(1)} %get-tuple-element.29.info.info_ref, s32[128,128]{1,0:T(8,128)S(1)} %get-tuple-element.30.col.col_ref, bf16[2048,256]{1,0:T(8,128)(2,1)S(1)} %get-tuple-element.31.left_head, ...), custom_call_target="tpu_custom_call" | custom-call | flops 2750000128 | tf_op jit(solution)/shard_map/terms_to_first/pallas_call | solution.py:310
  28.6 3.5 %all-to-all-start.1 = ((f32[16,8,256]{2,1,0:T(8,128)}), f32[16,8,256]{2,1,0:T(8,128)S(1)}, u32[]{:S(2)}, u32[]{:S(2)}) async-start(f32[16,8,256]{2,1,0:T(8,128)} %bitcast.5), calls=%async_computation.1 | async-start | bytes 262144 | tf_op jit(solution)/shard_map/all_to_all | solution.py:374
  32.1 0.0 collective-permute-done.3.received_ref
  32.2 0.1 collective-permute-start.4
  32.3 3.2 %collective-permute-done.4.received_ref = f32[16,256]{1,0:T(8,128)S(1)} collective-permute-done((f32[16,256]{1,0:T(8,128)S(1)}, f32[16,256]{1,0:T(8,128)S(1)}, u32[]{:S(2)}, u32[]{:S(2)}) %collective-permute-start.4) | collective-permute-done | bytes 16416 | tf_op jit(solution)/shard_map/ppermute | solution.py:332
  35.4 0.0 collective-permute-start.5
  35.4 1.2 %collective-permute-done.5.refs_2_ = f32[8,256]{1,0:T(8,128)S(1)} collective-permute-done((f32[8,256]{1,0:T(8,128)S(1)}, f32[8,256]{1,0:T(8,128)S(1)}, u32[]{:S(2)}, u32[]{:S(2)}) %collective-permute-start.5) | collective-permute-done | bytes 8224 | tf_op jit(solution)/shard_map/ppermute | solution.py:332
  36.6 2.9 %all-to-all-done.1.refs_0_ = f32[16,8,256]{2,1,0:T(8,128)S(1)} async-done(((f32[16,8,256]{2,1,0:T(8,128)}), f32[16,8,256]{2,1,0:T(8,128)S(1)}, u32[]{:S(2)}, u32[]{:S(2)}) %all-to-all-start.1) | async-done | bytes 131104 | tf_op jit(solution)/shard_map/all_to_all | solution.py:374
  39.5 0.9 %collective-permute-start.6 = (f32[8,256]{1,0:T(8,128)S(1)}, f32[8,256]{1,0:T(8,128)S(1)}, u32[]{:S(2)}, u32[]{:S(2)}) collective-permute-start(f32[8,256]{1,0:T(8,128)S(1)} %get-tuple-element.41.held_ref.own_ref), channel_id=1, source_target_pairs={{0,16},{16,0},{32,48},{48,32},{64,80},{80,64},{96,112},{112,96},{1... | collective-permute-start | bytes 24584 | tf_op jit(solution)/shard_map/ppermute | solution.py:332
  40.4 0.6 spread.3
  41.1 3.5 %all-to-all-start.2 = ((bf16[16,8,256]{2,1,0:T(8,128)(2,1)}), bf16[16,8,256]{2,1,0:T(8,128)(2,1)S(1)}, u32[]{:S(2)}, u32[]{:S(2)}) async-start(bf16[16,8,256]{2,1,0:T(8,128)(2,1)} %spread.3), calls=%async_computation.2 | async-start | bytes 131072 | tf_op jit(solution)/shard_map/all_to_all | solution.py:359
  44.6 0.0 collective-permute-done.6.received_ref
  44.6 0.3 collective-permute-start.7
  44.9 0.2 near_terms.6.near_0
  45.0 0.2 near_terms.7.near_1
  45.2 2.7 %collective-permute-done.7.received_ref = f32[16,256]{1,0:T(8,128)S(1)} collective-permute-done((f32[16,256]{1,0:T(8,128)S(1)}, f32[16,256]{1,0:T(8,128)S(1)}, u32[]{:S(2)}, u32[]{:S(2)}) %collective-permute-start.7) | collective-permute-done | bytes 16416 | tf_op jit(solution)/shard_map/ppermute | solution.py:332
  47.9 2.6 %collective-permute-start.8 = (f32[32,256]{1,0:T(8,128)S(1)}, f32[32,256]{1,0:T(8,128)S(1)}, u32[]{:S(2)}, u32[]{:S(2)}) collective-permute-start(f32[32,256]{1,0:T(8,128)S(1)} %join.7.line_ref), channel_id=1, source_target_pairs={{0,112},{16,96},{32,80},{48,64},{64,48},{80,32},{96,16},{112,0},{1... | collective-permute-start | bytes 98312 | tf_op jit(solution)/shard_map/ppermute | solution.py:332
  50.5 0.6 all-to-all-done.2
  51.0 3.7 %terms_to_second_again.1 = (f32[32,256]{1,0:T(8,128)S(1)}, f32[32,256]{1,0:T(8,128)S(1)}, bf16[6144,256]{1,0:T(8,128)(2,1)S(1)}, bf16[256,8192]{1,0:T(8,128)(2,1)S(1)}) custom-call(bf16[128,256]{1,0:T(8,128)(2,1)S(1)} %bitcast.14, f32[4,256]{1,0:T(4,128)S(1)} %near_terms.6.near_0, f32[4,256]{1,0:T(4,128)S(1)} %near_terms.7.near_1, ...), custom_call_target="tpu_custom_call" | custom-call | flops 5500000256 | tf_op jit(solution)/shard_map/terms_to_second_again/pallas_call | solution.py:310
  54.8 3.9 %collective-permute-start.9 = (f32[32,256]{1,0:T(8,128)S(1)}, f32[32,256]{1,0:T(8,128)S(1)}, u32[]{:S(2)}, u32[]{:S(2)}) collective-permute-start(f32[32,256]{1,0:T(8,128)S(1)} %get-tuple-element.46), channel_id=1, source_target_pairs={{0,112},{16,96},{32,80},{48,64},{64,48},{80,32},{96,16},{112,0},{1... | collective-permute-start | bytes 98312 | tf_op jit(solution)/shard_map/ppermute | solution.py:332
  58.7 0.0 collective-permute-done.8.more_ref
  58.7 2.2 %terms_to_first.3 = f32[128,256]{1,0:T(8,128)} custom-call(f32[32,256]{1,0:T(8,128)S(1)} %join.7.line_ref, f32[32,256]{1,0:T(8,128)S(1)} %collective-permute-done.8.more_ref, s32[8,128]{1,0:T(8,128)S(1)} %get-tuple-element.29.info.info_ref, s32[128,128]{1,0:T(8,128)S(1)} %get-tuple-element.30.col.col_ref, bf16[2048,256]{1,0:T(8,128)(2,1)S(1)} %get-tuple-element.31.left_head, ...), custom_call_target="tpu_custom_call" | custom-call | flops 2750000128 | tf_op jit(solution)/shard_map/terms_to_first/pallas_call | solution.py:310
  60.9 3.5 %all-to-all-start.3 = ((f32[16,8,256]{2,1,0:T(8,128)}), f32[16,8,256]{2,1,0:T(8,128)S(1)}, u32[]{:S(2)}, u32[]{:S(2)}) async-start(f32[16,8,256]{2,1,0:T(8,128)} %bitcast.7), calls=%async_computation.3 | async-start | bytes 262144 | tf_op jit(solution)/shard_map/all_to_all | solution.py:374
  64.4 0.0 collective-permute-done.9.received_ref
  64.5 0.1 collective-permute-start.10
  64.6 3.4 %collective-permute-done.10.received_ref = f32[16,256]{1,0:T(8,128)S(1)} collective-permute-done((f32[16,256]{1,0:T(8,128)S(1)}, f32[16,256]{1,0:T(8,128)S(1)}, u32[]{:S(2)}, u32[]{:S(2)}) %collective-permute-start.10) | collective-permute-done | bytes 16416 | tf_op jit(solution)/shard_map/ppermute | solution.py:332
  68.0 0.0 collective-permute-start.11
  68.0 1.2 %collective-permute-done.11.refs_2_ = f32[8,256]{1,0:T(8,128)S(1)} collective-permute-done((f32[8,256]{1,0:T(8,128)S(1)}, f32[8,256]{1,0:T(8,128)S(1)}, u32[]{:S(2)}, u32[]{:S(2)}) %collective-permute-start.11) | collective-permute-done | bytes 8224 | tf_op jit(solution)/shard_map/ppermute | solution.py:332
  69.2 2.4 %all-to-all-done.3.refs_0_ = f32[16,8,256]{2,1,0:T(8,128)S(1)} async-done(((f32[16,8,256]{2,1,0:T(8,128)}), f32[16,8,256]{2,1,0:T(8,128)S(1)}, u32[]{:S(2)}, u32[]{:S(2)}) %all-to-all-start.3) | async-done | bytes 131104 | tf_op jit(solution)/shard_map/all_to_all | solution.py:374
  71.6 0.2 last_step.1
  71.8 15.8 %all_to_all.31 = f32[128,1,128]{2,1,0:T(1,128)S(1)} all-to-all(f32[128,1,128]{2,1,0:T(1,128)S(1)} %bitcast.15), channel_id=1, replica_groups=mesh['row'=8,'col'=16] {'row','col'}, dimensions={0} | all-to-all | bytes 131072 | tf_op jit(solution)/shard_map/all_to_all | solution.py:384
  87.6 0.9 %finish.1 = (f32[2,2048]{1,0:T(2,128)}, f32[1,1]{1,0:T(1,128)}) custom-call(f32[128,128]{1,0:T(8,128)S(1)} %bitcast.16, f32[2,8,256]{2,1,0:T(8,128)S(1)} %get-tuple-element.53.new_ref, s32[1,2048]{1,0:T(1,128)S(1)} %bitcast.19), custom_call_target="tpu_custom_call" | custom-call | flops 1100000000 | tf_op jit(solution)/shard_map/finish/pallas_call | solution.py:310
  (9 shorter events, 0.1 us)
Async XLA Ops:
  0.6 10.9 %copy-start.5 = (s32[128,2]{0,1:T(2,128)S(1)}, s32[128,2]{0,1:T(2,128)}, u32[]{:S(2)}) copy-start(s32[128,2]{0,1:T(2,128)} %param.13) | copy-start | bytes 3076
  0.6 12.5 %copy-start.1 = (f32[3,2048]{1,0:T(4,128)S(1)}, f32[3,2048]{1,0:T(4,128)}, u32[]{:S(2)}) copy-start(f32[3,2048]{1,0:T(4,128)} %friction_ref.1) | copy-start | bytes 73732
  0.7 12.5 %copy-start.2 = (f32[2,2048]{1,0:T(2,128)S(1)}, f32[2,2048]{1,0:T(2,128)}, u32[]{:S(2)}) copy-start(f32[2,2048]{1,0:T(2,128)} %state_ref.3) | copy-start | bytes 49156
  0.7 12.5 %copy-start.3 = (s32[2048]{0:T(1024)S(1)}, s32[2048]{0:T(1024)}, u32[]{:S(2)}) copy-start(s32[2048]{0:T(1024)} %param.15) | copy-start | bytes 24580
  0.7 12.5 %copy-start.4 = (s32[128]{0:T(128)S(1)}, s32[128]{0:T(128)}, u32[]{:S(2)}) copy-start(s32[128]{0:T(128)} %param.14) | copy-start | bytes 1540
  1.7 12.1 %copy-start = (bf16[8,256,256]{2,1,0:T(8,128)(2,1)S(1)}, bf16[8,256,256]{2,1,0:T(8,128)(2,1)}, u32[]{:S(2)}) copy-start(bf16[8,256,256]{2,1,0:T(8,128)(2,1)} %near.7) | copy-start | bytes 3145732
  1.7 9.9 %collective-permute-start = (f32[8,256]{1,0:T(8,128)S(1)}, f32[8,256]{1,0:T(8,128)S(1)}, u32[]{:S(2)}, u32[]{:S(2)}) collective-permute-start(f32[8,256]{1,0:T(8,128)S(1)} %first_deficit.1.held_ref.own_ref), channel_id=1, source_target_pairs={{0,16},{16,0},{32,48},{48,32},{64,80},{80,64},{96,112},{112,96},{1... | collective-permute-start | bytes 24584 | tf_op jit(solution)/shard_map/ppermute | solution.py:332
  3.8 14.2 %all-to-all-start = ((bf16[16,8,256]{2,1,0:T(8,128)(2,1)}), bf16[16,8,256]{2,1,0:T(8,128)(2,1)S(1)}, u32[]{:S(2)}, u32[]{:S(2)}) async-start(bf16[16,8,256]{2,1,0:T(8,128)(2,1)} %spread.2), calls=%async_computation | async-start | bytes 131072 | tf_op jit(solution)/shard_map/all_to_all | solution.py:359
  11.6 3.5 %collective-permute-start.1 = (f32[16,256]{1,0:T(8,128)S(1)}, f32[16,256]{1,0:T(8,128)S(1)}, u32[]{:S(2)}, u32[]{:S(2)}) collective-permute-start(f32[16,256]{1,0:T(8,128)S(1)} %join.4.held_ref._.two_ref), channel_id=1, source_target_pairs={{0,48},{16,32},{32,16},{48,0},{64,112},{80,96},{96,80},{112,64},{1... | collective-permute-start | bytes 49160 | tf_op jit(solution)/shard_map/ppermute | solution.py:332
  15.1 11.2 %collective-permute-start.2 = (f32[32,256]{1,0:T(8,128)S(1)}, f32[32,256]{1,0:T(8,128)S(1)}, u32[]{:S(2)}, u32[]{:S(2)}) collective-permute-start(f32[32,256]{1,0:T(8,128)S(1)} %join.5.line_ref), channel_id=1, source_target_pairs={{0,112},{16,96},{32,80},{48,64},{64,48},{80,32},{96,16},{112,0},{1... | collective-permute-start | bytes 98312 | tf_op jit(solution)/shard_map/ppermute | solution.py:332
  22.2 9.9 %collective-permute-start.3 = (f32[32,256]{1,0:T(8,128)S(1)}, f32[32,256]{1,0:T(8,128)S(1)}, u32[]{:S(2)}, u32[]{:S(2)}) collective-permute-start(f32[32,256]{1,0:T(8,128)S(1)} %get-tuple-element.35), channel_id=1, source_target_pairs={{0,112},{16,96},{32,80},{48,64},{64,48},{80,32},{96,16},{112,0},{1... | collective-permute-start | bytes 98312 | tf_op jit(solution)/shard_map/ppermute | solution.py:332
  28.6 10.9 %all-to-all-start.1 = ((f32[16,8,256]{2,1,0:T(8,128)}), f32[16,8,256]{2,1,0:T(8,128)S(1)}, u32[]{:S(2)}, u32[]{:S(2)}) async-start(f32[16,8,256]{2,1,0:T(8,128)} %bitcast.5), calls=%async_computation.1 | async-start | bytes 262144 | tf_op jit(solution)/shard_map/all_to_all | solution.py:374
  32.2 3.2 %collective-permute-start.4 = (f32[16,256]{1,0:T(8,128)S(1)}, f32[16,256]{1,0:T(8,128)S(1)}, u32[]{:S(2)}, u32[]{:S(2)}) collective-permute-start(f32[16,256]{1,0:T(8,128)S(1)} %get-tuple-element.37), channel_id=1, source_target_pairs={{0,48},{16,32},{32,16},{48,0},{64,112},{80,96},{96,80},{112,64},{1... | collective-permute-start | bytes 49160 | tf_op jit(solution)/shard_map/ppermute | solution.py:332
  35.4 1.2 %collective-permute-start.5 = (f32[8,256]{1,0:T(8,128)S(1)}, f32[8,256]{1,0:T(8,128)S(1)}, u32[]{:S(2)}, u32[]{:S(2)}) collective-permute-start(f32[8,256]{1,0:T(8,128)S(1)} %get-tuple-element.39), channel_id=1, source_target_pairs={{0,16},{16,0},{32,48},{48,32},{64,80},{80,64},{96,112},{112,96},{1... | collective-permute-start | bytes 24584 | tf_op jit(solution)/shard_map/ppermute | solution.py:332
  39.5 5.1 %collective-permute-start.6 = (f32[8,256]{1,0:T(8,128)S(1)}, f32[8,256]{1,0:T(8,128)S(1)}, u32[]{:S(2)}, u32[]{:S(2)}) collective-permute-start(f32[8,256]{1,0:T(8,128)S(1)} %get-tuple-element.41.held_ref.own_ref), channel_id=1, source_target_pairs={{0,16},{16,0},{32,48},{48,32},{64,80},{80,64},{96,112},{112,96},{1... | collective-permute-start | bytes 24584 | tf_op jit(solution)/shard_map/ppermute | solution.py:332
  41.1 10.0 %all-to-all-start.2 = ((bf16[16,8,256]{2,1,0:T(8,128)(2,1)}), bf16[16,8,256]{2,1,0:T(8,128)(2,1)S(1)}, u32[]{:S(2)}, u32[]{:S(2)}) async-start(bf16[16,8,256]{2,1,0:T(8,128)(2,1)} %spread.3), calls=%async_computation.2 | async-start | bytes 131072 | tf_op jit(solution)/shard_map/all_to_all | solution.py:359
  44.6 3.3 %collective-permute-start.7 = (f32[16,256]{1,0:T(8,128)S(1)}, f32[16,256]{1,0:T(8,128)S(1)}, u32[]{:S(2)}, u32[]{:S(2)}) collective-permute-start(f32[16,256]{1,0:T(8,128)S(1)} %join.6.held_ref.two_ref), channel_id=1, source_target_pairs={{0,48},{16,32},{32,16},{48,0},{64,112},{80,96},{96,80},{112,64},{1... | collective-permute-start | bytes 49160 | tf_op jit(solution)/shard_map/ppermute | solution.py:332
  47.9 10.8 %collective-permute-start.8 = (f32[32,256]{1,0:T(8,128)S(1)}, f32[32,256]{1,0:T(8,128)S(1)}, u32[]{:S(2)}, u32[]{:S(2)}) collective-permute-start(f32[32,256]{1,0:T(8,128)S(1)} %join.7.line_ref), channel_id=1, source_target_pairs={{0,112},{16,96},{32,80},{48,64},{64,48},{80,32},{96,16},{112,0},{1... | collective-permute-start | bytes 98312 | tf_op jit(solution)/shard_map/ppermute | solution.py:332
  54.8 9.7 %collective-permute-start.9 = (f32[32,256]{1,0:T(8,128)S(1)}, f32[32,256]{1,0:T(8,128)S(1)}, u32[]{:S(2)}, u32[]{:S(2)}) collective-permute-start(f32[32,256]{1,0:T(8,128)S(1)} %get-tuple-element.46), channel_id=1, source_target_pairs={{0,112},{16,96},{32,80},{48,64},{64,48},{80,32},{96,16},{112,0},{1... | collective-permute-start | bytes 98312 | tf_op jit(solution)/shard_map/ppermute | solution.py:332
  60.9 10.7 %all-to-all-start.3 = ((f32[16,8,256]{2,1,0:T(8,128)}), f32[16,8,256]{2,1,0:T(8,128)S(1)}, u32[]{:S(2)}, u32[]{:S(2)}) async-start(f32[16,8,256]{2,1,0:T(8,128)} %bitcast.7), calls=%async_computation.3 | async-start | bytes 262144 | tf_op jit(solution)/shard_map/all_to_all | solution.py:374
  64.5 3.5 %collective-permute-start.10 = (f32[16,256]{1,0:T(8,128)S(1)}, f32[16,256]{1,0:T(8,128)S(1)}, u32[]{:S(2)}, u32[]{:S(2)}) collective-permute-start(f32[16,256]{1,0:T(8,128)S(1)} %get-tuple-element.48), channel_id=1, source_target_pairs={{0,48},{16,32},{32,16},{48,0},{64,112},{80,96},{96,80},{112,64},{1... | collective-permute-start | bytes 49160 | tf_op jit(solution)/shard_map/ppermute | solution.py:332
  68.0 1.2 %collective-permute-start.11 = (f32[8,256]{1,0:T(8,128)S(1)}, f32[8,256]{1,0:T(8,128)S(1)}, u32[]{:S(2)}, u32[]{:S(2)}) collective-permute-start(f32[8,256]{1,0:T(8,128)S(1)} %get-tuple-element.50), channel_id=1, source_target_pairs={{0,16},{16,0},{32,48},{48,32},{64,80},{80,64},{96,112},{112,96},{1... | collective-permute-start | bytes 24584 | tf_op jit(solution)/shard_map/ppermute | solution.py:332
